TPU v7x, 32 devices: a whole 2x2x4 slice. The times are simulated.
32 devices in a mesh: dp: 8 (over y, x, core), tensor: 4 (over z).
Axes of the slice: x: 2, y: 2, z: 4, core: 2. Of those that a mesh axis runs over, the one named last changes fastest.
Arguments:
- tokens: bfloat16 [8, 2048, 768], P('dp', 'tensor'), may hold values from -6 to 6
- segments: int32 [8, 2048], P('dp'), may hold values from 0 to 7, never falling along the last dimension, each value on 1 to 1024 neighbouring positions
- w_qkv: bfloat16 [768, 3, 768], P(None, None, 'tensor'), may hold values from -0.21875 to 0.21875
- w_out: bfloat16 [768, 768], P('tensor'), may hold values from -0.875 to 0.875
- w_gate_up: bfloat16 [768, 2, 3072], P(None, None, 'tensor'), may hold values from -0.21875 to 0.21875
- w_down: bfloat16 [3072, 768], P('tensor'), may hold values from -0.109375 to 0.109375
- norm_gain: float32 [2, 768], replicated, may hold values from 0.25 to 1.75
- norm_bias: float32 [2, 768], replicated, may hold values from -4 to 4
- cotangent: bfloat16 [8, 2048, 768], P('dp', 'tensor'), may hold values from -6 to 6
Outputs:
- output: bfloat16 [8, 2048, 768], P('dp', 'tensor')
- grad_tokens: float32 [8, 2048, 768], P('dp', 'tensor')
- grad_w_qkv: float32 [768, 3, 768], P(None, None, 'tensor')
- grad_w_out: float32 [768, 768], P('tensor')
- grad_w_gate_up: float32 [768, 2, 3072], P(None, None, 'tensor')
- grad_w_down: float32 [3072, 768], P('tensor')
- grad_norm_gain: float32 [2, 768], replicated
- grad_norm_bias: float32 [2, 768], replicated
Inputs may be any that keep to these rules, and one draw needn't show every extreme that they name: `segments`: along each row of 2048 positions the segment numbers never fall.
All inputs are finite; a program needn't handle non-finite values.
Results may differ from a plain program's by a relative error of at most 0.017.
Values may be sent and summed in bfloat16 or wider, within the bound.
A program may use at most 128 MiB of HBM per device.

v0:
```python
import math

import jax
import jax.numpy as jnp
from jax import lax
from jax.sharding import PartitionSpec as P

HEAD_DIM = 64
QBLK = 512
SEGS = 8


epsilon = 1e-05
far_below = -1e30
log_base = math.log(1000.0)


def rotary_tables(segments_row):
    length = segments_row.shape[0]
    onehot = (segments_row[:, None] == jnp.arange(SEGS, dtype=jnp.int32)[None, :]).astype(jnp.int32)
    counts = jnp.sum(onehot, axis=0)
    starts = jnp.cumsum(counts) - counts
    first_place = jnp.sum(onehot * starts[None, :], axis=1)
    places = (jnp.arange(length, dtype=jnp.int32) - first_place).astype(jnp.float32)
    inverse = jnp.exp(-2.0 * jnp.arange(HEAD_DIM // 2, dtype=jnp.float32) / HEAD_DIM * log_base)
    angles = places[:, None] * inverse[None, :]
    return (jnp.cos(angles), jnp.sin(angles))


def rotate(values, cosine_table, sine_table):
    half_width = values.shape[-1] // 2
    first_half = values[..., :half_width]
    second_half = values[..., half_width:]
    cosine_wide = cosine_table[:, None, :]
    sine_wide = sine_table[:, None, :]
    return jnp.concatenate(
        [
            first_half * cosine_wide - second_half * sine_wide,
            second_half * cosine_wide + first_half * sine_wide,
        ],
        axis=-1,
    )


def rotate_back(grads, cosine_table, sine_table):
    half_width = grads.shape[-1] // 2
    first_half = grads[..., :half_width]
    second_half = grads[..., half_width:]
    cosine_wide = cosine_table[:, None, :]
    sine_wide = sine_table[:, None, :]
    return jnp.concatenate(
        [
            first_half * cosine_wide + second_half * sine_wide,
            second_half * cosine_wide - first_half * sine_wide,
        ],
        axis=-1,
    )


def norm_forward(summed, gain_row, bias_row):
    centred = summed - jnp.mean(summed, axis=-1, keepdims=True)
    variance = jnp.mean(centred * centred, axis=-1, keepdims=True)
    inverse = lax.rsqrt(variance + epsilon)
    normalized = centred * inverse
    return (normalized * gain_row + bias_row, normalized, inverse)


def norm_backward(grad_out, normalized, inverse, gain_row):
    grad_gain = jnp.sum(grad_out * normalized, axis=0)
    grad_bias = jnp.sum(grad_out, axis=0)
    scaled_grad = grad_out * gain_row
    grad_in = inverse * (
        scaled_grad
        - jnp.mean(scaled_grad, axis=-1, keepdims=True)
        - normalized * jnp.mean(scaled_grad * normalized, axis=-1, keepdims=True)
    )
    return (grad_in, grad_gain, grad_bias)


def block_scores(query_block, segment_block, keys_all, segments_row):
    score_scale = 1.0 / math.sqrt(HEAD_DIM)
    scores = (
        jnp.einsum("qhe,khe->hqk", query_block, keys_all, preferred_element_type=jnp.float32)
        * score_scale
    )
    allowed = segment_block[:, None] == segments_row[None, :]
    return jnp.where(allowed[None], scores, far_below)


def attend_forward(queries, keys_all, values_all, segments_row):
    length, heads_here, _ = queries.shape
    blocks = length // QBLK

    def one_block(inputs):
        query_block, segment_block = inputs
        scores = block_scores(query_block, segment_block, keys_all, segments_row)
        largest = jnp.max(scores, axis=-1, keepdims=True)
        weights = jnp.exp(scores - largest)
        row_total = jnp.sum(weights, axis=-1, keepdims=True)
        mixed_heads = jnp.einsum(
            "hqk,khe->qhe",
            (weights / row_total).astype(jnp.bfloat16),
            values_all,
            preferred_element_type=jnp.float32,
        )
        return (mixed_heads.astype(jnp.bfloat16), largest[..., 0] + jnp.log(row_total[..., 0]))

    mixed_heads, logsum = lax.map(
        one_block,
        (queries.reshape(blocks, QBLK, heads_here, HEAD_DIM), segments_row.reshape(blocks, QBLK)),
    )
    return (mixed_heads.reshape(length, heads_here * HEAD_DIM), logsum)


def attend_backward(queries, keys_all, values_all, segments_row, grad_heads, logsum):
    length, heads_here, _ = queries.shape
    blocks = length // QBLK
    score_scale = 1.0 / math.sqrt(HEAD_DIM)

    def one_block(carried, inputs):
        grad_keys, grad_values = carried
        query_block, segment_block, grad_block, logsum_block = inputs
        scores = block_scores(query_block, segment_block, keys_all, segments_row)
        probability = jnp.exp(scores - logsum_block[..., None])
        grad_probability = jnp.einsum(
            "qhe,khe->hqk", grad_block, values_all, preferred_element_type=jnp.float32
        )
        inner_sum = jnp.sum(probability * grad_probability, axis=-1, keepdims=True)
        grad_scores = (probability * (grad_probability - inner_sum)).astype(jnp.bfloat16)
        grad_query = (
            jnp.einsum("hqk,khe->qhe", grad_scores, keys_all, preferred_element_type=jnp.float32)
            * score_scale
        )
        grad_keys = (
            grad_keys
            + jnp.einsum(
                "hqk,qhe->khe", grad_scores, query_block, preferred_element_type=jnp.float32
            )
            * score_scale
        )
        grad_values = grad_values + jnp.einsum(
            "hqk,qhe->khe",
            probability.astype(jnp.bfloat16),
            grad_block,
            preferred_element_type=jnp.float32,
        )
        return ((grad_keys, grad_values), grad_query)

    zeros_block = jnp.zeros((length, heads_here, HEAD_DIM), jnp.float32)
    (grad_keys, grad_values), grad_queries = lax.scan(
        one_block,
        (zeros_block, zeros_block),
        (
            queries.reshape(blocks, QBLK, heads_here, HEAD_DIM),
            segments_row.reshape(blocks, QBLK),
            grad_heads.reshape(blocks, QBLK, heads_here, HEAD_DIM),
            logsum,
        ),
    )
    return (grad_queries.reshape(length, heads_here, HEAD_DIM), grad_keys, grad_values)


def on_device(tokens, segments, w_qkv, w_out, w_gate_up, w_down, norm_gain, norm_bias, cotangent):
    local_tokens = tokens[0]
    segments_row = segments[0]
    width_here = w_qkv.shape[2]
    heads_here = width_here // HEAD_DIM
    cosine_table, sine_table = rotary_tables(segments_row)
    gathered = lax.all_gather(local_tokens, "tensor", axis=0, tiled=True)
    length = gathered.shape[0]
    projected = jnp.einsum("sd,dcf->scf", gathered, w_qkv, preferred_element_type=jnp.float32)
    queries = rotate(
        projected[:, 0].reshape(length, heads_here, HEAD_DIM), cosine_table, sine_table
    ).astype(jnp.bfloat16)
    keys_all = rotate(
        projected[:, 1].reshape(length, heads_here, HEAD_DIM), cosine_table, sine_table
    ).astype(jnp.bfloat16)
    values_all = projected[:, 2].reshape(length, heads_here, HEAD_DIM).astype(jnp.bfloat16)
    heads_out, logsum = attend_forward(queries, keys_all, values_all, segments_row)
    branch = lax.psum_scatter(
        jnp.dot(heads_out, w_out, preferred_element_type=jnp.float32),
        "tensor",
        scatter_dimension=0,
        tiled=True,
    )
    normed, normal_one, inverse_one = norm_forward(
        local_tokens.astype(jnp.float32) + branch, norm_gain[0], norm_bias[0]
    )
    normed_low = normed.astype(jnp.bfloat16)
    normed_all = lax.all_gather(normed_low, "tensor", axis=0, tiled=True)
    gate_up = jnp.einsum("sd,dcf->scf", normed_all, w_gate_up, preferred_element_type=jnp.float32)
    gate_value = gate_up[:, 0]
    up_value = gate_up[:, 1]
    sigmoid_gate = jax.nn.sigmoid(gate_value)
    active = gate_value * sigmoid_gate
    hidden = (active * up_value).astype(jnp.bfloat16)
    mlp_out = lax.psum_scatter(
        jnp.dot(hidden, w_down, preferred_element_type=jnp.float32),
        "tensor",
        scatter_dimension=0,
        tiled=True,
    )
    result, normal_two, inverse_two = norm_forward(normed + mlp_out, norm_gain[1], norm_bias[1])
    output = result.astype(jnp.bfloat16)[None]
    grad_z2, gain_two, bias_two = norm_backward(
        cotangent[0].astype(jnp.float32), normal_two, inverse_two, norm_gain[1]
    )
    grad_mlp_all = lax.all_gather(grad_z2.astype(jnp.bfloat16), "tensor", axis=0, tiled=True)
    grad_hidden = jnp.einsum("sd,fd->sf", grad_mlp_all, w_down, preferred_element_type=jnp.float32)
    grad_w_down = jnp.einsum("sf,sd->fd", hidden, grad_mlp_all, preferred_element_type=jnp.float32)
    grad_gate = grad_hidden * up_value * sigmoid_gate * (1.0 + gate_value * (1.0 - sigmoid_gate))
    grad_up = grad_hidden * active
    grad_gate_up = jnp.stack([grad_gate, grad_up], axis=1).astype(jnp.bfloat16)
    normed_used = lax.all_gather(normed_low, "tensor", axis=0, tiled=True)
    grad_w_gate_up = jnp.einsum(
        "sd,scf->dcf", normed_used, grad_gate_up, preferred_element_type=jnp.float32
    )
    normed_part = jnp.einsum(
        "scf,dcf->sd", grad_gate_up, w_gate_up, preferred_element_type=jnp.float32
    )
    grad_normed = grad_z2 + lax.psum_scatter(normed_part, "tensor", scatter_dimension=0, tiled=True)
    grad_z1, gain_one, bias_one = norm_backward(grad_normed, normal_one, inverse_one, norm_gain[0])
    grad_branch_all = lax.all_gather(grad_z1.astype(jnp.bfloat16), "tensor", axis=0, tiled=True)
    grad_heads = jnp.einsum(
        "sd,fd->sf", grad_branch_all, w_out, preferred_element_type=jnp.float32
    ).astype(jnp.bfloat16)
    grad_w_out = jnp.einsum(
        "sf,sd->fd", heads_out, grad_branch_all, preferred_element_type=jnp.float32
    )
    grad_queries, grad_keys, grad_values = attend_backward(
        queries, keys_all, values_all, segments_row, grad_heads, logsum
    )
    grad_projected = jnp.stack(
        [
            rotate_back(grad_queries, cosine_table, sine_table).reshape(length, width_here),
            rotate_back(grad_keys, cosine_table, sine_table).reshape(length, width_here),
            grad_values.reshape(length, width_here),
        ],
        axis=1,
    ).astype(jnp.bfloat16)
    tokens_used = lax.all_gather(local_tokens, "tensor", axis=0, tiled=True)
    grad_w_qkv = jnp.einsum(
        "sd,scf->dcf", tokens_used, grad_projected, preferred_element_type=jnp.float32
    )
    input_part = jnp.einsum(
        "scf,dcf->sd", grad_projected, w_qkv, preferred_element_type=jnp.float32
    )
    grad_tokens = grad_z1 + lax.psum_scatter(
        input_part.astype(jnp.bfloat16), "tensor", scatter_dimension=0, tiled=True
    ).astype(jnp.float32)
    gains_part = jnp.stack([gain_one, gain_two], axis=0)
    biases_part = jnp.stack([bias_one, bias_two], axis=0)
    gains_sum, biases_sum = lax.psum((gains_part, biases_part), "tensor")
    grad_w_qkv, grad_w_out, grad_w_gate_up, grad_w_down, gains_sum, biases_sum = lax.psum(
        (grad_w_qkv, grad_w_out, grad_w_gate_up, grad_w_down, gains_sum, biases_sum), "dp"
    )
    return (
        output,
        grad_tokens[None],
        grad_w_qkv,
        grad_w_out,
        grad_w_gate_up,
        grad_w_down,
        gains_sum,
        biases_sum,
    )


def solution(mesh):
    placed = (
        P("dp", "tensor", None),
        P("dp", None),
        P(None, None, "tensor"),
        P("tensor", None),
        P(None, None, "tensor"),
        P("tensor", None),
        P(),
        P(),
        P("dp", "tensor", None),
    )
    return jax.shard_map(
        on_device,
        mesh=mesh,
        in_specs=placed,
        out_specs=(
            P("dp", "tensor", None),
            P("dp", "tensor", None),
            P(None, None, "tensor"),
            P("tensor", None),
            P(None, None, "tensor"),
            P("tensor", None),
            P(),
            P(),
        ),
        check_vma=False,
    )
```

profile of v0, /device:TPU:0, one launch (start us, length us, event | category | flops | bytes accessed | tf_op | source)
XLA Modules:
  0.0 1140.8 jit_solution(13494483288783922852)
XLA Ops:
  12.7 63.1 %all-gather.12.cloned.1.call-done = bf16[1,2048,768]{2,1,0:T(8,128)(2,1)} async-done(((bf16[1,512,768]{2,1,0:T(8,128)(2,1)}), bf16[1,2048,768]{2,1,0:T(8,128)(2,1)}) %all-gather.12.cloned.1.call-update) | async-done | bytes 3145744 | tf_op jit(solution)/shard_map/all_gather | solution.py:169
  75.8 4.1 fusion.51
  83.5 87.0 %while.27 = (s32[]{:T(128)}, bf16[4,512,3,64]{1,3,2,0:T(8,128)(2,1)}, f32[4,3,512]{2,1,0:T(4,128)S(1)}, s32[4,512]{1,0:T(4,128)S(1)}, s32[1,2048]{1,0:T(1,128)S(...) while((s32[]{:T(128)}, ...), condition=%wide.region_6.7_spmd, body=%wide.region_3.6_spmd.sunk | while | flops 844200448 | bytes 47124624 | solution.py:108
  84.2 6.8 fusion.128
  91.0 6.8 fusion.129
  97.8 7.4 fusion.130
  105.9 6.8 fusion.128
  112.7 6.8 fusion.129
  119.6 7.4 fusion.130
  127.7 6.8 fusion.128
  134.5 6.8 fusion.129
  141.3 7.4 fusion.130
  149.4 6.8 fusion.128
  156.2 6.8 fusion.129
  163.1 7.4 fusion.130
  173.4 3.7 fusion.83
  177.8 108.8 %reduce-scatter.5.cloned.1.call-done = f32[512,768]{1,0:T(8,128)} async-done(((f32[2048,768]{1,0:T(8,128)}), f32[512,768]{1,0:T(8,128)}) %reduce-scatter.5.cloned.1.call-update) | async-done | bytes 1572880 | tf_op jit(solution)/shard_map/reduce_scatter | solution.py:180
  291.1 63.9 %all-gather.6.cloned.1.call-done = bf16[2048,768]{1,0:T(8,128)(2,1)} async-done(((bf16[512,768]{1,0:T(8,128)(2,1)}), bf16[2048,768]{1,0:T(8,128)(2,1)}) %all-gather.6.cloned.1.call-update) | async-done | bytes 3145744 | tf_op jit(solution)/shard_map/all_gather | solution.py:190
  355.0 7.1 fusion.49
  368.5 4.5 fusion.84
  373.0 109.5 %reduce-scatter.7.cloned.1.call-done = f32[512,768]{1,0:T(8,128)} async-done(((f32[2048,768]{1,0:T(8,128)}), f32[512,768]{1,0:T(8,128)}) %reduce-scatter.7.cloned.1.call-update) | async-done | bytes 1572880 | tf_op jit(solution)/shard_map/reduce_scatter | solution.py:197
  488.4 63.7 %all-gather.8.cloned.1.call-done = bf16[2048,768]{1,0:T(8,128)(2,1)} async-done(((bf16[512,768]{1,0:T(8,128)(2,1)}), bf16[2048,768]{1,0:T(8,128)(2,1)}) %all-gather.8.cloned.1.call-update) | async-done | bytes 3145744 | tf_op jit(solution)/shard_map/all_gather | solution.py:208
  552.2 8.8 fusion.53
  563.7 7.0 fusion.44
  570.8 109.5 %reduce-scatter.9.cloned.1.call-done = f32[512,768]{1,0:T(8,128)} async-done(((f32[2048,768]{1,0:T(8,128)}), f32[512,768]{1,0:T(8,128)}) %reduce-scatter.9.cloned.1.call-update) | async-done | bytes 1572880 | tf_op jit(solution)/shard_map/reduce_scatter | solution.py:221
  680.3 4.1 multiply_reduce_fusion.1
  686.4 7.1 fusion.86
  693.5 6.8 fusion.42
  700.3 50.2 %all-gather.10.cloned.1.call-done = bf16[2048,768]{1,0:T(8,128)(2,1)} async-done(((bf16[512,768]{1,0:T(8,128)(2,1)}), bf16[2048,768]{1,0:T(8,128)(2,1)}) %all-gather.10.cloned.1.call-update) | async-done | bytes 3145744 | tf_op jit(solution)/shard_map/all_gather | solution.py:223
  750.5 3.1 convolution_convert_fusion
  755.2 159.2 %while.28 = (s32[]{:T(128)}, f32[2048,3,64]{0,2,1:T(8,128)}, f32[2048,3,64]{0,2,1:T(8,128)}, f32[4,512,3,64]{1,0,3,2:T(4,128)}, bf16[4,512,3,64]{1,3,2,0:T(8,128...) while((s32[]{:T(128)}, f32[2048,3,64]{0,2,1:T(8,128)}, ...), condition=%wide.region_20.21_spmd.clone, body=%wide.region_18.20_spmd.clone.sunk | while | flops 2063563264 | bytes 145678608 | solution.py:150
  756.1 3.0 fusion.140
  759.1 5.6 fusion.142
  764.7 5.8 multiply_reduce_fusion.7
  770.5 6.1 multiply_convert_fusion.5
  776.6 5.1 fusion.143
  781.7 3.4 fusion.141
  785.6 8.6 dynamic_update_slice.20
  797.9 6.2 fusion.142
  804.1 5.8 multiply_reduce_fusion.7
  809.9 6.1 multiply_convert_fusion.5
  816.0 5.1 fusion.143
  821.2 4.0 fusion.141
  825.6 8.6 dynamic_update_slice.20
  837.9 6.2 fusion.142
  844.1 5.8 multiply_reduce_fusion.7
  849.9 6.1 multiply_convert_fusion.5
  856.0 5.1 fusion.143
  861.2 4.0 fusion.141
  865.6 8.6 dynamic_update_slice.20
  874.9 3.0 fusion.140
  877.9 6.2 fusion.142
  884.2 5.8 multiply_reduce_fusion.7
  889.9 6.1 multiply_convert_fusion.5
  896.0 5.1 fusion.143
  901.2 4.0 fusion.141
  905.6 8.6 dynamic_update_slice.20
  923.0 3.2 fusion.65
  927.7 4.0 bitcast_convert_fusion
  933.1 16.1 %all-reduce.2 = (f32[2,768]{1,0:T(2,128)S(1)}, f32[2,768]{1,0:T(2,128)S(1)}) all-reduce(f32[2,768]{1,0:T(2,128)S(1)} %pad_maximum_fusion.11, f32[2,768]{1,0:T(2,128)S(1)} %pad_maximum_fusion.12), channel_id=1, replica_groups=mesh['dp'=8,'tensor'=4] {'tensor'}, use_global_device_ids=true, to_apply=%region_28.29 | all-reduce | flops 3072 | bytes 24576 | tf_op jit(solution)/shard_map/psum | solution.py:253
  949.1 23.7 %all-reduce = (f32[2,768]{1,0:T(2,128)}, f32[2,768]{1,0:T(2,128)}) all-reduce(f32[2,768]{1,0:T(2,128)S(1)} %get-tuple-element.263, f32[2,768]{1,0:T(2,128)S(1)} %get-tuple-element.264), channel_id=1, replica_groups=mesh['dp'=8,'tensor'=4] {'dp'}, use_global_device_ids=true, to_apply=%region_29.30 | all-reduce | flops 3072 | bytes 24576 | tf_op jit(solution)/shard_map/psum | solution.py:254
  972.9 91.7 %all-reduce.5.cloned.1.call-done = (f32[768,3,192]{0,2,1:T(8,128)}, f32[192,768]{1,0:T(8,128)}, f32[768,2,768]{2,0,1:T(8,128)}, f32[768,768]{1,0:T(8,128)}) async-done(((f32[768,3,192]{0,2,1:T(8,128)}, f32[192,768]{1,0:T(8,128)}, f32[768,2,768]{2,0,1:T(8,128)}, f32[768,768]{1,0:T(8,128)}), (f32[768,3,192]{0,2,1:T(8,128)}, f32[192,768]{1,0:T(8,128)}, f32[768,2,768]{2,0,1:T(8,128)}, ...) | async-done | bytes 9437200 | tf_op jit(solution)/shard_map/psum | solution.py:254
  1064.6 8.3 copy.41
  1072.9 54.5 %reduce-scatter.11.cloned.1.call-done = bf16[512,768]{1,0:T(8,128)(2,1)} async-done(((bf16[2048,768]{1,0:T(8,128)(2,1)}), bf16[512,768]{1,0:T(8,128)(2,1)}) %reduce-scatter.11.cloned.1.call-update) | async-done | bytes 786448 | tf_op jit(solution)/shard_map/reduce_scatter | solution.py:248
  (226 shorter events, 66.4 us)
Async XLA Ops:
  7.2 347.9 %copy-start = (bf16[768,2,768]{2,1,0:T(2,128)(2,1)S(1)}, bf16[768,2,768]{2,1,0:T(2,128)(2,1)}, u32[]{:S(2)}) copy-start(bf16[768,2,768]{2,1,0:T(2,128)(2,1)} %param.17) | copy-start | bytes 7077892
  7.2 68.6 %all-gather.12.cloned.1.call-start = ((), (), s32[]{:S(2)}) async-start(), calls=%async_computation.11 | async-start | bytes 3932160 | tf_op jit(solution)/shard_map/all_gather | solution.py:169
  7.9 278.7 %reduce-scatter.5.cloned.1.call-start = ((), (), s32[]{:S(2)}) async-start(), calls=%async_computation.4 | async-start | bytes 7864320 | tf_op jit(solution)/shard_map/reduce_scatter | solution.py:180
  12.7 68.6 %copy-start.20 = (f32[2048,32]{0,1:T(8,128)}, f32[2048,32]{0,1:T(8,128)S(1)}, u32[]{:S(2)}) copy-start(f32[2048,32]{0,1:T(8,128)S(1)} %get-tuple-element.293) | copy-start | bytes 786436
  12.7 68.6 %copy-start.22 = (f32[2048,32]{0,1:T(8,128)}, f32[2048,32]{0,1:T(8,128)S(1)}, u32[]{:S(2)}) copy-start(f32[2048,32]{0,1:T(8,128)S(1)} %get-tuple-element.294) | copy-start | bytes 786436
  81.8 1.7 copy-start.26
  91.0 6.8 copy-start.9
  112.7 6.8 copy-start.9
  134.5 6.8 copy-start.9
  156.2 6.8 copy-start.9
  170.5 2.9 copy-start.30
  177.1 177.9 %all-gather.6.cloned.1.call-start = ((), (), s32[]{:S(2)}) async-start(), calls=%async_computation.5 | async-start | bytes 3932160 | tf_op jit(solution)/shard_map/all_gather | solution.py:190
  288.5 1.1 copy-start.7
  290.9 191.6 %reduce-scatter.7.cloned.1.call-start = ((), (), s32[]{:S(2)}) async-start(), calls=%async_computation.6 | async-start | bytes 7864320 | tf_op jit(solution)/shard_map/reduce_scatter | solution.py:197
  362.1 4.6 copy-start.14
  362.1 6.4 copy-start.38
  366.7 1.8 copy-start.19
  372.9 179.2 %all-gather.8.cloned.1.call-start = ((), (), s32[]{:S(2)}) async-start(), calls=%async_computation.7 | async-start | bytes 3932160 | tf_op jit(solution)/shard_map/all_gather | solution.py:208
  482.5 2.8 copy-start.11
  484.9 1.7 copy-start.10
  488.0 192.3 %reduce-scatter.9.cloned.1.call-start = ((), (), s32[]{:S(2)}) async-start(), calls=%async_computation.8 | async-start | bytes 7864320 | tf_op jit(solution)/shard_map/reduce_scatter | solution.py:221
  561.0 1.6 copy-start.40
  561.0 2.7 copy-start.42
  570.7 109.6 %copy-start.8 = (f32[512,768]{1,0:T(8,128)S(1)}, f32[512,768]{1,0:T(8,128)}, u32[]{:S(2)}) copy-start(f32[512,768]{1,0:T(8,128)} %copy-done.7) | copy-start | bytes 4718596
  570.7 109.6 %copy-start.12 = (bf16[1,512,768]{2,1,0:T(8,128)(2,1)S(1)}, bf16[1,512,768]{2,1,0:T(8,128)(2,1)}, u32[]{:S(2)}) copy-start(bf16[1,512,768]{2,1,0:T(8,128)(2,1)} %param.21) | copy-start | bytes 2359300
  570.7 179.8 %all-gather.10.cloned.1.call-start = ((), (), s32[]{:S(2)}) async-start(), calls=%async_computation.9 | async-start | bytes 3932160 | tf_op jit(solution)/shard_map/all_gather | solution.py:223
  686.3 378.3 %all-reduce.5.cloned.1.call-start = ((), (), s32[]{:S(2)}) async-start(), calls=%async_computation.12 | async-start | bytes 18874368 | tf_op jit(solution)/shard_map/psum | solution.py:254
  686.4 7.1 copy-start.37
  686.4 7.1 copy-start.41
  686.4 7.1 copy-start.43
  755.3 3.7 copy-start.4
  756.1 3.0 copy-start.3
  776.6 5.1 copy-start.2
  781.7 12.5 %copy-start.5 = (bf16[2048,3,64]{0,2,1:T(8,128)(2,1)S(1)}, bf16[2048,3,64]{0,2,1:T(8,128)(2,1)}, u32[]{:S(2)}) copy-start(bf16[2048,3,64]{0,2,1:T(8,128)(2,1)} %copy-done.4) | copy-start | bytes 2359300 | tf_op jit(solution)/shard_map/while
  794.2 3.7 copy-start.4
  794.9 3.0 copy-start.3
  816.0 5.1 copy-start.2
  821.1 13.1 %copy-start.5 = (bf16[2048,3,64]{0,2,1:T(8,128)(2,1)S(1)}, bf16[2048,3,64]{0,2,1:T(8,128)(2,1)}, u32[]{:S(2)}) copy-start(bf16[2048,3,64]{0,2,1:T(8,128)(2,1)} %copy-done.4) | copy-start | bytes 2359300 | tf_op jit(solution)/shard_map/while
  834.2 3.7 copy-start.4
  834.9 3.0 copy-start.3
  856.0 5.1 copy-start.2
  861.2 13.1 %copy-start.5 = (bf16[2048,3,64]{0,2,1:T(8,128)(2,1)S(1)}, bf16[2048,3,64]{0,2,1:T(8,128)(2,1)}, u32[]{:S(2)}) copy-start(bf16[2048,3,64]{0,2,1:T(8,128)(2,1)} %copy-done.4) | copy-start | bytes 2359300 | tf_op jit(solution)/shard_map/while
  874.2 3.7 copy-start.4
  874.9 3.0 copy-start.3
  896.0 5.1 copy-start.2
  901.2 13.1 %copy-start.5 = (bf16[2048,3,64]{0,2,1:T(8,128)(2,1)S(1)}, bf16[2048,3,64]{0,2,1:T(8,128)(2,1)}, u32[]{:S(2)}) copy-start(bf16[2048,3,64]{0,2,1:T(8,128)(2,1)} %copy-done.4) | copy-start | bytes 2359300 | tf_op jit(solution)/shard_map/while
  914.4 4.1 copy-start.6
  914.4 4.1 copy-start.21
  916.9 1.6 copy-start.23
  918.5 4.1 copy-start.27
  918.5 2.2 copy-start.18
  919.0 1.9 copy-start.16
  920.9 2.1 copy-start.36
  926.3 1.4 copy-start.39
  926.3 201.1 %reduce-scatter.11.cloned.1.call-start = ((), (), s32[]{:S(2)}) async-start(), calls=%async_computation.10 | async-start | bytes 3932160 | tf_op jit(solution)/shard_map/reduce_scatter | solution.py:248
  931.7 1.1 copy-start.13
  931.7 1.3 copy-start.33
  931.7 1.3 copy-start.32
  931.7 1.3 copy-start.31
  1064.6 62.8 %copy-start.17 = (f32[512,768]{1,0:T(8,128)S(1)}, f32[512,768]{1,0:T(8,128)}, u32[]{:S(2)}) copy-start(f32[512,768]{1,0:T(8,128)} %get-tuple-element.266) | copy-start | bytes 4718596
  1072.9 56.9 %copy-start.25 = (f32[768,3,192]{0,2,1:T(8,128)S(1)}, f32[768,3,192]{0,2,1:T(8,128)}, u32[]{:S(2)}) copy-start(f32[768,3,192]{0,2,1:T(8,128)} %get-tuple-element.489) | copy-start | bytes 5308420
  1129.8 1.4 copy-start.29
  1129.8 2.7 copy-start.24
  1131.2 2.6 copy-start.1
  (4 other events, 3.5 us)
Sparse Core Ops, SparseCore 0:
  9.6 66.1 all-gather.11
  177.2 109.3 reduce-scatter.4
  291.0 64.0 all-gather.5
  373.1 109.3 reduce-scatter.6
  488.1 64.0 all-gather.7
  570.8 109.3 reduce-scatter.8
  686.4 64.0 all-gather.9
  926.4 138.1 all-reduce.4
  1067.0 60.3 reduce-scatter.10
where the time goes:
time: 1150 us; the launch traced here: 1140 us
  waiting for transfers between devices  716 us (62%)
  matrix products  213 us (19%)
  other arithmetic  83.2 us (7%)
  local copies, waits for them, and re-layouts  72.4 us (6%)
  blocking collectives  39.8 us (3%)
  between operations  14.8 us (1%)
    reduce_scatter x1, waiting for transfers between devices, on_device(): lax.psum_scatter(normed_part, 'tensor', scatter_dimension=0, tiled=True)  110 us
    reduce_scatter x1, waiting for transfers between devices, on_device(): lax.psum_scatter(jnp.dot(hidden, w_down, preferred_element_type=jnp.float...  110 us
    reduce_scatter x1, waiting for transfers between devices, on_device(): lax.psum_scatter(jnp.dot(heads_out, w_out, preferred_element_type=jnp.flo...  109 us
    psum x1, waiting for transfers between devices, on_device(): lax.psum((grad_w_qkv, grad_w_out, grad_w_gate_up, grad_w_down, gains_sum,...  91.7 us
    all_gather x1, waiting for transfers between devices, on_device(): normed_all = lax.all_gather(normed_low, 'tensor', axis=0, tiled=True)  63.9 us
    all_gather x1, waiting for transfers between devices, on_device(): lax.all_gather(grad_z2.astype(jnp.bfloat16), 'tensor', axis=0, tiled=True)  63.7 us
    all_gather x1, waiting for transfers between devices, on_device(): gathered = lax.all_gather(local_tokens, 'tensor', axis=0, tiled=True)  63.1 us
    reduce_scatter x1, waiting for transfers between devices, on_device(): lax.psum_scatter(input_part.astype(jnp.bfloat16), 'tensor', scatter_dimen...  54.5 us
  transfers between devices with their start and end apart: 9, of which 9 were waited for; matrix products, arithmetic and copies ran while one was open for 3% of the time, Pallas kernels for 0%

commit v1 on v0

--- a/solution.py
+++ b/solution.py
@@ -19,7 +19,8 @@
     length = segments_row.shape[0]
     onehot = (segments_row[:, None] == jnp.arange(SEGS, dtype=jnp.int32)[None, :]).astype(jnp.int32)
     counts = jnp.sum(onehot, axis=0)
-    starts = jnp.cumsum(counts) - counts
+    order = jnp.arange(SEGS, dtype=jnp.int32)
+    starts = jnp.sum(jnp.where(order[None, :] < order[:, None], counts[None, :], 0), axis=1)
     first_place = jnp.sum(onehot * starts[None, :], axis=1)
     places = (jnp.arange(length, dtype=jnp.int32) - first_place).astype(jnp.float32)
     inverse = jnp.exp(-2.0 * jnp.arange(HEAD_DIM // 2, dtype=jnp.float32) / HEAD_DIM * log_base)

time: 1150 us -> 1150 us (level)
  no operation moved by 1% of the time
where the time goes in v1:
time: 1150 us; the launch traced here: 1140 us
  waiting for transfers between devices  716 us (62%)
  matrix products  213 us (19%)
  other arithmetic  83.1 us (7%)
  local copies, waits for them, and re-layouts  72.4 us (6%)
  blocking collectives  39.8 us (3%)
  between operations  14.8 us (1%)
    reduce_scatter x1, waiting for transfers between devices, on_device(): lax.psum_scatter(normed_part, 'tensor', scatter_dimension=0, tiled=True)  110 us
    reduce_scatter x1, waiting for transfers between devices, on_device(): lax.psum_scatter(jnp.dot(hidden, w_down, preferred_element_type=jnp.float...  110 us
    reduce_scatter x1, waiting for transfers between devices, on_device(): lax.psum_scatter(jnp.dot(heads_out, w_out, preferred_element_type=jnp.flo...  109 us
    psum x1, waiting for transfers between devices, on_device(): lax.psum((grad_w_qkv, grad_w_out, grad_w_gate_up, grad_w_down, gains_sum,...  91.7 us
    all_gather x1, waiting for transfers between devices, on_device(): normed_all = lax.all_gather(normed_low, 'tensor', axis=0, tiled=True)  63.9 us
    all_gather x1, waiting for transfers between devices, on_device(): lax.all_gather(grad_z2.astype(jnp.bfloat16), 'tensor', axis=0, tiled=True)  63.7 us
    all_gather x1, waiting for transfers between devices, on_device(): gathered = lax.all_gather(local_tokens, 'tensor', axis=0, tiled=True)  63.2 us
    reduce_scatter x1, waiting for transfers between devices, on_device(): lax.psum_scatter(input_part.astype(jnp.bfloat16), 'tensor', scatter_dimen...  54.5 us
  transfers between devices with their start and end apart: 9, of which 9 were waited for; matrix products, arithmetic and copies ran while one was open for 3% of the time, Pallas kernels for 0%

profile of v1, /device:TPU:0, one launch (start us, length us, event | category | flops | bytes accessed | tf_op | source)
XLA Modules:
  0.0 1140.8 jit_solution(12358380017882607845)
XLA Ops:
  12.7 63.2 %all-gather.12.cloned.1.call-done = bf16[1,2048,768]{2,1,0:T(8,128)(2,1)} async-done(((bf16[1,512,768]{2,1,0:T(8,128)(2,1)}), bf16[1,2048,768]{2,1,0:T(8,128)(2,1)}) %all-gather.12.cloned.1.call-update) | async-done | bytes 3145744 | tf_op jit(solution)/shard_map/all_gather | solution.py:170
  75.8 4.1 fusion.51
  83.5 87.0 %while.27 = (s32[]{:T(128)}, bf16[4,512,3,64]{1,3,2,0:T(8,128)(2,1)}, f32[4,3,512]{2,1,0:T(4,128)S(1)}, s32[4,512]{1,0:T(4,128)S(1)}, s32[1,2048]{1,0:T(1,128)S(...) while((s32[]{:T(128)}, ...), condition=%wide.region_6.7_spmd, body=%wide.region_3.6_spmd.sunk | while | flops 844200448 | bytes 47124624 | solution.py:109
  84.2 6.8 fusion.128
  91.0 6.8 fusion.129
  97.8 7.4 fusion.130
  105.9 6.8 fusion.128
  112.7 6.8 fusion.129
  119.6 7.4 fusion.130
  127.7 6.8 fusion.128
  134.5 6.8 fusion.129
  141.3 7.4 fusion.130
  149.4 6.8 fusion.128
  156.2 6.8 fusion.129
  163.1 7.4 fusion.130
  173.4 3.7 fusion.83
  177.8 108.8 %reduce-scatter.5.cloned.1.call-done = f32[512,768]{1,0:T(8,128)} async-done(((f32[2048,768]{1,0:T(8,128)}), f32[512,768]{1,0:T(8,128)}) %reduce-scatter.5.cloned.1.call-update) | async-done | bytes 1572880 | tf_op jit(solution)/shard_map/reduce_scatter | solution.py:181
  291.1 63.9 %all-gather.6.cloned.1.call-done = bf16[2048,768]{1,0:T(8,128)(2,1)} async-done(((bf16[512,768]{1,0:T(8,128)(2,1)}), bf16[2048,768]{1,0:T(8,128)(2,1)}) %all-gather.6.cloned.1.call-update) | async-done | bytes 3145744 | tf_op jit(solution)/shard_map/all_gather | solution.py:191
  355.0 7.1 fusion.49
  368.5 4.5 fusion.84
  373.0 109.5 %reduce-scatter.7.cloned.1.call-done = f32[512,768]{1,0:T(8,128)} async-done(((f32[2048,768]{1,0:T(8,128)}), f32[512,768]{1,0:T(8,128)}) %reduce-scatter.7.cloned.1.call-update) | async-done | bytes 1572880 | tf_op jit(solution)/shard_map/reduce_scatter | solution.py:198
  488.4 63.7 %all-gather.8.cloned.1.call-done = bf16[2048,768]{1,0:T(8,128)(2,1)} async-done(((bf16[512,768]{1,0:T(8,128)(2,1)}), bf16[2048,768]{1,0:T(8,128)(2,1)}) %all-gather.8.cloned.1.call-update) | async-done | bytes 3145744 | tf_op jit(solution)/shard_map/all_gather | solution.py:209
  552.2 8.8 fusion.53
  563.7 7.0 fusion.44
  570.8 109.5 %reduce-scatter.9.cloned.1.call-done = f32[512,768]{1,0:T(8,128)} async-done(((f32[2048,768]{1,0:T(8,128)}), f32[512,768]{1,0:T(8,128)}) %reduce-scatter.9.cloned.1.call-update) | async-done | bytes 1572880 | tf_op jit(solution)/shard_map/reduce_scatter | solution.py:222
  680.3 4.1 multiply_reduce_fusion.1
  686.4 7.1 fusion.86
  693.5 6.8 fusion.42
  700.3 50.2 %all-gather.10.cloned.1.call-done = bf16[2048,768]{1,0:T(8,128)(2,1)} async-done(((bf16[512,768]{1,0:T(8,128)(2,1)}), bf16[2048,768]{1,0:T(8,128)(2,1)}) %all-gather.10.cloned.1.call-update) | async-done | bytes 3145744 | tf_op jit(solution)/shard_map/all_gather | solution.py:224
  750.5 3.1 convolution_convert_fusion
  755.2 159.2 %while.28 = (s32[]{:T(128)}, f32[2048,3,64]{0,2,1:T(8,128)}, f32[2048,3,64]{0,2,1:T(8,128)}, f32[4,512,3,64]{1,0,3,2:T(4,128)}, bf16[4,512,3,64]{1,3,2,0:T(8,128...) while((s32[]{:T(128)}, f32[2048,3,64]{0,2,1:T(8,128)}, ...), condition=%wide.region_20.21_spmd.clone, body=%wide.region_18.20_spmd.clone.sunk | while | flops 2063563264 | bytes 145678608 | solution.py:151
  756.1 3.0 fusion.140
  759.1 5.6 fusion.142
  764.7 5.8 multiply_reduce_fusion.7
  770.5 6.1 multiply_convert_fusion.5
  776.6 5.1 fusion.143
  781.7 3.4 fusion.141
  785.6 8.6 dynamic_update_slice.20
  797.9 6.2 fusion.142
  804.1 5.8 multiply_reduce_fusion.7
  809.9 6.1 multiply_convert_fusion.5
  816.0 5.1 fusion.143
  821.2 4.0 fusion.141
  825.6 8.6 dynamic_update_slice.20
  837.9 6.2 fusion.142
  844.1 5.8 multiply_reduce_fusion.7
  849.9 6.1 multiply_convert_fusion.5
  856.0 5.1 fusion.143
  861.2 4.0 fusion.141
  865.6 8.6 dynamic_update_slice.20
  874.9 3.0 fusion.140
  877.9 6.2 fusion.142
  884.2 5.8 multiply_reduce_fusion.7
  889.9 6.1 multiply_convert_fusion.5
  896.0 5.1 fusion.143
  901.2 4.0 fusion.141
  905.6 8.6 dynamic_update_slice.20
  923.0 3.2 fusion.65
  927.7 4.0 bitcast_convert_fusion
  933.1 16.1 %all-reduce.2 = (f32[2,768]{1,0:T(2,128)S(1)}, f32[2,768]{1,0:T(2,128)S(1)}) all-reduce(f32[2,768]{1,0:T(2,128)S(1)} %pad_maximum_fusion.11, f32[2,768]{1,0:T(2,128)S(1)} %pad_maximum_fusion.12), channel_id=1, replica_groups=mesh['dp'=8,'tensor'=4] {'tensor'}, use_global_device_ids=true, to_apply=%region_28.29 | all-reduce | flops 3072 | bytes 24576 | tf_op jit(solution)/shard_map/psum | solution.py:254
  949.1 23.7 %all-reduce = (f32[2,768]{1,0:T(2,128)}, f32[2,768]{1,0:T(2,128)}) all-reduce(f32[2,768]{1,0:T(2,128)S(1)} %get-tuple-element.263, f32[2,768]{1,0:T(2,128)S(1)} %get-tuple-element.264), channel_id=1, replica_groups=mesh['dp'=8,'tensor'=4] {'dp'}, use_global_device_ids=true, to_apply=%region_29.30 | all-reduce | flops 3072 | bytes 24576 | tf_op jit(solution)/shard_map/psum | solution.py:255
  972.9 91.7 %all-reduce.5.cloned.1.call-done = (f32[768,3,192]{0,2,1:T(8,128)}, f32[192,768]{1,0:T(8,128)}, f32[768,2,768]{2,0,1:T(8,128)}, f32[768,768]{1,0:T(8,128)}) async-done(((f32[768,3,192]{0,2,1:T(8,128)}, f32[192,768]{1,0:T(8,128)}, f32[768,2,768]{2,0,1:T(8,128)}, f32[768,768]{1,0:T(8,128)}), (f32[768,3,192]{0,2,1:T(8,128)}, f32[192,768]{1,0:T(8,128)}, f32[768,2,768]{2,0,1:T(8,128)}, ...) | async-done | bytes 9437200 | tf_op jit(solution)/shard_map/psum | solution.py:255
  1064.6 8.3 copy.41
  1072.9 54.5 %reduce-scatter.11.cloned.1.call-done = bf16[512,768]{1,0:T(8,128)(2,1)} async-done(((bf16[2048,768]{1,0:T(8,128)(2,1)}), bf16[512,768]{1,0:T(8,128)(2,1)}) %reduce-scatter.11.cloned.1.call-update) | async-done | bytes 786448 | tf_op jit(solution)/shard_map/reduce_scatter | solution.py:249
  (225 shorter events, 66.3 us)
Async XLA Ops:
  7.2 347.9 %copy-start = (bf16[768,2,768]{2,1,0:T(2,128)(2,1)S(1)}, bf16[768,2,768]{2,1,0:T(2,128)(2,1)}, u32[]{:S(2)}) copy-start(bf16[768,2,768]{2,1,0:T(2,128)(2,1)} %param.17) | copy-start | bytes 7077892
  7.2 68.6 %all-gather.12.cloned.1.call-start = ((), (), s32[]{:S(2)}) async-start(), calls=%async_computation.11 | async-start | bytes 3932160 | tf_op jit(solution)/shard_map/all_gather | solution.py:170
  7.9 278.7 %reduce-scatter.5.cloned.1.call-start = ((), (), s32[]{:S(2)}) async-start(), calls=%async_computation.4 | async-start | bytes 7864320 | tf_op jit(solution)/shard_map/reduce_scatter | solution.py:181
  12.6 68.7 %copy-start.20 = (f32[2048,32]{0,1:T(8,128)}, f32[2048,32]{0,1:T(8,128)S(1)}, u32[]{:S(2)}) copy-start(f32[2048,32]{0,1:T(8,128)S(1)} %get-tuple-element.293) | copy-start | bytes 786436
  12.6 68.7 %copy-start.22 = (f32[2048,32]{0,1:T(8,128)}, f32[2048,32]{0,1:T(8,128)S(1)}, u32[]{:S(2)}) copy-start(f32[2048,32]{0,1:T(8,128)S(1)} %get-tuple-element.294) | copy-start | bytes 786436
  81.8 1.7 copy-start.26
  91.0 6.8 copy-start.9
  112.7 6.8 copy-start.9
  134.5 6.8 copy-start.9
  156.2 6.8 copy-start.9
  170.5 2.9 copy-start.30
  177.1 177.9 %all-gather.6.cloned.1.call-start = ((), (), s32[]{:S(2)}) async-start(), calls=%async_computation.5 | async-start | bytes 3932160 | tf_op jit(solution)/shard_map/all_gather | solution.py:191
  288.5 1.1 copy-start.7
  290.9 191.6 %reduce-scatter.7.cloned.1.call-start = ((), (), s32[]{:S(2)}) async-start(), calls=%async_computation.6 | async-start | bytes 7864320 | tf_op jit(solution)/shard_map/reduce_scatter | solution.py:198
  362.1 4.6 copy-start.14
  362.1 6.4 copy-start.38
  366.7 1.8 copy-start.19
  372.9 179.2 %all-gather.8.cloned.1.call-start = ((), (), s32[]{:S(2)}) async-start(), calls=%async_computation.7 | async-start | bytes 3932160 | tf_op jit(solution)/shard_map/all_gather | solution.py:209
  482.5 2.8 copy-start.11
  484.9 1.7 copy-start.10
  488.0 192.3 %reduce-scatter.9.cloned.1.call-start = ((), (), s32[]{:S(2)}) async-start(), calls=%async_computation.8 | async-start | bytes 7864320 | tf_op jit(solution)/shard_map/reduce_scatter | solution.py:222
  561.0 1.6 copy-start.40
  561.0 2.7 copy-start.42
  570.7 109.6 %copy-start.8 = (f32[512,768]{1,0:T(8,128)S(1)}, f32[512,768]{1,0:T(8,128)}, u32[]{:S(2)}) copy-start(f32[512,768]{1,0:T(8,128)} %copy-done.7) | copy-start | bytes 4718596
  570.7 109.6 %copy-start.12 = (bf16[1,512,768]{2,1,0:T(8,128)(2,1)S(1)}, bf16[1,512,768]{2,1,0:T(8,128)(2,1)}, u32[]{:S(2)}) copy-start(bf16[1,512,768]{2,1,0:T(8,128)(2,1)} %param.21) | copy-start | bytes 2359300
  570.7 179.8 %all-gather.10.cloned.1.call-start = ((), (), s32[]{:S(2)}) async-start(), calls=%async_computation.9 | async-start | bytes 3932160 | tf_op jit(solution)/shard_map/all_gather | solution.py:224
  686.3 378.3 %all-reduce.5.cloned.1.call-start = ((), (), s32[]{:S(2)}) async-start(), calls=%async_computation.12 | async-start | bytes 18874368 | tf_op jit(solution)/shard_map/psum | solution.py:255
  686.4 7.1 copy-start.37
  686.4 7.1 copy-start.41
  686.4 7.1 copy-start.43
  755.3 3.7 copy-start.4
  756.0 3.0 copy-start.3
  776.6 5.1 copy-start.2
  781.7 12.5 %copy-start.5 = (bf16[2048,3,64]{0,2,1:T(8,128)(2,1)S(1)}, bf16[2048,3,64]{0,2,1:T(8,128)(2,1)}, u32[]{:S(2)}) copy-start(bf16[2048,3,64]{0,2,1:T(8,128)(2,1)} %copy-done.4) | copy-start | bytes 2359300 | tf_op jit(solution)/shard_map/while
  794.2 3.7 copy-start.4
  794.9 3.0 copy-start.3
  816.0 5.1 copy-start.2
  821.1 13.1 %copy-start.5 = (bf16[2048,3,64]{0,2,1:T(8,128)(2,1)S(1)}, bf16[2048,3,64]{0,2,1:T(8,128)(2,1)}, u32[]{:S(2)}) copy-start(bf16[2048,3,64]{0,2,1:T(8,128)(2,1)} %copy-done.4) | copy-start | bytes 2359300 | tf_op jit(solution)/shard_map/while
  834.2 3.7 copy-start.4
  834.9 3.0 copy-start.3
  856.0 5.1 copy-start.2
  861.2 13.1 %copy-start.5 = (bf16[2048,3,64]{0,2,1:T(8,128)(2,1)S(1)}, bf16[2048,3,64]{0,2,1:T(8,128)(2,1)}, u32[]{:S(2)}) copy-start(bf16[2048,3,64]{0,2,1:T(8,128)(2,1)} %copy-done.4) | copy-start | bytes 2359300 | tf_op jit(solution)/shard_map/while
  874.2 3.7 copy-start.4
  874.9 3.0 copy-start.3
  896.0 5.1 copy-start.2
  901.2 13.1 %copy-start.5 = (bf16[2048,3,64]{0,2,1:T(8,128)(2,1)S(1)}, bf16[2048,3,64]{0,2,1:T(8,128)(2,1)}, u32[]{:S(2)}) copy-start(bf16[2048,3,64]{0,2,1:T(8,128)(2,1)} %copy-done.4) | copy-start | bytes 2359300 | tf_op jit(solution)/shard_map/while
  914.4 4.1 copy-start.6
  914.4 4.1 copy-start.21
  916.9 1.6 copy-start.23
  918.5 4.1 copy-start.27
  918.5 2.2 copy-start.18
  919.0 1.9 copy-start.16
  920.9 2.1 copy-start.36
  926.3 1.4 copy-start.39
  926.3 201.1 %reduce-scatter.11.cloned.1.call-start = ((), (), s32[]{:S(2)}) async-start(), calls=%async_computation.10 | async-start | bytes 3932160 | tf_op jit(solution)/shard_map/reduce_scatter | solution.py:249
  931.7 1.1 copy-start.13
  931.7 1.3 copy-start.33
  931.7 1.3 copy-start.32
  931.7 1.3 copy-start.31
  1064.6 62.8 %copy-start.17 = (f32[512,768]{1,0:T(8,128)S(1)}, f32[512,768]{1,0:T(8,128)}, u32[]{:S(2)}) copy-start(f32[512,768]{1,0:T(8,128)} %get-tuple-element.266) | copy-start | bytes 4718596
  1072.9 56.9 %copy-start.25 = (f32[768,3,192]{0,2,1:T(8,128)S(1)}, f32[768,3,192]{0,2,1:T(8,128)}, u32[]{:S(2)}) copy-start(f32[768,3,192]{0,2,1:T(8,128)} %get-tuple-element.489) | copy-start | bytes 5308420
  1129.8 1.4 copy-start.29
  1129.8 2.7 copy-start.24
  1131.2 2.6 copy-start.1
  (4 other events, 3.5 us)
Sparse Core Ops, SparseCore 0:
  9.6 66.1 all-gather.11
  177.2 109.3 reduce-scatter.4
  291.0 64.0 all-gather.5
  373.1 109.3 reduce-scatter.6
  488.1 64.0 all-gather.7
  570.8 109.3 reduce-scatter.8
  686.4 64.0 all-gather.9
  926.4 138.1 all-reduce.4
  1067.0 60.3 reduce-scatter.10

commit v2 on v0

v2 whole, which is shorter than its diff:
```python
import math

import jax
import jax.numpy as jnp
from jax import lax
from jax.experimental import pallas as pl
from jax.experimental.pallas import tpu as pltpu
from jax.sharding import PartitionSpec as P

HEAD_DIM = 64
SEGS = 8
BLK = 256
F32 = jnp.float32
BF16 = jnp.bfloat16

epsilon = 1e-05
far_below = -1e30
log_base = math.log(1000.0)


def nn(a, b):
    return lax.dot_general(a, b, (((1,), (0,)), ((), ())), preferred_element_type=F32)


def nt(a, b):
    return lax.dot_general(a, b, (((1,), (1,)), ((), ())), preferred_element_type=F32)


def tn(a, b):
    return lax.dot_general(a, b, (((0,), (0,)), ((), ())), preferred_element_type=F32)


def owner_bits(core, h, k):
    low, high = k & 1, k >> 1
    return (core | (low << 1) | (high << 2)) if h == 0 else (core | (high << 1) | (low << 2))


def attend_forward_kernel(
    sc, tok, cos, sin, seg, own, half, other, w, qa, ka, kt, vn, ot, logsum, keep, send, va, mx, acc, sem
):
    heads = 3
    width = heads * HEAD_DIM
    cross = sc[0]
    place = sc[1]

    @pl.when(sc[2] == 0)
    def _():
        copy = pltpu.make_async_copy(own, w, sem.at[0])
        copy.start()
        copy.wait()

    @pl.when(sc[2] == 1)
    def _():
        copies = []
        for core, source in enumerate((half, other)):
            for h in range(2):
                for k in range(4):
                    row = pl.multiple_of((place ^ owner_bits(core, h, k)) * 96 + h * 48, 16)
                    copies.append(
                        pltpu.make_async_copy(
                            source.at[h * 4 + k], w.at[pl.ds(row, 48)], sem.at[len(copies)]
                        )
                    )
                    copies[-1].start()
        for copy in copies:
            copy.wait()

    def project(e, _):
        at = pl.ds(pl.multiple_of(e * 512, 512), 512)
        made = nt(w[: 3 * width], tok[e])
        c, s = cos[:, at], sin[:, at]
        hot = (seg[:, at] == lax.broadcasted_iota(jnp.int32, (SEGS, 512), 0)).astype(F32)
        rest = jnp.zeros((64 - SEGS, 512), F32)
        one_row = (lax.broadcasted_iota(jnp.int32, (16, 512), 0) == 0).astype(F32)
        for h in range(heads):
            r = h * HEAD_DIM
            a1, a2 = made[r : r + 32], made[r + 32 : r + 64]
            q = jnp.concatenate([a1 * c - a2 * s, a2 * c + a1 * s], axis=0).astype(BF16).astype(F32)
            qa[h, :, at] = jnp.concatenate([q * 0.125, hot, rest], axis=0).astype(BF16)
            r += width
            a1, a2 = made[r : r + 32], made[r + 32 : r + 64]
            k = jnp.concatenate([a1 * c - a2 * s, a2 * c + a1 * s], axis=0)
            kt[h * HEAD_DIM : (h + 1) * HEAD_DIM, at] = k.astype(BF16)
            ka[h, at, :] = jnp.concatenate([k, (1.0 - hot) * far_below, rest], axis=0).T.astype(BF16)
            r += width
            v = made[r : r + 64]
            va[h, :, at] = jnp.concatenate([v, one_row], axis=0).astype(BF16)
            vn[h, at, :] = jnp.concatenate([v, jnp.zeros_like(v)], axis=0).T[:, :HEAD_DIM].astype(BF16)
        return 0

    lax.fori_loop(0, 4, project, 0)

    def query_block(i, _):
        at = pl.ds(pl.multiple_of(i * BLK, BLK), BLK)
        for h in range(heads):
            mx[h] = jnp.full((1, BLK), -3e38, F32)
            acc[h] = jnp.zeros((80, BLK), F32)

        def key_block(j, _):
            here = pl.ds(pl.multiple_of((j ^ cross) * BLK, BLK), BLK)
            for h in range(heads):
                scores = nn(ka[h, here, :], qa[h, :, at])
                before = mx[h]
                largest = jnp.maximum(before, jnp.max(scores, axis=0, keepdims=True))
                weights = jnp.exp(scores - largest).astype(BF16)
                acc[h] = acc[h] * jnp.exp(before - largest) + nn(va[h, :, here], weights)
                mx[h] = largest
            return 0

        lax.fori_loop(sc[8 + (i ^ cross)], sc[16 + (i ^ cross)], key_block, 0)
        for h in range(heads):
            total = acc[h, 64:65, :]
            ot[h * HEAD_DIM : (h + 1) * HEAD_DIM, at] = (acc[h, :64, :] / total).astype(BF16)
            logsum[pl.ds(h, 1), at] = mx[h] + jnp.log(total)
        return 0

    lax.fori_loop(0, 2048 // BLK, query_block, 0)
    for e in range(4):
        part = tn(ot[:, e * 512 : (e + 1) * 512], w[3 * width :])
        if e < 2:
            keep[e] = part
        else:
            send[e - 2] = part.astype(BF16)


def attend_backward_kernel(
    sc, gb, tok, w, qa, ka, kt, vn, ot, logsum, cos, sin, grads, keep, send, dot_, inner, dq, dk, dv, gp
):
    heads = 3
    width = heads * HEAD_DIM
    cross = sc[0]
    quarter = sc[3]

    def begin(e, _):
        at = pl.ds(pl.multiple_of(e * 512, 512), 512)
        made = nt(w[3 * width :], gb[e]).astype(BF16)
        dot_[:, at] = made
        product = made.astype(F32) * ot[:, at].astype(F32)
        for h in range(heads):
            inner[pl.ds(h, 1), at] = jnp.sum(product[h * HEAD_DIM : (h + 1) * HEAD_DIM], axis=0, keepdims=True)
        return 0

    lax.fori_loop(0, 4, begin, 0)
    dq[...] = jnp.zeros_like(dq)

    def key_block(j, _):
        here = pl.ds(pl.multiple_of(j * BLK, BLK), BLK)
        for h in range(heads):
            dk[h] = jnp.zeros((HEAD_DIM, BLK), F32)
            dv[h] = jnp.zeros((HEAD_DIM, BLK), F32)

        def query_block(i, _):
            at = pl.ds(pl.multiple_of((i ^ cross) * BLK, BLK), BLK)
            for h in range(heads):
                rows = slice(h * HEAD_DIM, (h + 1) * HEAD_DIM)
                scores = nn(ka[h, here, :], qa[h, :, at])
                probability = jnp.exp(scores - logsum[pl.ds(h, 1), at])
                rise = nn(vn[h, here, :], dot_[rows, at])
                slope = (probability * (rise - inner[pl.ds(h, 1), at])).astype(BF16)
                dv[h] += nt(dot_[rows, at], probability.astype(BF16))
                dk[h] += nt(qa[h, :HEAD_DIM, at], slope)
                dq[rows, at] += nn(kt[rows, here], slope)
            return 0

        lax.fori_loop(sc[8 + (j ^ cross)], sc[16 + (j ^ cross)], query_block, 0)
        c, s = cos[:, here], sin[:, here]
        for h in range(heads):
            d1, d2 = dk[h, :32, :], dk[h, 32:, :]
            r = width + h * HEAD_DIM
            gp[r : r + 64, here] = jnp.concatenate([d1 * c + d2 * s, d2 * c - d1 * s], axis=0).astype(BF16)
            r += width
            gp[r : r + 64, here] = dv[h].astype(BF16)
        return 0

    lax.fori_loop(0, 2048 // BLK, key_block, 0)

    def turn(e, _):
        at = pl.ds(pl.multiple_of(e * 512, 512), 512)
        c, s = cos[:, at] * 0.125, sin[:, at] * 0.125
        for h in range(heads):
            r = h * HEAD_DIM
            d1, d2 = dq[r : r + 32, at], dq[r + 32 : r + 64, at]
            gp[r : r + 64, at] = jnp.concatenate([d1 * c + d2 * s, d2 * c - d1 * s], axis=0).astype(BF16)
        return 0

    lax.fori_loop(0, 4, turn, 0)
    for e in range(4):
        part = tn(gp[:, e * 512 : (e + 1) * 512], w[: 3 * width])
        if e < 2:
            keep[e] = part
        else:
            send[e - 2] = part.astype(BF16)
    for block in range(4):
        if block < 3:
            rows = slice(block * width, (block + 1) * width)
            made = sum(nn(gp[rows, e * 512 : (e + 1) * 512], tok[e]) for e in range(4))
        else:
            made = sum(nn(ot[:, e * 512 : (e + 1) * 512], gb[e]) for e in range(4))
        away = block ^ quarter
        grads[0, away] = made[:96].astype(BF16)
        grads[1, ((away & 1) << 1) | (away >> 1)] = made[96:].astype(BF16)


def row_mean(v):
    return jnp.mean(v, axis=-1, keepdims=True)


def norm_forward(summed):
    centred = summed - row_mean(summed)
    inverse = lax.rsqrt(row_mean(centred * centred) + epsilon)
    return centred * inverse, inverse


def norm_backward(scaled, normalized, inverse):
    return inverse * (scaled - row_mean(scaled) - normalized * row_mean(scaled * normalized))


def feed_forward_kernel(sc, x, b_own, b_far, cot, gain, bias, *refs):
    pieces = refs[:8]
    out, gz1, gz1_low, sums, keep_hi, send_hi, keep_lo, send_lo = refs[8:16]
    w, slope_g, slope_u, hid, nb, nbt, gm, gmt, total, norm1, inv1, dw, in_sem, out_sem = refs[16:]
    place = sc[1]

    def loads(ez):
        copies = []
        for core in range(2):
            for h in range(2):
                for k in range(4):
                    row = pl.multiple_of((place ^ owner_bits(core, h, k)) * 96 + h * 48, 16)
                    copies.append(
                        pltpu.make_async_copy(
                            pieces[ez * 2 + core].at[h * 4 + k],
                            w.at[ez, :, pl.ds(row, 48), :],
                            in_sem.at[ez, len(copies)],
                        )
                    )
        return copies

    for ez in range(4):
        for copy in loads(ez):
            copy.start()

    n1, i1 = norm_forward(x[...].astype(F32) + (b_own[...] + b_far[...].astype(F32)))
    norm1[...] = n1
    inv1[...] = jnp.broadcast_to(i1, inv1.shape)
    low = (n1 * gain[0:1, :] + bias[0:1, :]).astype(BF16)
    nb[...] = low
    nbt[...] = low.astype(F32).T.astype(BF16)
    total[...] = n1 * gain[0:1, :] + bias[0:1, :]
    for ez in range(4):
        for copy in loads(ez):
            copy.wait()

    def forward(ez, _):
        gate = nn(nb[...], w[ez, 0])
        up = nn(nb[...], w[ez, 1])
        sig = 1.0 / (1.0 + jnp.exp(-gate))
        active = gate * sig
        low = (active * up).astype(BF16)
        hid[ez] = low
        slope_u[ez] = active
        slope_g[ez] = up * sig * (1.0 + gate * (1.0 - sig))
        total[...] += nn(low, w[ez, 2])
        return 0

    lax.fori_loop(0, 4, forward, 0)
    n2, i2 = norm_forward(total[...])
    out[...] = (n2 * gain[1:2, :] + bias[1:2, :]).astype(BF16)
    g = cot[...].astype(F32)
    sums[1:2, :] = jnp.sum(g * n2, axis=0, keepdims=True)
    sums[3:4, :] = jnp.sum(g, axis=0, keepdims=True)
    gz2 = norm_backward(g * gain[1:2, :], n2, i2)
    total[...] = gz2
    gm[...] = gz2.astype(BF16)
    gmt[...] = gz2.T.astype(BF16)

    def stores(keep, send, i):
        copies = []
        for core, target in enumerate((keep, send)):
            for h in range(2):
                for k in range(4):
                    row = pl.multiple_of((place ^ owner_bits(core, h, k)) * 96 + h * 48, 16)
                    copies.append(
                        pltpu.make_async_copy(
                            dw.at[i, :, pl.ds(row, 48), :],
                            target.at[i, h * 4 + k],
                            out_sem.at[i, len(copies)],
                        )
                    )
        return copies

    groups = ((2, keep_hi, send_hi), (0, keep_lo, send_lo))
    for number, (first, keep, send) in enumerate(groups):

        def backward(i, _, first=first, keep=keep, send=send, number=number):
            ez = first + i
            if number:
                for copy in stores(*groups[0][1:], i):
                    copy.wait()
            grad_hidden = nt(gm[...], w[ez, 2])
            dw[i, 2] = nn(gmt[...], hid[ez]).astype(BF16)
            gate = (grad_hidden * slope_g[ez]).astype(BF16)
            dw[i, 0] = nn(nbt[...], gate).astype(BF16)
            up = (grad_hidden * slope_u[ez]).astype(BF16)
            dw[i, 1] = nn(nbt[...], up).astype(BF16)
            total[...] += nt(gate, w[ez, 0]) + nt(up, w[ez, 1])
            for copy in stores(keep, send, i):
                copy.start()
            return 0

        lax.fori_loop(0, 2, backward, 0)

    g = total[...]
    sums[0:1, :] = jnp.sum(g * norm1[...], axis=0, keepdims=True)
    sums[2:3, :] = jnp.sum(g, axis=0, keepdims=True)
    sums[4:8, :] = jnp.zeros((4, 768), F32)
    made = norm_backward(g * gain[0:1, :], norm1[...], inv1[:, 0:1])
    gz1[...] = made
    gz1_low[...] = made.astype(BF16)
    for i in range(2):
        for copy in stores(*groups[1][1:], i):
            copy.wait()


def solution(mesh):
    dp, tensor = mesh.shape["dp"], mesh.shape["tensor"]
    assert tensor == 4 and dp >= 8 and dp & (dp - 1) == 0
    extra = [1 << b for b in range(3, dp.bit_length() - 1)]
    both = ("dp", "tensor")

    def cell(i, k):
        return i * tensor + k

    def over(x, bit):
        return lax.ppermute(x, "dp", [(i, i ^ bit) for i in range(dp)])

    def along(x, bit):
        return lax.ppermute(x, "tensor", [(i, i ^ bit) for i in range(tensor)])

    away = [(i, k) for i in range(dp) for k in range(tensor) if (i & 1) != (k >> 1)]

    def trade(x):
        return lax.ppermute(x, both, [(cell(i, k), cell(i ^ 1, k ^ 2)) for i, k in away])

    def core(x):
        return over(x, 1)

    def across(x):
        return over(x, 2)

    def down(x):
        return over(x, 4)

    def plane_gather(a, b):
        a2 = jnp.stack([a, across(a)])
        b2 = jnp.stack([b, down(b)])
        half = jnp.concatenate([a2, down(a2), b2, across(b2)])
        return half, core(half)

    def on_device(tokens, segments, w_qkv, w_out, w_gate_up, w_down, norm_gain, norm_bias, cotangent):
        p, z = lax.axis_index("dp"), lax.axis_index("tensor")
        rho = z >> 1
        swapped = (p & 1) != rho
        slot = jnp.where(swapped, z ^ 2, z)
        place = p & 7

        x = tokens[0]
        traded = trade(jnp.stack([x, cotangent[0]]))
        x = jnp.where(swapped, traded[0], x)
        cot = jnp.where(swapped, traded[1], cotangent[0])
        pair = jnp.stack([x, along(x, 1)])
        tok = jnp.concatenate([pair, core(pair)])

        own = jnp.concatenate([w_qkv.transpose(1, 2, 0).reshape(576, 768), w_out])
        block = along(lax.dynamic_slice(own, (place * 96, 0), (96, 768)), 2)
        far_half, far_other = plane_gather(block[:48], block[48:])

        rows = lax.dynamic_slice(w_gate_up, (place * 96, 0, 0), (96, 2, 768))
        block = jnp.stack(
            [rows[:, 0], rows[:, 1], lax.dynamic_slice(w_down, (place * 96, 0), (96, 768))]
        ).reshape(3, 2, 48, 768)
        blocks = [block, along(block, 1)]
        blocks += [along(blocks[0], 2), along(blocks[1], 2)]
        pieces = []
        for b in blocks:
            pieces += plane_gather(b[:, 0], b[:, 1])

        row = jnp.where(swapped, core(segments), segments)[0]
        length = row.shape[0]
        onehot = (row[None, :] == jnp.arange(SEGS, dtype=jnp.int32)[:, None]).astype(jnp.int32)
        counts = jnp.sum(onehot, axis=1)
        order = jnp.arange(SEGS, dtype=jnp.int32)
        starts = jnp.sum(jnp.where(order[None, :] < order[:, None], counts[None, :], 0), axis=1)
        first_place = jnp.sum(onehot * starts[:, None], axis=0)
        end_place = first_place + jnp.sum(onehot * counts[:, None], axis=0)
        lo = first_place.reshape(-1, BLK)[:, 0] // BLK
        hi = (end_place.reshape(-1, BLK)[:, -1] + (BLK - 1)) // BLK

        def shards(v):
            v = v.reshape(4, 512)
            v = jnp.where((slot & 1) == 1, jnp.concatenate([v[1:2], v[0:1], v[3:4], v[2:3]]), v)
            v = jnp.where((slot & 2) == 2, jnp.concatenate([v[2:4], v[0:2]]), v)
            return v.reshape(1, length)

        seg = shards(row)
        places = shards(jnp.arange(length, dtype=jnp.int32) - first_place).astype(F32)
        inverse = jnp.exp(-2.0 * jnp.arange(HEAD_DIM // 2, dtype=F32) / HEAD_DIM * log_base)
        angles = inverse[:, None] * places
        cos, sin = jnp.cos(angles), jnp.sin(angles)
        head = jnp.stack([slot * 2, place, swapped.astype(jnp.int32), place >> 1] + [slot * 0] * 4)
        sc = jnp.concatenate([head.astype(jnp.int32), lo, hi]).astype(jnp.int32)

        smem = pl.BlockSpec(memory_space=pltpu.SMEM)
        vmem = pl.BlockSpec(memory_space=pltpu.VMEM)
        hbm = pl.BlockSpec(memory_space=pl.ANY)

        def shape(*dims, dtype=BF16):
            return jax.ShapeDtypeStruct(dims, dtype)

        w, qa, ka, kt, vn, ot, logsum, keep, send = pl.pallas_call(
            attend_forward_kernel,
            name="attend_forward",
            out_shape=(
                shape(768, 768), shape(3, 128, length), shape(3, length, 128), shape(192, length),
                shape(3, length, 64), shape(192, length), shape(8, length, dtype=F32),
                shape(2, 512, 768, dtype=F32), shape(2, 512, 768),
            ),
            in_specs=[smem, vmem, vmem, vmem, vmem, hbm, hbm, hbm],
            out_specs=(vmem,) * 9,
            scratch_shapes=[
                pltpu.VMEM((3, 80, length), BF16),
                pltpu.VMEM((3, 1, BLK), F32),
                pltpu.VMEM((3, 80, BLK), F32),
                pltpu.SemaphoreType.DMA((16,)),
            ],
            compiler_params=pltpu.CompilerParams(vmem_limit_bytes=48 << 20),
            cost_estimate=pl.CostEstimate(flops=20_000_000_000, bytes_accessed=24_000_000, transcendentals=6_000_000),
        )(sc, tok, cos, sin, seg, own, far_half, far_other)

        mine = keep + core(send)
        far = along(mine[1].astype(BF16), 1)

        scratch = [
            pltpu.VMEM((4, 3, 768, 768), BF16),
            pltpu.VMEM((4, 512, 768), F32),
            pltpu.VMEM((4, 512, 768), F32),
            pltpu.VMEM((4, 512, 768), BF16),
            pltpu.VMEM((512, 768), BF16),
            pltpu.VMEM((768, 512), BF16),
            pltpu.VMEM((512, 768), BF16),
            pltpu.VMEM((768, 512), BF16),
            pltpu.VMEM((512, 768), F32),
            pltpu.VMEM((512, 768), F32),
            pltpu.VMEM((512, 128), F32),
            pltpu.VMEM((2, 3, 768, 768), BF16),
            pltpu.SemaphoreType.DMA((4, 16)),
            pltpu.SemaphoreType.DMA((2, 16)),
        ]
        out, gz1, gz1_low, sums, keep_hi, send_hi, keep_lo, send_lo = pl.pallas_call(
            feed_forward_kernel,
            name="feed_forward",
            out_shape=(
                shape(512, 768), shape(512, 768, dtype=F32), shape(512, 768), shape(8, 768, dtype=F32),
                shape(2, 8, 3, 48, 768), shape(2, 8, 3, 48, 768), shape(2, 8, 3, 48, 768), shape(2, 8, 3, 48, 768),
            ),
            in_specs=[smem] + [vmem] * 6 + [hbm] * 8,
            out_specs=(vmem,) * 4 + (hbm,) * 4,
            scratch_shapes=scratch,
            compiler_params=pltpu.CompilerParams(vmem_limit_bytes=60 << 20),
            cost_estimate=pl.CostEstimate(flops=22_000_000_000, bytes_accessed=36_000_000, transcendentals=3_000_000),
        )(sc, x, mine[0], far, cot, norm_gain, norm_bias, *pieces)

        pair = jnp.stack([gz1_low, along(gz1_low, 1)])
        gb = jnp.concatenate([pair, core(pair)])
        back = trade(out)
        output = jnp.where(swapped, back, out)[None]

        def add(a, b):
            return (a.astype(F32) + b.astype(F32)).astype(BF16)

        parts = []
        for keep_w, send_w in ((keep_hi, send_hi), (keep_lo, send_lo)):
            v = add(keep_w, core(send_w))
            a, b = v[:, 0:4], v[:, 4:8]
            a, b = add(a[:, 0:2], down(a[:, 2:4])), add(b[:, 0:2], across(b[:, 2:4]))
            a, b = add(a[:, 0], across(a[:, 1])), add(b[:, 0], down(b[:, 1]))
            parts.append(jnp.stack([a, b], axis=1))
        v = add(parts[1], along(parts[0], 2))
        v = add(v[0], along(v[1], 1))
        for bit in extra:
            v = add(v, over(v, bit))
        ff_half, ff_other = plane_gather(v[0], v[1])

        for bit in [1 << b for b in range(dp.bit_length() - 1)]:
            sums = sums + over(sums, bit)
        for bit in (1, 2):
            sums = sums + along(sums, bit)

        grads, keep, send = pl.pallas_call(
            attend_backward_kernel,
            name="attend_backward",
            out_shape=(shape(2, 4, 96, 768), shape(2, 512, 768, dtype=F32), shape(2, 512, 768)),
            in_specs=[smem] + [vmem] * 11,
            out_specs=(vmem,) * 3,
            scratch_shapes=[
                pltpu.VMEM((192, length), BF16),
                pltpu.VMEM((8, length), F32),
                pltpu.VMEM((192, length), F32),
                pltpu.VMEM((3, 64, BLK), F32),
                pltpu.VMEM((3, 64, BLK), F32),
                pltpu.VMEM((576, length), BF16),
            ],
            compiler_params=pltpu.CompilerParams(vmem_limit_bytes=48 << 20),
            cost_estimate=pl.CostEstimate(flops=40_000_000_000, bytes_accessed=24_000_000, transcendentals=6_000_000),
        )(sc, gb, tok, w, qa, ka, kt, vn, ot, logsum, cos, sin)

        mine = keep + core(send)
        got = gz1 + (mine[0] + along(mine[1].astype(BF16), 1).astype(F32))
        back = trade(got.astype(BF16))
        grad_tokens = jnp.where(swapped, back.astype(F32), got)[None]

        a, b = grads[0], grads[1]
        a, b = add(a[0:2], down(a[2:4])), add(b[0:2], across(b[2:4]))
        a, b = add(a[0], across(a[1])), add(b[0], down(b[1]))
        v = jnp.stack([a, b])
        v = add(v, lax.ppermute(v, both, [(cell(i, k), cell(i, k ^ 2)) for i, k in away]))
        for bit in extra:
            v = add(v, over(v, bit))
        sibling = lax.ppermute(
            v, both, [(cell(i, k), cell(i ^ 1, k)) for i in range(dp) for k in range(tensor) if (i, k) not in away]
        )
        v = jnp.where(swapped, sibling, v)
        a = jnp.stack([v[0], across(v[0])])
        a = jnp.concatenate([a, down(a)])
        b = jnp.stack([v[1], down(v[1])])
        b = jnp.concatenate([b, across(b)])
        b = b.reshape(2, 2, 96, 768).transpose(1, 0, 2, 3).reshape(4, 96, 768)
        full = jnp.stack([a, b], axis=1)

        def unturn(v, bit, axis_index):
            n = v.shape[0]
            turned = v.reshape(n // (2 << axis_index), 2, 1 << axis_index, *v.shape[1:])[:, ::-1].reshape(v.shape)
            return jnp.where(((place >> bit) & 1) == 1, turned, v)

        full = unturn(unturn(full, 1, 0), 2, 1).reshape(768, 768).astype(F32)
        grad_w_qkv = full[:576].reshape(3, 192, 768).transpose(2, 0, 1)
        grad_w_out = full[576:]

        ff = jnp.stack([ff_half, ff_other]).reshape(2, 2, 2, 2, 3, 48, 768)
        ff = jnp.stack([ff[:, 0], ff[:, 1].transpose(0, 2, 1, 3, 4, 5)], axis=3)
        ff = ff.transpose(1, 2, 0, 3, 4, 5, 6).reshape(8, 2, 3, 48, 768)
        ff = unturn(unturn(unturn(ff, 0, 0), 1, 1), 2, 2)
        ff = ff.transpose(2, 0, 1, 3, 4).reshape(3, 768, 768)
        grad_w_gate_up = ff[:2].transpose(1, 0, 2).astype(F32)
        grad_w_down = ff[2].T.astype(F32)
        return (
            output, grad_tokens, grad_w_qkv, grad_w_out, grad_w_gate_up, grad_w_down, sums[0:2], sums[2:4],
        )

    placed = (
        P("dp", "tensor", None),
        P("dp", None),
        P(None, None, "tensor"),
        P("tensor", None),
        P(None, None, "tensor"),
        P("tensor", None),
        P(),
        P(),
        P("dp", "tensor", None),
    )
    return jax.shard_map(
        on_device,
        mesh=mesh,
        in_specs=placed,
        out_specs=(
            P("dp", "tensor", None),
            P("dp", "tensor", None),
            P(None, None, "tensor"),
            P("tensor", None),
            P(None, None, "tensor"),
            P("tensor", None),
            P(),
            P(),
        ),
        check_vma=False,
    )
```

time: 1150 us -> 588 us (0.51)
  waiting for transfers between devices: 716 us -> 272 us
  matrix products: 213 us -> 0 us
  Pallas kernels: 0 us -> 107 us
  starting transfers between devices: 0.99 us -> 88.1 us
  blocking collectives: 39.8 us -> 0 us
  other arithmetic: 83.2 us -> 48.2 us
  local copies, waits for them, and re-layouts: 72.4 us -> 58 us
  between operations: 14.8 us -> 2.46 us
    reduce_scatter x4 -> x0, waiting for transfers between devices: 382 us -> none  [the longest x1 110 us: on_device(): lax.psum_scatter(normed_part, 'tensor', scatter_dimension=0, tiled=True)]
    ppermute x0 -> x73, waiting for transfers between devices: none -> 272 us  [the longest x12 141 us: along(): return lax.ppermute(x, 'tensor', [(i, i ^ bit) for i in range(tensor)])]
    all_gather x4 -> x0, waiting for transfers between devices: 241 us -> none  [the longest x1 63.9 us: on_device(): normed_all = lax.all_gather(normed_low, 'tensor', axis=0, tiled=True)]
    dot_general x39 -> x0, matrix products: 209 us -> none  [the longest x8 39.2 us: block_scores(): jnp.einsum('qhe,khe->hqk', query_block, keys_all, preferred_element_type=...]
    pallas_call x0 -> x3, Pallas kernels: none -> 107 us  [the longest x1 37.9 us: on_device(): pl.pallas_call(feed_forward_kernel, name='feed_forward', out_shape=(shape...]
    psum x1 -> x0, waiting for transfers between devices: 91.7 us -> none  [on_device(): lax.psum((grad_w_qkv, grad_w_out, grad_w_gate_up, grad_w_down, gains_sum,...]
    ppermute x0 -> x73, starting transfers between devices: none -> 88.1 us  [the longest x56 69.4 us: over(): return lax.ppermute(x, 'dp', [(i, i ^ bit) for i in range(dp)])]
    psum x2 -> x0, blocking collectives: 39.8 us -> none  [the longest x1 23.7 us: on_device(): lax.psum((grad_w_qkv, grad_w_out, grad_w_gate_up, grad_w_down, gains_sum,...]
  transfers between devices with their start and end apart: 9 -> 73, of which waited for: 9 -> 37; matrix products, arithmetic and copies ran while one was open for 3% -> 11% of each run, Pallas kernels for 0% -> 12%
where the time goes in v2:
time: 588 us; the launch traced here: 576 us
  waiting for transfers between devices  272 us (46%)
  Pallas kernels  107 us (18%)
  starting transfers between devices  88.1 us (15%)
  local copies, waits for them, and re-layouts  58 us (10%)
  other arithmetic  48.2 us (8%)
    ppermute x12, waiting for transfers between devices, along(): return lax.ppermute(x, 'tensor', [(i, i ^ bit) for i in range(tensor)])  141 us
    ppermute x56, waiting for transfers between devices, over(): return lax.ppermute(x, 'dp', [(i, i ^ bit) for i in range(dp)])  127 us
    ppermute x56, starting transfers between devices, over(): return lax.ppermute(x, 'dp', [(i, i ^ bit) for i in range(dp)])  69.4 us
    pallas_call x1, Pallas kernels, on_device(): pl.pallas_call(feed_forward_kernel, name='feed_forward', out_shape=(shape...  37.9 us
    pallas_call x1, Pallas kernels, on_device(): pl.pallas_call(attend_backward_kernel, name='attend_backward', out_shape=...  35 us
    pallas_call x1, Pallas kernels, on_device(): pl.pallas_call(attend_forward_kernel, name='attend_forward', out_shape=(s...  34.1 us
    unnamed x129, local copies, waits for them, and re-layouts  23.3 us
    rev x7, local copies, waits for them, and re-layouts, unturn(): v.reshape(n // (2 << axis_index), 2, 1 << axis_index, *v.shape[1:])[:, ::-1]  16.5 us
  transfers between devices with their start and end apart: 73, of which 37 were waited for; matrix products, arithmetic and copies ran while one was open for 11% of the time, Pallas kernels for 12%

profile of v2, /device:TPU:0, one launch (start us, length us, event | category | flops | bytes accessed | tf_op | source)
XLA Modules:
  0.0 576.2 jit_solution(12507704075058971690)
XLA Ops:
  2.6 3.1 collective-permute-start.17
  5.6 2.6 collective-permute-start.23
  10.6 1.8 collective-permute-start.1
  18.9 32.0 %collective-permute-done.4 = bf16[96,768]{1,0:T(8,128)(2,1)} collective-permute-done((bf16[96,768]{1,0:T(8,128)(2,1)}, bf16[96,768]{1,0:T(8,128)(2,1)}, u32[]{:S(2)}, u32[]{:S(2)}) %collective-permute-start.4) | collective-permute-done | bytes 147488 | tf_op jit(solution)/shard_map/ppermute | solution.py:338
  59.3 4.6 collective-permute-done.7
  66.0 4.5 collective-permute-done.6
  77.9 8.3 %collective-permute-done.18 = bf16[3,48,768]{2,1,0:T(8,128)(2,1)S(1)} collective-permute-done((bf16[3,48,768]{2,1,0:T(8,128)(2,1)S(1)}, bf16[3,48,768]{2,1,0:T(8,128)(2,1)S(1)}, u32[]{:S(2)}, u32[]{:S(2)}) %collective-permute-start.18) | collective-permute-done | bytes 221216 | tf_op jit(solution)/shard_map/ppermute | solution.py:335
  89.4 2.7 collective-permute-done.24
  95.5 2.5 fusion.15
  98.0 3.6 collective-permute-start.2
  102.3 23.6 %collective-permute-done.2 = bf16[512,768]{1,0:T(8,128)(2,1)S(1)} collective-permute-done((bf16[512,768]{1,0:T(8,128)(2,1)S(1)}, bf16[512,768]{1,0:T(8,128)(2,1)S(1)}, u32[]{:S(2)}, u32[]{:S(2)}) %collective-permute-start.2) | collective-permute-done | bytes 786464 | tf_op jit(solution)/shard_map/ppermute | solution.py:338
  125.9 2.0 collective-permute-start.25
  130.6 5.5 collective-permute-done.25
  136.1 2.5 collective-permute-start.30
  139.6 6.7 %collective-permute-done.30 = bf16[3,48,768]{2,1,0:T(8,128)(2,1)S(1)} collective-permute-done((bf16[3,48,768]{2,1,0:T(8,128)(2,1)S(1)}, bf16[3,48,768]{2,1,0:T(8,128)(2,1)S(1)}, u32[]{:S(2)}, u32[]{:S(2)}) %collective-permute-start.30) | collective-permute-done | bytes 221216 | tf_op jit(solution)/shard_map/ppermute | solution.py:335
  147.8 2.0 pad_maximum_fusion.1.tok
  149.8 2.0 collective-permute-start.31
  151.8 34.1 %attend_forward.1 = (bf16[768,768]{1,0:T(8,128)(2,1)S(1)}, bf16[3,128,2048]{2,1,0:T(8,128)(2,1)}, bf16[3,2048,128]{2,1,0:T(8,128)(2,1)}, bf16[192,2048]{1,0:T(8,...) custom-call(s32[24]{0:T(128)S(1)} %concatenate.76.sc, ...), custom_call_target="tpu_custom_call" | custom-call | flops 20000000000 | bytes 24000000 | tf_op jit(solution)/shard_map/attend_forward/pallas_call | solution.py:420
  187.4 10.4 %collective-permute-start.33 = (bf16[2,3,48,768]{3,2,1,0:T(8,128)(2,1)S(1)}, bf16[2,3,48,768]{3,2,1,0:T(8,128)(2,1)S(1)}, u32[]{:S(2)}, u32[]{:S(2)}) collective-permute-start(bf16[2,3,48,768]{3,2,1,0:T(8,128)(2,1)S(1)} %pad_maximum_fusion.21), channel_id=1, source_target_pairs={{0,8},{4,12},{8,0},{12,4},{16,24},{20,28},{24,16},{28,20},{1,9},{5... | collective-permute-start | bytes 1327112 | tf_op jit(solution)/shard_map/ppermute | solution.py:335
  200.1 8.0 %collective-permute-done.33 = bf16[2,3,48,768]{3,2,1,0:T(8,128)(2,1)S(1)} collective-permute-done((bf16[2,3,48,768]{3,2,1,0:T(8,128)(2,1)S(1)}, bf16[2,3,48,768]{3,2,1,0:T(8,128)(2,1)S(1)}, u32[]{:S(2)}, u32[]{:S(2)}) %collective-permute-start.33) | collective-permute-done | bytes 442400 | tf_op jit(solution)/shard_map/ppermute | solution.py:335
  211.9 16.7 %collective-permute-done.11.b_far = bf16[512,768]{1,0:T(8,128)(2,1)S(1)} collective-permute-done((bf16[512,768]{1,0:T(8,128)(2,1)S(1)}, bf16[512,768]{1,0:T(8,128)(2,1)S(1)}, u32[]{:S(2)}, u32[]{:S(2)}) %collective-permute-start.11) | collective-permute-done | bytes 786464 | tf_op jit(solution)/shard_map/ppermute | solution.py:338
  229.6 37.9 %feed_forward.1 = (bf16[512,768]{1,0:T(8,128)(2,1)}, f32[512,768]{1,0:T(8,128)}, bf16[512,768]{1,0:T(8,128)(2,1)}, f32[8,768]{1,0:T(8,128)}, bf16[2,8,3,48,768]{...) custom-call(s32[24]{0:T(128)} %copy-done.2, ...), custom_call_target="tpu_custom_call" | custom-call | flops 22000001024 | bytes 36000000 | tf_op jit(solution)/shard_map/feed_forward/pallas_call | solution.py:459
  267.8 18.2 %collective-permute-done.36 = bf16[512,768]{1,0:T(8,128)(2,1)S(1)} collective-permute-done((bf16[512,768]{1,0:T(8,128)(2,1)}, bf16[512,768]{1,0:T(8,128)(2,1)S(1)}, u32[]{:S(2)}, u32[]{:S(2)}) %collective-permute-start.36) | collective-permute-done | bytes 786464 | tf_op jit(solution)/shard_map/ppermute | solution.py:338
  287.8 4.2 copy.83
  292.2 1.9 pad_maximum_fusion.2.gb
  294.6 35.0 %attend_backward.1 = (bf16[2,4,96,768]{3,2,1,0:T(8,128)(2,1)S(1)}, f32[2,512,768]{2,1,0:T(8,128)}, bf16[2,512,768]{2,1,0:T(8,128)(2,1)S(1)}) custom-call(s32[24]{0:T(128)S(1)} %copy-done.3, bf16[4,512,768]{2,1,0:T(8,128)(2,1)} %pad_maximum_fusion.2.gb, bf16[4,512,768]{2,1,0:T(8,128)(2,1)} %pad_maximum_fusion.1.tok, bf16[768,768]{1,0:T(8,128)(2,1)S(1)} %copy-done.5, ...), custom_call_target="tpu_custom_call" | custom-call | flops 40000000000 | bytes 24000000 | tf_op jit(solution)/shard_map/attend_backward/pallas_call | solution.py:499
  329.6 5.9 %collective-permute-start.41 = (bf16[2,96,768]{2,1,0:T(8,128)(2,1)S(1)}, bf16[2,96,768]{2,1,0:T(8,128)(2,1)S(1)}, u32[]{:S(2)}, u32[]{:S(2)}) collective-permute-start(bf16[2,96,768]{2,1,0:T(8,128)(2,1)S(1)} %get-tuple-element.93), channel_id=1, source_target_pairs={{0,16},{4,20},{8,24},{12,28},{16,0},{20,4},{24,8},{28,12},{1,17},{... | collective-permute-start | bytes 884744 | tf_op jit(solution)/shard_map/ppermute | solution.py:335
  335.6 4.8 collective-permute-start.43
  340.3 2.4 collective-permute-done.41
  342.7 4.8 collective-permute-done.43
  347.7 1.8 collective-permute-start.42
  357.6 3.5 collective-permute-done.69
  362.8 4.7 collective-permute-done.45
  367.6 2.2 collective-permute-start.46
  369.9 3.8 collective-permute-done.71
  374.5 4.0 collective-permute-done.72
  379.2 4.0 add_convert_fusion
  385.4 3.0 add_convert_fusion.1
  388.6 1.8 collective-permute-start.54
  390.9 14.8 %collective-permute-done.57 = bf16[2,2,3,48,768]{4,3,2,0,1:T(8,128)(2,1)S(1)} collective-permute-done((bf16[2,2,3,48,768]{4,3,2,0,1:T(8,128)(2,1)S(1)}, bf16[2,2,3,48,768]{4,3,2,0,1:T(8,128)(2,1)S(1)}, u32[]{:S(2)}, u32[]{:S(2)}) %collective-permute-start.57) | collective-permute-done | bytes 884768 | tf_op jit(solution)/shard_map/ppermute | solution.py:335
  408.5 18.1 %collective-permute-done.54 = bf16[2,2,3,48,768]{4,3,2,1,0:T(8,128)(2,1)S(1)} collective-permute-done((bf16[2,2,3,48,768]{4,3,2,1,0:T(8,128)(2,1)S(1)}, bf16[2,2,3,48,768]{4,3,2,1,0:T(8,128)(2,1)S(1)}, u32[]{:S(2)}, u32[]{:S(2)}) %collective-permute-start.54) | collective-permute-done | bytes 884768 | tf_op jit(solution)/shard_map/ppermute | solution.py:335
  427.1 3.7 collective-permute-done.52
  432.7 6.5 %collective-permute-done.58 = bf16[2,3,48,768]{3,2,1,0:T(8,128)(2,1)S(1)} collective-permute-done((bf16[2,3,48,768]{3,2,1,0:T(8,128)(2,1)S(1)}, bf16[2,3,48,768]{3,2,1,0:T(8,128)(2,1)S(1)}, u32[]{:S(2)}, u32[]{:S(2)}) %collective-permute-start.58) | collective-permute-done | bytes 442400 | tf_op jit(solution)/shard_map/ppermute | solution.py:335
  439.6 2.8 collective-permute-done.60
  444.7 6.2 %collective-permute-done.53 = bf16[2,3,48,768]{3,2,1,0:T(8,128)(2,1)S(1)} collective-permute-done((bf16[2,3,48,768]{3,2,1,0:T(8,128)(2,1)S(1)}, bf16[2,3,48,768]{3,2,1,0:T(8,128)(2,1)S(1)}, u32[]{:S(2)}, u32[]{:S(2)}) %collective-permute-start.53) | collective-permute-done | bytes 442400 | tf_op jit(solution)/shard_map/ppermute | solution.py:335
  451.4 3.7 collective-permute-done.55
  455.5 26.6 %collective-permute-done.61 = bf16[2,2,3,48,768]{4,3,2,0,1:T(8,128)(2,1)S(1)} collective-permute-done((bf16[2,2,3,48,768]{4,3,2,0,1:T(8,128)(2,1)S(1)}, bf16[2,2,3,48,768]{4,3,2,0,1:T(8,128)(2,1)S(1)}, u32[]{:S(2)}, u32[]{:S(2)}) %collective-permute-start.61) | collective-permute-done | bytes 884768 | tf_op jit(solution)/shard_map/ppermute | solution.py:338
  484.5 10.1 %collective-permute-done.62 = bf16[2,3,48,768]{3,2,1,0:T(8,128)(2,1)S(1)} collective-permute-done((bf16[2,3,48,768]{3,2,1,0:T(8,128)(2,1)S(1)}, bf16[2,3,48,768]{3,2,1,0:T(8,128)(2,1)S(1)}, u32[]{:S(2)}, u32[]{:S(2)}) %collective-permute-start.62) | collective-permute-done | bytes 442400 | tf_op jit(solution)/shard_map/ppermute | solution.py:338
  497.8 4.2 collective-permute-done.63
  505.7 6.7 %collective-permute-done.64 = bf16[2,3,48,768]{3,2,1,0:T(8,128)(2,1)S(1)} collective-permute-done((bf16[2,3,48,768]{3,2,1,0:T(8,128)(2,1)S(1)}, bf16[2,3,48,768]{3,2,1,0:T(8,128)(2,1)S(1)}, u32[]{:S(2)}, u32[]{:S(2)}) %collective-permute-start.64) | collective-permute-done | bytes 442400 | tf_op jit(solution)/shard_map/ppermute | solution.py:335
  515.5 5.8 %collective-permute-done.39 = bf16[512,768]{1,0:T(8,128)(2,1)S(1)} collective-permute-done((bf16[512,768]{1,0:T(8,128)(2,1)S(1)}, bf16[512,768]{1,0:T(8,128)(2,1)S(1)}, u32[]{:S(2)}, u32[]{:S(2)}) %collective-permute-start.39) | collective-permute-done | bytes 786464 | tf_op jit(solution)/shard_map/ppermute | solution.py:338
  525.5 2.4 rev.15
  527.9 2.9 maximum_select_fusion
  530.8 2.4 rev.16
  538.9 2.7 select_bitcast_fusion
  541.6 2.3 fusion.3
  545.7 2.1 rev.17
  547.8 3.7 bitcast_select_fusion.1
  551.5 4.1 rev.18
  555.6 2.2 select_select_fusion
  557.8 4.1 rev.19
  561.9 4.8 fusion.1
  567.8 5.8 %copy.89 = f32[768,2,768]{2,1,0:T(2,128)} copy(f32[768,2,768]{2,0,1:T(8,128)S(1)} %bitcast.297) | data formatting | bytes 9437184
  573.8 2.0 copy.90
  (346 shorter events, 99.9 us)
Async XLA Ops:
  2.6 71.0 %collective-permute-start.17 = (bf16[3,2,48,768]{3,2,0,1:T(8,128)(2,1)S(1)}, bf16[3,2,48,768]{3,2,0,1:T(8,128)(2,1)}, u32[]{:S(2)}, u32[]{:S(2)}) collective-permute-start(bf16[3,2,48,768]{3,2,0,1:T(8,128)(2,1)S(1)} %pad_maximum_fusion.13), channel_id=1, source_target_pairs={{0,1},{1,0},{2,3},{3,2},{4,5},{5,4},{6,7},{7,6},{8,9},{9,8},{10,11... | collective-permute-start | bytes 1327112 | tf_op jit(solution)/shard_map/ppermute | solution.py:338
  5.6 70.6 %collective-permute-start.23 = (bf16[3,2,48,768]{3,2,0,1:T(8,128)(2,1)S(1)}, bf16[3,2,48,768]{3,2,0,1:T(8,128)(2,1)S(1)}, u32[]{:S(2)}, u32[]{:S(2)}) collective-permute-start(bf16[3,2,48,768]{3,2,0,1:T(8,128)(2,1)S(1)} %pad_maximum_fusion.13), channel_id=1, source_target_pairs={{0,2},{1,3},{2,0},{3,1},{4,6},{5,7},{6,4},{7,5},{8,10},{9,11},{10,... | collective-permute-start | bytes 1327112 | tf_op jit(solution)/shard_map/ppermute | solution.py:338
  8.2 5.9 %collective-permute-start = (s32[1,2048]{1,0:T(1,128)S(1)}, s32[1,2048]{1,0:T(1,128)S(1)}, u32[]{:S(2)}, u32[]{:S(2)}) collective-permute-start(s32[1,2048]{1,0:T(1,128)S(1)} %copy-done.40), channel_id=1, source_target_pairs={{0,4},{4,0},{8,12},{12,8},{16,20},{20,16},{24,28},{28,24},{1,5},{5... | collective-permute-start | bytes 24584 | tf_op jit(solution)/shard_map/ppermute | solution.py:335
  9.0 42.0 %collective-permute-start.4 = (bf16[96,768]{1,0:T(8,128)(2,1)}, bf16[96,768]{1,0:T(8,128)(2,1)}, u32[]{:S(2)}, u32[]{:S(2)}) collective-permute-start(bf16[96,768]{1,0:T(8,128)(2,1)} %fusion.24), channel_id=1, source_target_pairs={{0,2},{1,3},{2,0},{3,1},{4,6},{5,7},{6,4},{7,5},{8,10},{9,11},{10,... | collective-permute-start | bytes 442376 | tf_op jit(solution)/shard_map/ppermute | solution.py:338
  10.6 84.8 %collective-permute-start.1 = (bf16[2,512,768]{2,1,0:T(8,128)(2,1)}, bf16[2,512,768]{2,1,0:T(8,128)(2,1)}, u32[]{:S(2)}, u32[]{:S(2)}) collective-permute-start(bf16[2,512,768]{2,1,0:T(8,128)(2,1)} %pad_maximum_fusion.4), channel_id=1, source_target_pairs={{2,4},{3,5},{4,2},{5,3},{10,12},{11,13},{12,10},{13,11},{18,20},{1... | collective-permute-start | bytes 4718600 | tf_op jit(solution)/shard_map/ppermute | solution.py:343
  14.1 40.2 %collective-permute-start.12 = (bf16[3,48,768]{2,1,0:T(8,128)(2,1)}, bf16[3,48,768]{2,1,0:T(8,128)(2,1)S(1)}, u32[]{:S(2)}, u32[]{:S(2)}) collective-permute-start(bf16[3,48,768]{2,1,0:T(8,128)(2,1)} %get-tuple-element.115), channel_id=1, source_target_pairs={{0,8},{4,12},{8,0},{12,4},{16,24},{20,28},{24,16},{28,20},{1,9},{5... | collective-permute-start | bytes 663560 | tf_op jit(solution)/shard_map/ppermute | solution.py:335
  51.0 13.4 %collective-permute-start.14 = (bf16[3,48,768]{2,1,0:T(8,128)(2,1)}, bf16[3,48,768]{2,1,0:T(8,128)(2,1)S(1)}, u32[]{:S(2)}, u32[]{:S(2)}) collective-permute-start(bf16[3,48,768]{2,1,0:T(8,128)(2,1)} %get-tuple-element.116), channel_id=1, source_target_pairs={{0,16},{4,20},{8,24},{12,28},{16,0},{20,4},{24,8},{28,12},{1,17},{... | collective-permute-start | bytes 663560 | tf_op jit(solution)/shard_map/ppermute | solution.py:335
  63.9 6.7 %collective-permute-start.6 = (bf16[2,48,768]{2,1,0:T(8,128)(2,1)S(1)}, bf16[2,48,768]{2,1,0:T(8,128)(2,1)S(1)}, u32[]{:S(2)}, u32[]{:S(2)}) collective-permute-start(bf16[2,48,768]{2,1,0:T(8,128)(2,1)S(1)} %pad_maximum_fusion.27), channel_id=1, source_target_pairs={{0,16},{4,20},{8,24},{12,28},{16,0},{20,4},{24,8},{28,12},{1,17},{... | collective-permute-start | bytes 442376 | tf_op jit(solution)/shard_map/ppermute | solution.py:335
  64.4 7.5 %collective-permute-start.8 = (bf16[2,48,768]{2,1,0:T(8,128)(2,1)S(1)}, bf16[2,48,768]{2,1,0:T(8,128)(2,1)S(1)}, u32[]{:S(2)}, u32[]{:S(2)}) collective-permute-start(bf16[2,48,768]{2,1,0:T(8,128)(2,1)S(1)} %pad_maximum_fusion.28), channel_id=1, source_target_pairs={{0,8},{4,12},{8,0},{12,4},{16,24},{20,28},{24,16},{28,20},{1,9},{5... | collective-permute-start | bytes 442376 | tf_op jit(solution)/shard_map/ppermute | solution.py:335
  70.5 23.3 %collective-permute-start.13 = (bf16[2,3,48,768]{3,2,1,0:T(8,128)(2,1)S(1)}, bf16[2,3,48,768]{3,2,1,0:T(8,128)(2,1)S(1)}, u32[]{:S(2)}, u32[]{:S(2)}) collective-permute-start(bf16[2,3,48,768]{3,2,1,0:T(8,128)(2,1)S(1)} %pad_maximum_fusion.14), channel_id=1, source_target_pairs={{0,16},{4,20},{8,24},{12,28},{16,0},{20,4},{24,8},{28,12},{1,17},{... | collective-permute-start | bytes 1327112 | tf_op jit(solution)/shard_map/ppermute | solution.py:335
  72.0 29.7 %collective-permute-start.15 = (bf16[2,3,48,768]{3,2,1,0:T(8,128)(2,1)S(1)}, bf16[2,3,48,768]{3,2,1,0:T(8,128)(2,1)S(1)}, u32[]{:S(2)}, u32[]{:S(2)}) collective-permute-start(bf16[2,3,48,768]{3,2,1,0:T(8,128)(2,1)S(1)} %pad_maximum_fusion.15), channel_id=1, source_target_pairs={{0,8},{4,12},{8,0},{12,4},{16,24},{20,28},{24,16},{28,20},{1,9},{5... | collective-permute-start | bytes 1327112 | tf_op jit(solution)/shard_map/ppermute | solution.py:335
  74.7 11.6 %collective-permute-start.18 = (bf16[3,48,768]{2,1,0:T(8,128)(2,1)S(1)}, bf16[3,48,768]{2,1,0:T(8,128)(2,1)S(1)}, u32[]{:S(2)}, u32[]{:S(2)}) collective-permute-start(bf16[3,48,768]{2,1,0:T(8,128)(2,1)S(1)} %get-tuple-element.111), channel_id=1, source_target_pairs={{0,8},{4,12},{8,0},{12,4},{16,24},{20,28},{24,16},{28,20},{1,9},{5... | collective-permute-start | bytes 663560 | tf_op jit(solution)/shard_map/ppermute | solution.py:335
  76.2 11.5 %collective-permute-start.20 = (bf16[3,48,768]{2,1,0:T(8,128)(2,1)S(1)}, bf16[3,48,768]{2,1,0:T(8,128)(2,1)S(1)}, u32[]{:S(2)}, u32[]{:S(2)}) collective-permute-start(bf16[3,48,768]{2,1,0:T(8,128)(2,1)S(1)} %get-tuple-element.112), channel_id=1, source_target_pairs={{0,16},{4,20},{8,24},{12,28},{16,0},{20,4},{24,8},{28,12},{1,17},{... | collective-permute-start | bytes 663560 | tf_op jit(solution)/shard_map/ppermute | solution.py:335
  86.2 5.9 %collective-permute-start.24 = (bf16[3,48,768]{2,1,0:T(8,128)(2,1)S(1)}, bf16[3,48,768]{2,1,0:T(8,128)(2,1)S(1)}, u32[]{:S(2)}, u32[]{:S(2)}) collective-permute-start(bf16[3,48,768]{2,1,0:T(8,128)(2,1)S(1)} %get-tuple-element.107), channel_id=1, source_target_pairs={{0,8},{4,12},{8,0},{12,4},{16,24},{20,28},{24,16},{28,20},{1,9},{5... | collective-permute-start | bytes 663560 | tf_op jit(solution)/shard_map/ppermute | solution.py:335
  87.8 6.0 %collective-permute-start.26 = (bf16[3,48,768]{2,1,0:T(8,128)(2,1)S(1)}, bf16[3,48,768]{2,1,0:T(8,128)(2,1)S(1)}, u32[]{:S(2)}, u32[]{:S(2)}) collective-permute-start(bf16[3,48,768]{2,1,0:T(8,128)(2,1)S(1)} %get-tuple-element.108), channel_id=1, source_target_pairs={{0,16},{4,20},{8,24},{12,28},{16,0},{20,4},{24,8},{28,12},{1,17},{... | collective-permute-start | bytes 663560 | tf_op jit(solution)/shard_map/ppermute | solution.py:335
  92.2 57.6 %collective-permute-start.9 = (bf16[8,48,768]{2,1,0:T(8,128)(2,1)S(1)}, bf16[8,48,768]{2,1,0:T(8,128)(2,1)S(1)}, u32[]{:S(2)}, u32[]{:S(2)}) collective-permute-start(bf16[8,48,768]{2,1,0:T(8,128)(2,1)S(1)} %constant_dynamic-update-slice_fusion.half), channel_id=1, source_target_pairs={{0,4},{4,0},{8,12},{12,8},{16,20},{20,16},{24,28},{28,24},{1,5},{5... | collective-permute-start | bytes 1769480 | tf_op jit(solution)/shard_map/ppermute | solution.py:335
  93.8 34.3 %collective-permute-start.29 = (bf16[3,2,48,768]{3,2,0,1:T(8,128)(2,1)}, bf16[3,2,48,768]{3,2,0,1:T(8,128)(2,1)S(1)}, u32[]{:S(2)}, u32[]{:S(2)}) collective-permute-start(bf16[3,2,48,768]{3,2,0,1:T(8,128)(2,1)} %collective-permute-done.17), channel_id=1, source_target_pairs={{0,2},{1,3},{2,0},{3,1},{4,6},{5,7},{6,4},{7,5},{8,10},{9,11},{10,... | collective-permute-start | bytes 1327112 | tf_op jit(solution)/shard_map/ppermute | solution.py:338
  93.8 35.2 %collective-permute-start.19 = (bf16[2,3,48,768]{3,2,1,0:T(8,128)(2,1)S(1)}, bf16[2,3,48,768]{3,2,1,0:T(8,128)(2,1)S(1)}, u32[]{:S(2)}, u32[]{:S(2)}) collective-permute-start(bf16[2,3,48,768]{3,2,1,0:T(8,128)(2,1)S(1)} %pad_maximum_fusion.16), channel_id=1, source_target_pairs={{0,16},{4,20},{8,24},{12,28},{16,0},{20,4},{24,8},{28,12},{1,17},{... | collective-permute-start | bytes 1327112 | tf_op jit(solution)/shard_map/ppermute | solution.py:335
  98.0 28.0 %collective-permute-start.2 = (bf16[512,768]{1,0:T(8,128)(2,1)S(1)}, bf16[512,768]{1,0:T(8,128)(2,1)S(1)}, u32[]{:S(2)}, u32[]{:S(2)}) collective-permute-start(bf16[512,768]{1,0:T(8,128)(2,1)S(1)} %bitcast.305), channel_id=1, source_target_pairs={{0,1},{1,0},{2,3},{3,2},{4,5},{5,4},{6,7},{7,6},{8,9},{9,8},{10,11... | collective-permute-start | bytes 2359304 | tf_op jit(solution)/shard_map/ppermute | solution.py:338
  101.6 85.7 %collective-permute-start.21 = (bf16[2,3,48,768]{3,2,1,0:T(8,128)(2,1)S(1)}, bf16[2,3,48,768]{3,2,1,0:T(8,128)(2,1)S(1)}, u32[]{:S(2)}, u32[]{:S(2)}) collective-permute-start(bf16[2,3,48,768]{3,2,1,0:T(8,128)(2,1)S(1)} %pad_maximum_fusion.17), channel_id=1, source_target_pairs={{0,8},{4,12},{8,0},{12,4},{16,24},{20,28},{24,16},{28,20},{1,9},{5... | collective-permute-start | bytes 1327112 | tf_op jit(solution)/shard_map/ppermute | solution.py:335
  125.9 10.2 %collective-permute-start.25 = (bf16[2,3,48,768]{3,2,1,0:T(8,128)(2,1)S(1)}, bf16[2,3,48,768]{3,2,1,0:T(8,128)(2,1)S(1)}, u32[]{:S(2)}, u32[]{:S(2)}) collective-permute-start(bf16[2,3,48,768]{3,2,1,0:T(8,128)(2,1)S(1)} %pad_maximum_fusion.18), channel_id=1, source_target_pairs={{0,16},{4,20},{8,24},{12,28},{16,0},{20,4},{24,8},{28,12},{1,17},{... | collective-permute-start | bytes 1327112 | tf_op jit(solution)/shard_map/ppermute | solution.py:335
  128.1 18.3 %collective-permute-start.3 = (bf16[2,512,768]{2,1,0:T(8,128)(2,1)S(1)}, bf16[2,512,768]{2,1,0:T(8,128)(2,1)S(1)}, u32[]{:S(2)}, u32[]{:S(2)}) collective-permute-start(bf16[2,512,768]{2,1,0:T(8,128)(2,1)S(1)} %pad_maximum_fusion.5), channel_id=1, source_target_pairs={{0,4},{4,0},{8,12},{12,8},{16,20},{20,16},{24,28},{28,24},{1,5},{5... | collective-permute-start | bytes 4718600 | tf_op jit(solution)/shard_map/ppermute | solution.py:335
  129.0 69.6 %collective-permute-start.27 = (bf16[2,3,48,768]{3,2,1,0:T(8,128)(2,1)S(1)}, bf16[2,3,48,768]{3,2,1,0:T(8,128)(2,1)S(1)}, u32[]{:S(2)}, u32[]{:S(2)}) collective-permute-start(bf16[2,3,48,768]{3,2,1,0:T(8,128)(2,1)S(1)} %pad_maximum_fusion.19), channel_id=1, source_target_pairs={{0,8},{4,12},{8,0},{12,4},{16,24},{20,28},{24,16},{28,20},{1,9},{5... | collective-permute-start | bytes 1327112 | tf_op jit(solution)/shard_map/ppermute | solution.py:335
  136.1 10.3 %collective-permute-start.30 = (bf16[3,48,768]{2,1,0:T(8,128)(2,1)S(1)}, bf16[3,48,768]{2,1,0:T(8,128)(2,1)S(1)}, u32[]{:S(2)}, u32[]{:S(2)}) collective-permute-start(bf16[3,48,768]{2,1,0:T(8,128)(2,1)S(1)} %get-tuple-element.103), channel_id=1, source_target_pairs={{0,8},{4,12},{8,0},{12,4},{16,24},{20,28},{24,16},{28,20},{1,9},{5... | collective-permute-start | bytes 663560 | tf_op jit(solution)/shard_map/ppermute | solution.py:335
  146.4 64.4 %collective-permute-start.16 = (bf16[8,3,48,768]{3,2,1,0:T(8,128)(2,1)S(1)}, bf16[8,3,48,768]{3,2,1,0:T(8,128)(2,1)}, u32[]{:S(2)}, u32[]{:S(2)}) collective-permute-start(bf16[8,3,48,768]{3,2,1,0:T(8,128)(2,1)S(1)} %constant_dynamic-update-slice_fusion.6.refs_0_), channel_id=1, source_target_pairs={{0,4},{4,0},{8,12},{12,8},{16,20},{20,16},{24,28},{28,24},{1,5},{5... | collective-permute-start | bytes 5308424 | tf_op jit(solution)/shard_map/ppermute | solution.py:335
  147.8 38.2 %collective-permute-start.32 = (bf16[3,48,768]{2,1,0:T(8,128)(2,1)S(1)}, bf16[3,48,768]{2,1,0:T(8,128)(2,1)S(1)}, u32[]{:S(2)}, u32[]{:S(2)}) collective-permute-start(bf16[3,48,768]{2,1,0:T(8,128)(2,1)S(1)} %get-tuple-element.104), channel_id=1, source_target_pairs={{0,16},{4,20},{8,24},{12,28},{16,0},{20,4},{24,8},{28,12},{1,17},{... | collective-permute-start | bytes 663560 | tf_op jit(solution)/shard_map/ppermute | solution.py:335
  149.8 49.6 %collective-permute-start.31 = (bf16[2,3,48,768]{3,2,1,0:T(8,128)(2,1)S(1)}, bf16[2,3,48,768]{3,2,1,0:T(8,128)(2,1)S(1)}, u32[]{:S(2)}, u32[]{:S(2)}) collective-permute-start(bf16[2,3,48,768]{3,2,1,0:T(8,128)(2,1)S(1)} %pad_maximum_fusion.20), channel_id=1, source_target_pairs={{0,16},{4,20},{8,24},{12,28},{16,0},{20,4},{24,8},{28,12},{1,17},{... | collective-permute-start | bytes 1327112 | tf_op jit(solution)/shard_map/ppermute | solution.py:335
  186.0 22.3 %collective-permute-start.10 = (bf16[2,512,768]{2,1,0:T(8,128)(2,1)}, bf16[2,512,768]{2,1,0:T(8,128)(2,1)S(1)}, u32[]{:S(2)}, u32[]{:S(2)}) collective-permute-start(bf16[2,512,768]{2,1,0:T(8,128)(2,1)} %get-tuple-element.29), channel_id=1, source_target_pairs={{0,4},{4,0},{8,12},{12,8},{16,20},{20,16},{24,28},{28,24},{1,5},{5... | collective-permute-start | bytes 4718600 | tf_op jit(solution)/shard_map/ppermute | solution.py:335
  187.4 20.7 %collective-permute-start.33 = (bf16[2,3,48,768]{3,2,1,0:T(8,128)(2,1)S(1)}, bf16[2,3,48,768]{3,2,1,0:T(8,128)(2,1)S(1)}, u32[]{:S(2)}, u32[]{:S(2)}) collective-permute-start(bf16[2,3,48,768]{3,2,1,0:T(8,128)(2,1)S(1)} %pad_maximum_fusion.21), channel_id=1, source_target_pairs={{0,8},{4,12},{8,0},{12,4},{16,24},{20,28},{24,16},{28,20},{1,9},{5... | collective-permute-start | bytes 1327112 | tf_op jit(solution)/shard_map/ppermute | solution.py:335
  198.6 12.2 %collective-permute-start.22 = (bf16[8,3,48,768]{3,2,1,0:T(8,128)(2,1)}, bf16[8,3,48,768]{3,2,1,0:T(8,128)(2,1)S(1)}, u32[]{:S(2)}, u32[]{:S(2)}) collective-permute-start(bf16[8,3,48,768]{3,2,1,0:T(8,128)(2,1)} %constant_dynamic-update-slice_fusion.12.refs_2_), channel_id=1, source_target_pairs={{0,4},{4,0},{8,12},{12,8},{16,20},{20,16},{24,28},{28,24},{1,5},{5... | collective-permute-start | bytes 5308424 | tf_op jit(solution)/shard_map/ppermute | solution.py:335
  199.4 11.4 %collective-permute-start.28 = (bf16[8,3,48,768]{3,2,1,0:T(8,128)(2,1)}, bf16[8,3,48,768]{3,2,1,0:T(8,128)(2,1)S(1)}, u32[]{:S(2)}, u32[]{:S(2)}) collective-permute-start(bf16[8,3,48,768]{3,2,1,0:T(8,128)(2,1)} %constant_dynamic-update-slice_fusion.18.refs_4_), channel_id=1, source_target_pairs={{0,4},{4,0},{8,12},{12,8},{16,20},{20,16},{24,28},{28,24},{1,5},{5... | collective-permute-start | bytes 5308424 | tf_op jit(solution)/shard_map/ppermute | solution.py:335
  209.5 19.2 %collective-permute-start.11 = (bf16[512,768]{1,0:T(8,128)(2,1)S(1)}, bf16[512,768]{1,0:T(8,128)(2,1)S(1)}, u32[]{:S(2)}, u32[]{:S(2)}) collective-permute-start(bf16[512,768]{1,0:T(8,128)(2,1)S(1)} %fusion.13), channel_id=1, source_target_pairs={{0,1},{1,0},{2,3},{3,2},{4,5},{5,4},{6,7},{7,6},{8,9},{9,8},{10,11... | collective-permute-start | bytes 2359304 | tf_op jit(solution)/shard_map/ppermute | solution.py:338
  267.5 18.5 %collective-permute-start.36 = (bf16[512,768]{1,0:T(8,128)(2,1)}, bf16[512,768]{1,0:T(8,128)(2,1)S(1)}, u32[]{:S(2)}, u32[]{:S(2)}) collective-permute-start(bf16[512,768]{1,0:T(8,128)(2,1)} %get-tuple-element.32), channel_id=1, source_target_pairs={{0,1},{1,0},{2,3},{3,2},{4,5},{5,4},{6,7},{7,6},{8,9},{9,8},{10,11... | collective-permute-start | bytes 2359304 | tf_op jit(solution)/shard_map/ppermute | solution.py:338
  287.3 98.1 %collective-permute-start.51 = (bf16[2,8,3,48,768]{4,3,2,1,0:T(8,128)(2,1)}, bf16[2,8,3,48,768]{4,3,2,1,0:T(8,128)(2,1)}, u32[]{:S(2)}, u32[]{:S(2)}) collective-permute-start(bf16[2,8,3,48,768]{4,3,2,1,0:T(8,128)(2,1)} %get-tuple-element.44), channel_id=1, source_target_pairs={{0,4},{4,0},{8,12},{12,8},{16,20},{20,16},{24,28},{28,24},{1,5},{5... | collective-permute-start | bytes 10616840 | tf_op jit(solution)/shard_map/ppermute | solution.py:335
  292.0 87.2 %collective-permute-start.56 = (bf16[2,8,3,48,768]{4,3,2,0,1:T(8,128)(2,1)}, bf16[2,8,3,48,768]{4,3,2,0,1:T(8,128)(2,1)}, u32[]{:S(2)}, u32[]{:S(2)}) collective-permute-start(bf16[2,8,3,48,768]{4,3,2,0,1:T(8,128)(2,1)} %copy.83), channel_id=1, source_target_pairs={{0,4},{4,0},{8,12},{12,8},{16,20},{20,16},{24,28},{28,24},{1,5},{5... | collective-permute-start | bytes 10616840 | tf_op jit(solution)/shard_map/ppermute | solution.py:335
  329.6 13.1 %collective-permute-start.41 = (bf16[2,96,768]{2,1,0:T(8,128)(2,1)S(1)}, bf16[2,96,768]{2,1,0:T(8,128)(2,1)S(1)}, u32[]{:S(2)}, u32[]{:S(2)}) collective-permute-start(bf16[2,96,768]{2,1,0:T(8,128)(2,1)S(1)} %get-tuple-element.93), channel_id=1, source_target_pairs={{0,16},{4,20},{8,24},{12,28},{16,0},{20,4},{24,8},{28,12},{1,17},{... | collective-permute-start | bytes 884744 | tf_op jit(solution)/shard_map/ppermute | solution.py:335
  335.6 11.9 %collective-permute-start.43 = (bf16[2,96,768]{2,1,0:T(8,128)(2,1)S(1)}, bf16[2,96,768]{2,1,0:T(8,128)(2,1)S(1)}, u32[]{:S(2)}, u32[]{:S(2)}) collective-permute-start(bf16[2,96,768]{2,1,0:T(8,128)(2,1)S(1)} %get-tuple-element.94), channel_id=1, source_target_pairs={{0,8},{4,12},{8,0},{12,4},{16,24},{20,28},{24,16},{28,20},{1,9},{5... | collective-permute-start | bytes 884744 | tf_op jit(solution)/shard_map/ppermute | solution.py:335
  347.7 5.3 collective-permute-start.42
  354.8 12.7 %collective-permute-start.45 = (bf16[2,96,768]{2,1,0:T(8,128)(2,1)S(1)}, bf16[2,96,768]{2,1,0:T(8,128)(2,1)S(1)}, u32[]{:S(2)}, u32[]{:S(2)}) collective-permute-start(bf16[2,96,768]{2,1,0:T(8,128)(2,1)S(1)} %pad_maximum_fusion.24), channel_id=1, source_target_pairs={{2,0},{3,1},{4,6},{5,7},{10,8},{11,9},{12,14},{13,15},{18,16},{19,... | collective-permute-start | bytes 884744 | tf_op jit(solution)/shard_map/ppermute | solution.py:526
  361.2 8.6 %collective-permute-start.70 = (f32[8,768]{1,0:T(8,128)S(1)}, f32[8,768]{1,0:T(8,128)S(1)}, u32[]{:S(2)}, u32[]{:S(2)}) collective-permute-start(f32[8,768]{1,0:T(8,128)S(1)} %add.122), channel_id=1, source_target_pairs={{0,16},{4,20},{8,24},{12,28},{16,0},{20,4},{24,8},{28,12},{1,17},{... | collective-permute-start | bytes 73736 | tf_op jit(solution)/shard_map/ppermute | solution.py:335
  367.6 11.5 %collective-permute-start.46 = (bf16[2,96,768]{2,1,0:T(8,128)(2,1)S(1)}, bf16[2,96,768]{2,1,0:T(8,128)(2,1)}, u32[]{:S(2)}, u32[]{:S(2)}) collective-permute-start(bf16[2,96,768]{2,1,0:T(8,128)(2,1)S(1)} %add_convert_fusion.7), channel_id=1, source_target_pairs={{0,4},{1,5},{6,2},{7,3},{8,12},{9,13},{14,10},{15,11},{16,20},{17,... | collective-permute-start | bytes 884744 | tf_op jit(solution)/shard_map/ppermute | solution.py:529
  373.8 108.8 %collective-permute-start.35 = (bf16[512,768]{1,0:T(8,128)(2,1)S(1)}, bf16[512,768]{1,0:T(8,128)(2,1)S(1)}, u32[]{:S(2)}, u32[]{:S(2)}) collective-permute-start(bf16[512,768]{1,0:T(8,128)(2,1)S(1)} %copy-done.32), channel_id=1, source_target_pairs={{2,4},{3,5},{4,2},{5,3},{10,12},{11,13},{12,10},{13,11},{18,20},{1... | collective-permute-start | bytes 2359304 | tf_op jit(solution)/shard_map/ppermute | solution.py:343
  383.4 22.4 %collective-permute-start.57 = (bf16[2,2,3,48,768]{4,3,2,0,1:T(8,128)(2,1)S(1)}, bf16[2,2,3,48,768]{4,3,2,0,1:T(8,128)(2,1)S(1)}, u32[]{:S(2)}, u32[]{:S(2)}) collective-permute-start(bf16[2,2,3,48,768]{4,3,2,0,1:T(8,128)(2,1)S(1)} %get-tuple-element.85), channel_id=1, source_target_pairs={{0,16},{4,20},{8,24},{12,28},{16,0},{20,4},{24,8},{28,12},{1,17},{... | collective-permute-start | bytes 2654216 | tf_op jit(solution)/shard_map/ppermute | solution.py:335
  385.1 22.5 %collective-permute-start.59 = (bf16[2,2,3,48,768]{4,3,2,0,1:T(8,128)(2,1)S(1)}, bf16[2,2,3,48,768]{4,3,2,0,1:T(8,128)(2,1)S(1)}, u32[]{:S(2)}, u32[]{:S(2)}) collective-permute-start(bf16[2,2,3,48,768]{4,3,2,0,1:T(8,128)(2,1)S(1)} %get-tuple-element.86), channel_id=1, source_target_pairs={{0,8},{4,12},{8,0},{12,4},{16,24},{20,28},{24,16},{28,20},{1,9},{5... | collective-permute-start | bytes 2654216 | tf_op jit(solution)/shard_map/ppermute | solution.py:335
  388.6 38.0 %collective-permute-start.54 = (bf16[2,2,3,48,768]{4,3,2,1,0:T(8,128)(2,1)S(1)}, bf16[2,2,3,48,768]{4,3,2,1,0:T(8,128)(2,1)S(1)}, u32[]{:S(2)}, u32[]{:S(2)}) collective-permute-start(bf16[2,2,3,48,768]{4,3,2,1,0:T(8,128)(2,1)S(1)} %get-tuple-element.81), channel_id=1, source_target_pairs={{0,8},{4,12},{8,0},{12,4},{16,24},{20,28},{24,16},{28,20},{1,9},{5... | collective-permute-start | bytes 2654216 | tf_op jit(solution)/shard_map/ppermute | solution.py:335
  390.5 52.3 %collective-permute-start.47 = (bf16[96,768]{1,0:T(8,128)(2,1)S(1)}, bf16[96,768]{1,0:T(8,128)(2,1)S(1)}, u32[]{:S(2)}, u32[]{:S(2)}) collective-permute-start(bf16[96,768]{1,0:T(8,128)(2,1)S(1)} %get-tuple-element.119), channel_id=1, source_target_pairs={{0,8},{4,12},{8,0},{12,4},{16,24},{20,28},{24,16},{28,20},{1,9},{5... | collective-permute-start | bytes 442376 | tf_op jit(solution)/shard_map/ppermute | solution.py:335
  405.7 38.8 %collective-permute-start.49 = (bf16[96,768]{1,0:T(8,128)(2,1)S(1)}, bf16[96,768]{1,0:T(8,128)(2,1)S(1)}, u32[]{:S(2)}, u32[]{:S(2)}) collective-permute-start(bf16[96,768]{1,0:T(8,128)(2,1)S(1)} %get-tuple-element.120), channel_id=1, source_target_pairs={{0,16},{4,20},{8,24},{12,28},{16,0},{20,4},{24,8},{28,12},{1,17},{... | collective-permute-start | bytes 442376 | tf_op jit(solution)/shard_map/ppermute | solution.py:335
  407.6 23.1 %collective-permute-start.52 = (bf16[2,2,3,48,768]{4,3,2,0,1:T(8,128)(2,1)S(1)}, bf16[2,2,3,48,768]{4,3,2,0,1:T(8,128)(2,1)S(1)}, u32[]{:S(2)}, u32[]{:S(2)}) collective-permute-start(bf16[2,2,3,48,768]{4,3,2,0,1:T(8,128)(2,1)S(1)} %copy.96), channel_id=1, source_target_pairs={{0,16},{4,20},{8,24},{12,28},{16,0},{20,4},{24,8},{28,12},{1,17},{... | collective-permute-start | bytes 2654216 | tf_op jit(solution)/shard_map/ppermute | solution.py:335
  426.6 12.6 %collective-permute-start.58 = (bf16[2,3,48,768]{3,2,1,0:T(8,128)(2,1)S(1)}, bf16[2,3,48,768]{3,2,1,0:T(8,128)(2,1)S(1)}, u32[]{:S(2)}, u32[]{:S(2)}) collective-permute-start(bf16[2,3,48,768]{3,2,1,0:T(8,128)(2,1)S(1)} %slice_bitcast_fusion.6), channel_id=1, source_target_pairs={{0,8},{4,12},{8,0},{12,4},{16,24},{20,28},{24,16},{28,20},{1,9},{5... | collective-permute-start | bytes 1327112 | tf_op jit(solution)/shard_map/ppermute | solution.py:335
  430.8 11.6 %collective-permute-start.60 = (bf16[2,3,48,768]{3,2,1,0:T(8,128)(2,1)S(1)}, bf16[2,3,48,768]{3,2,1,0:T(8,128)(2,1)S(1)}, u32[]{:S(2)}, u32[]{:S(2)}) collective-permute-start(bf16[2,3,48,768]{3,2,1,0:T(8,128)(2,1)S(1)} %slice_bitcast_fusion.4), channel_id=1, source_target_pairs={{0,16},{4,20},{8,24},{12,28},{16,0},{20,4},{24,8},{28,12},{1,17},{... | collective-permute-start | bytes 1327112 | tf_op jit(solution)/shard_map/ppermute | solution.py:335
  439.2 11.7 %collective-permute-start.53 = (bf16[2,3,48,768]{3,2,1,0:T(8,128)(2,1)S(1)}, bf16[2,3,48,768]{3,2,1,0:T(8,128)(2,1)S(1)}, u32[]{:S(2)}, u32[]{:S(2)}) collective-permute-start(bf16[2,3,48,768]{3,2,1,0:T(8,128)(2,1)S(1)} %slice_bitcast_fusion.10), channel_id=1, source_target_pairs={{0,8},{4,12},{8,0},{12,4},{16,24},{20,28},{24,16},{28,20},{1,9},{5... | collective-permute-start | bytes 1327112 | tf_op jit(solution)/shard_map/ppermute | solution.py:335
  442.6 39.6 %collective-permute-start.61 = (bf16[2,2,3,48,768]{4,3,2,0,1:T(8,128)(2,1)S(1)}, bf16[2,2,3,48,768]{4,3,2,0,1:T(8,128)(2,1)S(1)}, u32[]{:S(2)}, u32[]{:S(2)}) collective-permute-start(bf16[2,2,3,48,768]{4,3,2,0,1:T(8,128)(2,1)S(1)} %pad_maximum_fusion.10), channel_id=1, source_target_pairs={{0,2},{1,3},{2,0},{3,1},{4,6},{5,7},{6,4},{7,5},{8,10},{9,11},{10,... | collective-permute-start | bytes 2654216 | tf_op jit(solution)/shard_map/ppermute | solution.py:338
  442.7 12.4 %collective-permute-start.55 = (bf16[2,3,48,768]{3,2,1,0:T(8,128)(2,1)S(1)}, bf16[2,3,48,768]{3,2,1,0:T(8,128)(2,1)S(1)}, u32[]{:S(2)}, u32[]{:S(2)}) collective-permute-start(bf16[2,3,48,768]{3,2,1,0:T(8,128)(2,1)S(1)} %slice_bitcast_fusion.8), channel_id=1, source_target_pairs={{0,16},{4,20},{8,24},{12,28},{16,0},{20,4},{24,8},{28,12},{1,17},{... | collective-permute-start | bytes 1327112 | tf_op jit(solution)/shard_map/ppermute | solution.py:335
  444.5 51.2 %collective-permute-start.38 = (bf16[2,512,768]{2,1,0:T(8,128)(2,1)S(1)}, bf16[2,512,768]{2,1,0:T(8,128)(2,1)S(1)}, u32[]{:S(2)}, u32[]{:S(2)}) collective-permute-start(bf16[2,512,768]{2,1,0:T(8,128)(2,1)S(1)} %get-tuple-element.41), channel_id=1, source_target_pairs={{0,4},{4,0},{8,12},{12,8},{16,20},{20,16},{24,28},{28,24},{1,5},{5... | collective-permute-start | bytes 4718600 | tf_op jit(solution)/shard_map/ppermute | solution.py:335
  450.9 32.6 %collective-permute-start.48 = (bf16[2,96,768]{2,1,0:T(8,128)(2,1)S(1)}, bf16[2,96,768]{2,1,0:T(8,128)(2,1)S(1)}, u32[]{:S(2)}, u32[]{:S(2)}) collective-permute-start(bf16[2,96,768]{2,1,0:T(8,128)(2,1)S(1)} %pad_maximum_fusion.25), channel_id=1, source_target_pairs={{0,16},{4,20},{8,24},{12,28},{16,0},{20,4},{24,8},{28,12},{1,17},{... | collective-permute-start | bytes 884744 | tf_op jit(solution)/shard_map/ppermute | solution.py:335
  455.1 29.3 %collective-permute-start.50 = (bf16[2,96,768]{2,1,0:T(8,128)(2,1)S(1)}, bf16[2,96,768]{2,1,0:T(8,128)(2,1)S(1)}, u32[]{:S(2)}, u32[]{:S(2)}) collective-permute-start(bf16[2,96,768]{2,1,0:T(8,128)(2,1)S(1)} %pad_maximum_fusion.26), channel_id=1, source_target_pairs={{0,8},{4,12},{8,0},{12,4},{16,24},{20,28},{24,16},{28,20},{1,9},{5... | collective-permute-start | bytes 884744 | tf_op jit(solution)/shard_map/ppermute | solution.py:335
  482.4 12.2 %collective-permute-start.62 = (bf16[2,3,48,768]{3,2,1,0:T(8,128)(2,1)S(1)}, bf16[2,3,48,768]{3,2,1,0:T(8,128)(2,1)S(1)}, u32[]{:S(2)}, u32[]{:S(2)}) collective-permute-start(bf16[2,3,48,768]{3,2,1,0:T(8,128)(2,1)S(1)} %slice_bitcast_fusion.2), channel_id=1, source_target_pairs={{0,1},{1,0},{2,3},{3,2},{4,5},{5,4},{6,7},{7,6},{8,9},{9,8},{10,11... | collective-permute-start | bytes 1327112 | tf_op jit(solution)/shard_map/ppermute | solution.py:338
  495.5 6.5 %collective-permute-start.63 = (bf16[3,48,768]{2,1,0:T(8,128)(2,1)S(1)}, bf16[3,48,768]{2,1,0:T(8,128)(2,1)S(1)}, u32[]{:S(2)}, u32[]{:S(2)}) collective-permute-start(bf16[3,48,768]{2,1,0:T(8,128)(2,1)S(1)} %get-tuple-element.98), channel_id=1, source_target_pairs={{0,8},{4,12},{8,0},{12,4},{16,24},{20,28},{24,16},{28,20},{1,9},{5... | collective-permute-start | bytes 663560 | tf_op jit(solution)/shard_map/ppermute | solution.py:335
  496.0 8.5 %collective-permute-start.65 = (bf16[3,48,768]{2,1,0:T(8,128)(2,1)S(1)}, bf16[3,48,768]{2,1,0:T(8,128)(2,1)S(1)}, u32[]{:S(2)}, u32[]{:S(2)}) collective-permute-start(bf16[3,48,768]{2,1,0:T(8,128)(2,1)S(1)} %get-tuple-element.100), channel_id=1, source_target_pairs={{0,16},{4,20},{8,24},{12,28},{16,0},{20,4},{24,8},{28,12},{1,17},{... | collective-permute-start | bytes 663560 | tf_op jit(solution)/shard_map/ppermute | solution.py:335
  502.0 10.4 %collective-permute-start.64 = (bf16[2,3,48,768]{3,2,1,0:T(8,128)(2,1)S(1)}, bf16[2,3,48,768]{3,2,1,0:T(8,128)(2,1)S(1)}, u32[]{:S(2)}, u32[]{:S(2)}) collective-permute-start(bf16[2,3,48,768]{3,2,1,0:T(8,128)(2,1)S(1)} %pad_maximum_fusion.22), channel_id=1, source_target_pairs={{0,16},{4,20},{8,24},{12,28},{16,0},{20,4},{24,8},{28,12},{1,17},{... | collective-permute-start | bytes 1327112 | tf_op jit(solution)/shard_map/ppermute | solution.py:335
  503.9 17.5 %collective-permute-start.39 = (bf16[512,768]{1,0:T(8,128)(2,1)S(1)}, bf16[512,768]{1,0:T(8,128)(2,1)S(1)}, u32[]{:S(2)}, u32[]{:S(2)}) collective-permute-start(bf16[512,768]{1,0:T(8,128)(2,1)S(1)} %fusion.14), channel_id=1, source_target_pairs={{0,1},{1,0},{2,3},{3,2},{4,5},{5,4},{6,7},{7,6},{8,9},{9,8},{10,11... | collective-permute-start | bytes 2359304 | tf_op jit(solution)/shard_map/ppermute | solution.py:338
  504.6 10.1 %collective-permute-start.66 = (bf16[2,3,48,768]{3,2,1,0:T(8,128)(2,1)S(1)}, bf16[2,3,48,768]{3,2,1,0:T(8,128)(2,1)S(1)}, u32[]{:S(2)}, u32[]{:S(2)}) collective-permute-start(bf16[2,3,48,768]{3,2,1,0:T(8,128)(2,1)S(1)} %pad_maximum_fusion.23), channel_id=1, source_target_pairs={{0,8},{4,12},{8,0},{12,4},{16,24},{20,28},{24,16},{28,20},{1,9},{5... | collective-permute-start | bytes 1327112 | tf_op jit(solution)/shard_map/ppermute | solution.py:335
  515.5 26.1 %collective-permute-start.67 = (bf16[8,3,48,768]{3,2,1,0:T(8,128)(2,1)}, bf16[8,3,48,768]{3,2,1,0:T(8,128)(2,1)}, u32[]{:S(2)}, u32[]{:S(2)}) collective-permute-start(bf16[8,3,48,768]{3,2,1,0:T(8,128)(2,1)} %constant_dynamic-update-slice_fusion.30), channel_id=1, source_target_pairs={{0,4},{4,0},{8,12},{12,8},{16,20},{20,16},{24,28},{28,24},{1,5},{5... | collective-permute-start | bytes 5308424 | tf_op jit(solution)/shard_map/ppermute | solution.py:335
  522.6 16.2 %collective-permute-start.40 = (bf16[512,768]{1,0:T(8,128)(2,1)}, bf16[512,768]{1,0:T(8,128)(2,1)}, u32[]{:S(2)}, u32[]{:S(2)}) collective-permute-start(bf16[512,768]{1,0:T(8,128)(2,1)} %fusion.27), channel_id=1, source_target_pairs={{2,4},{3,5},{4,2},{5,3},{10,12},{11,13},{12,10},{13,11},{18,20},{1... | collective-permute-start | bytes 2359304 | tf_op jit(solution)/shard_map/ppermute | solution.py:343
  (54 other events, 637.0 us)

commit v3 on v2

v3 whole, which is shorter than its diff:
```python
import functools
import math

import jax
import jax.numpy as jnp
from jax import lax
from jax.experimental import pallas as pl
from jax.experimental.pallas import tpu as pltpu
from jax.sharding import PartitionSpec as P

HEAD_DIM = 64
SEGS = 8
BLK = 256
F32 = jnp.float32
BF16 = jnp.bfloat16
MESH = pl.DeviceIdType.MESH
CHUNKS = 4
CHUNK = 128

epsilon = 1e-05
far_below = -1e30
log_base = math.log(1000.0)


def nn(a, b):
    return lax.dot_general(a, b, (((1,), (0,)), ((), ())), preferred_element_type=F32)


def nt(a, b):
    return lax.dot_general(a, b, (((1,), (1,)), ((), ())), preferred_element_type=F32)


def tn(a, b):
    return lax.dot_general(a, b, (((0,), (0,)), ((), ())), preferred_element_type=F32)


class Place:
    def __init__(self):
        p, z = lax.axis_index("dp"), lax.axis_index("tensor")
        self.p, self.z = p, z
        c, x, y = p % 2, (p // 2) % 2, (p // 4) % 2
        self.c, self.x, self.y = c, x, y
        self.place = p % 8
        self.x_place = self.place + 2 - 4 * x
        self.y_place = self.place + 4 - 8 * y
        self.d_place = self.x_place + 4 - 8 * y
        self.z1_at, self.z2_at = z + 1 - 2 * (z % 2), (z + 2) % 4
        self.sib = {"dp": p + 1 - 2 * c}
        self.xn = {"dp": p + 2 - 4 * x}
        self.yn = {"dp": p + 4 - 8 * y}
        self.z1 = {"tensor": self.z1_at}
        self.z2 = {"tensor": self.z2_at}
        self.pair = {"dp": p + 1 - 2 * c, "tensor": self.z2_at}
        self.cross = c + z // 2 - 2 * c * (z // 2)
        self.slot = (z + 2 * self.cross) % 4
        self.slot1 = self.slot + 1 - 2 * (self.slot % 2)
        self.slot2 = (self.slot + 2) % 4
        self.slot3 = (self.slot1 + 2) % 4


def greet(partners):
    barrier = pltpu.get_barrier_semaphore()
    for partner in partners:
        pl.semaphore_signal(barrier, inc=1, device_id=partner, device_id_type=MESH)
    pl.semaphore_wait(barrier, len(partners))


class Links:
    def __init__(self, send, recv):
        self.send, self.recv, self.count, self.started = send, recv, 0, []

    def make(self, src, dst, to):
        i = self.count
        self.count += 1
        return pltpu.make_async_remote_copy(
            src_ref=src, dst_ref=dst, send_sem=self.send.at[i], recv_sem=self.recv.at[i], device_id=to, device_id_type=MESH
        )

    def start(self, src, dst, to):
        copy = self.make(src, dst, to)
        copy.start()
        self.started.append(copy)
        return copy

    def wait_sends(self):
        for copy in self.started:
            copy.wait_send()


def rows_of(place, size=96, first=0):
    return pl.ds(pl.multiple_of(place * size + first, 16), size - first if first == 0 else size // 2)


class Spread:
    def __init__(self, me, links, view, src=None):
        self.me, self.links, self.view = me, links, view
        own = view(me.place, 0, 96)
        src = own if src is None else src
        self.from_x = links.start(src, own, me.xn)
        self.from_y = links.start(src, own, me.yn)
        self.from_sib = [links.start(src, own, me.sib)]

    def second(self):
        me, links, view = self.me, self.links, self.view
        self.from_x.wait_recv()
        part = view(me.x_place, 0, 48)
        self.low = links.start(part, part, me.yn)
        block = view(me.x_place, 0, 96)
        self.from_sib.append(links.start(block, block, me.sib))
        self.from_y.wait_recv()
        part = view(me.y_place, 48, 48)
        self.high = links.start(part, part, me.xn)
        block = view(me.y_place, 0, 96)
        self.from_sib.append(links.start(block, block, me.sib))

    def third(self):
        me, links, view = self.me, self.links, self.view
        self.low.wait_recv()
        self.high.wait_recv()
        block = view(me.d_place, 0, 96)
        self.from_sib.append(links.start(block, block, me.sib))

    def last(self):
        for copy in self.from_sib:
            copy.wait_recv()


def view_2d(ref):
    return lambda place, first, size: ref.at[pl.ds(pl.multiple_of(place * 96 + first, 16), size)]


def view_3d(ref):
    return lambda place, first, size: ref.at[:, pl.ds(pl.multiple_of(place * 96 + first, 16), size)]


def start_kernel(x, wo, fb, tok, wx, wf0, wf2, zb, token_send, token_recv, send, recv, local):
    me = Place()
    c, z = me.c, me.z
    away = z + c * (3 - 2 * z)

    barrier = pltpu.get_barrier_semaphore()
    partners = (me.sib, me.xn, me.yn, me.z1, me.z2)
    for partner in partners:
        pl.semaphore_signal(barrier, inc=1, device_id=partner, device_id_type=MESH)
    @pl.when(z % 3 != 0)
    def _():
        pl.semaphore_signal(barrier, inc=1, device_id={"tensor": 3 - z}, device_id_type=MESH)

    pl.semaphore_wait(barrier, len(partners) + z * (3 - z) // 2)

    def line(k):
        return k + c * (3 - 2 * k)

    def line_sib(k):
        return k + (1 - c) * (3 - 2 * k)

    far, near = {"tensor": line(0)}, {"tensor": line(1)}

    def part(ch):
        return pl.ds(ch * CHUNK, CHUNK)

    def copy(kind, k, ch, src, to):
        return pltpu.make_async_remote_copy(
            src_ref=src, dst_ref=tok.at[line(k), part(ch)], send_sem=token_send.at[kind, k, ch],
            recv_sem=token_recv.at[k, ch], device_id=to, device_id_type=MESH,
        )

    def own(ch):
        return x.at[part(ch)]

    def held(k, ch):
        return tok.at[line(k), part(ch)]

    for k, to in ((0, near), (1, far), (2, near), (3, near)):

        @pl.when(away == k)
        def _(k=k, to=to):
            for ch in range(CHUNKS):
                copy(0, k, ch, own(ch), to).start()
                if k < 2:
                    copy(1, k, ch, own(ch), me.sib).start()

    links = Links(send, recv)
    attn_z = links.start(view_2d(wo)(me.place, 0, 96), view_2d(wx)(me.place, 0, 96), me.z2)
    ff_z = links.start(fb, view_3d(wf2)(me.place, 0, 96), me.z2)
    ff0 = Spread(me, links, view_3d(wf0), fb)
    here = [
        pltpu.make_async_copy(fb, view_3d(wf0)(me.place, 0, 96), local.at[0]),
        pltpu.make_async_copy(fb, zb.at[0], local.at[1]),
    ]
    for h in here:
        h.start()

    @pl.when(away < 2)
    def _():
        mine = pltpu.make_async_copy(x, tok.at[z], local.at[2])
        mine.start()
        mine.wait()

    def forward(ch):
        @pl.when(away == 0)
        def _():
            for k in (1, 2, 3):
                copy(1, k, ch, held(k, ch), me.sib).wait_recv()
                copy(1, k, ch, held(k, ch), me.sib).start()

        @pl.when(away == 1)
        def _():
            for k in (2, 3, 0):
                copy(1, k, ch, held(k, ch), me.sib).wait_recv()
                if k:
                    copy(0, k, ch, held(k, ch), far).start()
                copy(1, k, ch, held(k, ch), me.sib).start()

    attn_z.wait_recv()
    attn = Spread(me, links, view_2d(wx))
    forward(0)
    attn.second()
    ff0.second()
    attn.third()
    forward(1)
    ff_z.wait_recv()
    ff2 = Spread(me, links, view_3d(wf2))
    keep = pltpu.make_async_copy(view_3d(wf2)(me.place, 0, 96), zb.at[1], local.at[3])
    keep.start()
    ff0.third()
    forward(2)
    ff2.second()
    forward(3)
    ff2.third()

    @pl.when(away >= 2)
    def _():
        for ch in range(CHUNKS):
            for k in range(4):
                pltpu.make_async_remote_copy(
                    src_ref=own(ch), dst_ref=tok.at[line_sib(k), part(ch)], send_sem=token_send.at[0, k, ch],
                    recv_sem=token_recv.at[k, ch], device_id=me.sib, device_id_type=MESH,
                ).wait_recv()

    for spread in (attn, ff0, ff2):
        spread.last()
    for h in here:
        h.wait()
    keep.wait()
    links.wait_sends()
    for k, to in ((0, near), (1, far), (2, near), (3, near)):

        @pl.when(away == k)
        def _(k=k, to=to):
            for ch in range(CHUNKS):
                copy(0, k, ch, own(ch), to).wait_send()
                if k == 1:
                    for j in (2, 3):
                        copy(0, j, ch, held(j, ch), to).wait_send()
                if k < 2:
                    for j in range(4):
                        copy(1, j, ch, own(ch) if j == k else held(j, ch), me.sib).wait_send()


def attend_forward_kernel(
    sc, tok, cos, sin, seg, own, other, w, qa, ka, kt, vn, ot, logsum, part, va, mx, acc, sem
):
    heads = 3
    width = heads * HEAD_DIM

    @pl.when(sc[0] == 0)
    def _():
        copy = pltpu.make_async_copy(own, w, sem.at[0])
        copy.start()
        copy.wait()

    @pl.when(sc[0] == 1)
    def _():
        copy = pltpu.make_async_copy(other, w, sem.at[0])
        copy.start()
        copy.wait()

    def project(e, _):
        at = pl.ds(pl.multiple_of(e * 512, 512), 512)
        made = nt(w[: 3 * width], tok[e])
        c, s = cos[:, at], sin[:, at]
        hot = (seg[:, at] == lax.broadcasted_iota(jnp.int32, (SEGS, 512), 0)).astype(F32)
        rest = jnp.zeros((64 - SEGS, 512), F32)
        one_row = (lax.broadcasted_iota(jnp.int32, (16, 512), 0) == 0).astype(F32)
        for h in range(heads):
            r = h * HEAD_DIM
            a1, a2 = made[r : r + 32], made[r + 32 : r + 64]
            q = jnp.concatenate([a1 * c - a2 * s, a2 * c + a1 * s], axis=0).astype(BF16).astype(F32)
            qa[h, :, at] = jnp.concatenate([q * 0.125, hot, rest], axis=0).astype(BF16)
            r += width
            a1, a2 = made[r : r + 32], made[r + 32 : r + 64]
            k = jnp.concatenate([a1 * c - a2 * s, a2 * c + a1 * s], axis=0)
            kt[h * HEAD_DIM : (h + 1) * HEAD_DIM, at] = k.astype(BF16)
            ka[h, at, :] = jnp.concatenate([k, (1.0 - hot) * far_below, rest], axis=0).T.astype(BF16)
            r += width
            v = made[r : r + 64]
            va[h, :, at] = jnp.concatenate([v, one_row], axis=0).astype(BF16)
            vn[h, at, :] = jnp.concatenate([v, jnp.zeros_like(v)], axis=0).T[:, :HEAD_DIM].astype(BF16)
        return 0

    lax.fori_loop(0, 4, project, 0)

    def query_block(i, _):
        at = pl.ds(pl.multiple_of(i * BLK, BLK), BLK)
        for h in range(heads):
            mx[h] = jnp.full((1, BLK), -3e38, F32)
            acc[h] = jnp.zeros((80, BLK), F32)

        def key_block(j, _):
            here = pl.ds(pl.multiple_of(j * BLK, BLK), BLK)
            for h in range(heads):
                scores = nn(ka[h, here, :], qa[h, :, at])
                before = mx[h]
                largest = jnp.maximum(before, jnp.max(scores, axis=0, keepdims=True))
                weights = jnp.exp(scores - largest).astype(BF16)
                acc[h] = acc[h] * jnp.exp(before - largest) + nn(va[h, :, here], weights)
                mx[h] = largest
            return 0

        lax.fori_loop(sc[8 + i], sc[16 + i], key_block, 0)
        for h in range(heads):
            total = acc[h, 64:65, :]
            ot[h * HEAD_DIM : (h + 1) * HEAD_DIM, at] = (acc[h, :64, :] / total).astype(BF16)
            logsum[pl.ds(h, 1), at] = mx[h] + jnp.log(total)
        return 0

    lax.fori_loop(0, 2048 // BLK, query_block, 0)
    for e in range(4):
        part[e] = tn(ot[:, e * 512 : (e + 1) * 512], w[3 * width :]).astype(BF16)


def attend_backward_kernel(
    sc, gb, tok, w, qa, ka, kt, vn, ot, logsum, cos, sin, grads, part, dot_, inner, dq, dk, dv, gp
):
    heads = 3
    width = heads * HEAD_DIM

    def begin(e, _):
        at = pl.ds(pl.multiple_of(e * 512, 512), 512)
        made = nt(w[3 * width :], gb[e]).astype(BF16)
        dot_[:, at] = made
        product = made.astype(F32) * ot[:, at].astype(F32)
        for h in range(heads):
            inner[pl.ds(h, 1), at] = jnp.sum(product[h * HEAD_DIM : (h + 1) * HEAD_DIM], axis=0, keepdims=True)
        return 0

    lax.fori_loop(0, 4, begin, 0)
    dq[...] = jnp.zeros_like(dq)

    def key_block(j, _):
        here = pl.ds(pl.multiple_of(j * BLK, BLK), BLK)
        for h in range(heads):
            dk[h] = jnp.zeros((HEAD_DIM, BLK), F32)
            dv[h] = jnp.zeros((HEAD_DIM, BLK), F32)

        def query_block(i, _):
            at = pl.ds(pl.multiple_of(i * BLK, BLK), BLK)
            for h in range(heads):
                rows = slice(h * HEAD_DIM, (h + 1) * HEAD_DIM)
                scores = nn(ka[h, here, :], qa[h, :, at])
                probability = jnp.exp(scores - logsum[pl.ds(h, 1), at])
                rise = nn(vn[h, here, :], dot_[rows, at])
                slope = (probability * (rise - inner[pl.ds(h, 1), at])).astype(BF16)
                dv[h] += nt(dot_[rows, at], probability.astype(BF16))
                dk[h] += nt(qa[h, :HEAD_DIM, at], slope)
                dq[rows, at] += nn(kt[rows, here], slope)
            return 0

        lax.fori_loop(sc[8 + j], sc[16 + j], query_block, 0)
        c, s = cos[:, here], sin[:, here]
        for h in range(heads):
            d1, d2 = dk[h, :32, :], dk[h, 32:, :]
            r = width + h * HEAD_DIM
            gp[r : r + 64, here] = jnp.concatenate([d1 * c + d2 * s, d2 * c - d1 * s], axis=0).astype(BF16)
            r += width
            gp[r : r + 64, here] = dv[h].astype(BF16)
        return 0

    lax.fori_loop(0, 2048 // BLK, key_block, 0)

    def turn(e, _):
        at = pl.ds(pl.multiple_of(e * 512, 512), 512)
        c, s = cos[:, at] * 0.125, sin[:, at] * 0.125
        for h in range(heads):
            r = h * HEAD_DIM
            d1, d2 = dq[r : r + 32, at], dq[r + 32 : r + 64, at]
            gp[r : r + 64, at] = jnp.concatenate([d1 * c + d2 * s, d2 * c - d1 * s], axis=0).astype(BF16)
        return 0

    lax.fori_loop(0, 4, turn, 0)
    for e in range(4):
        part[e] = tn(gp[:, e * 512 : (e + 1) * 512], w[: 3 * width]).astype(BF16)
    for block in range(4):
        if block < 3:
            rows = slice(block * width, (block + 1) * width)
            made = sum(nn(gp[rows, e * 512 : (e + 1) * 512], tok[e]) for e in range(4))
        else:
            made = sum(nn(ot[:, e * 512 : (e + 1) * 512], gb[e]) for e in range(4))
        grads[block * width : (block + 1) * width] = made.astype(BF16)


def row_mean(v):
    return jnp.mean(v, axis=-1, keepdims=True)


def norm_forward(summed):
    centred = summed - row_mean(summed)
    inverse = lax.rsqrt(row_mean(centred * centred) + epsilon)
    return centred * inverse, inverse


def norm_backward(scaled, normalized, inverse):
    return inverse * (scaled - row_mean(scaled) - normalized * row_mean(scaled * normalized))


def feed_forward_kernel(
    tok, part, cot, gain, bias, wf0, wf2, zc,
    out, gz1, gb, sums, keep_a, keep_b, send_a, send_b,
    w, slope_g, slope_u, hid, nb, nbt, gm, gmt, total, norm1, inv1, dw, lw, xs, from_core, from_z, to_z,
    send, recv, local, out_sem,
):
    me = Place()
    greet((me.sib, me.xn, me.yn, me.z1))
    links = Links(send, recv)
    loads = [
        pltpu.make_async_copy(tok.at[me.slot], xs, local.at[0]),
        pltpu.make_async_copy(wf0, w.at[0], local.at[1]),
        pltpu.make_async_copy(wf2, w.at[2], local.at[2]),
        pltpu.make_async_copy(zc.at[0], view_3d(w.at[1])(me.place, 0, 96), local.at[3]),
        pltpu.make_async_copy(zc.at[1], view_3d(w.at[3])(me.place, 0, 96), local.at[4]),
    ]

    def rows(ch):
        return pl.ds(ch * CHUNK, CHUNK)

    cores = [
        [links.start(part.at[shard, rows(ch)], from_core.at[i, rows(ch)], me.sib) for ch in range(CHUNKS)]
        for i, shard in ((1, me.slot3), (0, me.slot2))
    ]
    ff1 = Spread(me, links, view_3d(w.at[1]), zc.at[0])
    ff3 = Spread(me, links, view_3d(w.at[3]), zc.at[1])
    for load in loads:
        load.start()
    zs = []
    for ch in range(CHUNKS):
        cores[0][ch].wait_recv()
        at = rows(ch)
        to_z[at] = (part[me.slot1, at].astype(F32) + from_core[1, at].astype(F32)).astype(BF16)
        zs.append(links.start(to_z.at[at], from_z.at[at], me.z1))
    ff1.second()
    loads[0].wait()
    for ch in range(CHUNKS):
        if ch == CHUNKS - 1:
            ff3.second()
        cores[1][ch].wait_recv()
        zs[ch].wait_recv()
        at = rows(ch)
        branch = part[me.slot, at].astype(F32) + from_core[0, at].astype(F32) + from_z[at].astype(F32)
        n1, i1 = norm_forward(xs[at].astype(F32) + branch)
        norm1[at] = n1
        inv1[at] = jnp.broadcast_to(i1, (CHUNK, 128))
        normed = n1 * gain[0:1, :] + bias[0:1, :]
        total[at] = normed
        nb[at] = normed.astype(BF16)
        nbt[:, ch * CHUNK : (ch + 1) * CHUNK] = normed.T.astype(BF16)
    ff1.third()

    def forward(ez):
        gate = nn(nb[...], w[ez, 0])
        up = nn(nb[...], w[ez, 1])
        sig = 1.0 / (1.0 + jnp.exp(-gate))
        active = gate * sig
        low = (active * up).astype(BF16)
        hid[ez] = low
        slope_u[ez] = active.astype(BF16)
        slope_g[ez] = (up * sig * (1.0 + gate * (1.0 - sig))).astype(BF16)
        total[...] += nn(low, w[ez, 2])

    loads[1].wait()
    forward(0)
    ff3.third()
    loads[2].wait()
    forward(2)
    loads[3].wait()
    ff1.last()
    forward(1)
    loads[4].wait()
    ff3.last()
    forward(3)
    n2, i2 = norm_forward(total[...])
    out[...] = (n2 * gain[1:2, :] + bias[1:2, :]).astype(BF16)
    g = cot[...].astype(F32)
    sums[1:2, :] = jnp.sum(g * n2, axis=0, keepdims=True)
    sums[3:4, :] = jnp.sum(g, axis=0, keepdims=True)
    gz2 = norm_backward(g * gain[1:2, :], n2, i2)
    total[...] = gz2
    gm[...] = gz2.astype(BF16)
    gmt[...] = gz2.T.astype(BF16)

    def block(quad, core):
        return pl.ds(pl.multiple_of((quad * 2 + core) * 96, 32), 96)

    def stores(ez, i):
        made = []
        for oy in range(2):
            for ox in range(2):
                row = pl.multiple_of(((oy * 2 + ox) * 2 + me.c) * 96, 32)
                made.append((me.y == oy, dw.at[i, :, pl.ds(row, 48)], keep_a.at[ez, ox], send_a.at[ez, ox]))
                row = pl.multiple_of(row + 48, 16)
                made.append((me.x == ox, dw.at[i, :, pl.ds(row, 48)], keep_b.at[ez, oy], send_b.at[ez, oy]))
        return made

    def store(ez, i):
        for n, (here, src, kept, sent) in enumerate(stores(ez, i)):

            @pl.when(here)
            def _(n=n, src=src, kept=kept):
                pltpu.make_async_copy(src, kept, out_sem.at[i, n]).start()

            @pl.when(jnp.logical_not(here))
            def _(n=n, src=src, sent=sent):
                pltpu.make_async_copy(src, sent, out_sem.at[i, n]).start()

    def stored(ez, i):
        for n, (_, src, kept, _) in enumerate(stores(ez, i)):
            pltpu.make_async_copy(src, kept, out_sem.at[i, n]).wait()

    order = (1, 3, 0, 2)
    halves = []

    def settle(n):
        i = n % 2
        for quad in range(4):
            halves[n][quad].wait_recv()
            at = block(quad, me.c)
            for m in range(3):
                dw[i, m, at] = (dw[i, m, at].astype(F32) + lw[n, quad, m].astype(F32)).astype(BF16)
        store(order[n], i)

    for n, ez in enumerate(order):
        i = n % 2
        if n >= 2:
            stored(order[n - 2], i)
            for copy in halves[n - 2]:
                copy.wait_send()
        grad_hidden = nt(gm[...], w[ez, 2])
        dw[i, 2] = nn(gmt[...], hid[ez]).astype(BF16)
        gate = (grad_hidden * slope_g[ez].astype(F32)).astype(BF16)
        dw[i, 0] = nn(nbt[...], gate).astype(BF16)
        up = (grad_hidden * slope_u[ez].astype(F32)).astype(BF16)
        dw[i, 1] = nn(nbt[...], up).astype(BF16)
        halves.append(
            [links.make(dw.at[i, :, block(quad, 1 - me.c)], lw.at[n, quad], me.sib) for quad in range(4)]
        )
        for copy in halves[n]:
            copy.start()
        total[...] += nt(gate, w[ez, 0]) + nt(up, w[ez, 1])
        if n:
            settle(n - 1)

    g = total[...]
    sums[0:1, :] = jnp.sum(g * norm1[...], axis=0, keepdims=True)
    sums[2:3, :] = jnp.sum(g, axis=0, keepdims=True)
    sums[4:8, :] = jnp.zeros((4, 768), F32)
    first, second, third = [], [], []
    for ch in range(CHUNKS):
        at = rows(ch)
        made = norm_backward(total[at] * gain[0:1, :], norm1[at], inv1[at, 0:1])
        gz1[at] = made
        gb[me.slot, at] = made.astype(BF16)
        mine = gb.at[me.slot, at]
        first.append(links.start(mine, mine, me.z1))
        second.append(links.start(mine, mine, me.sib))
    settle(len(order) - 1)
    for ch in range(CHUNKS):
        at = rows(ch)
        first[ch].wait_recv()
        other = gb.at[me.slot1, at]
        third.append(links.start(other, other, me.sib))
    for copy in second + third:
        copy.wait_recv()
    for n in (2, 3):
        stored(order[n], n % 2)
        for copy in halves[n]:
            copy.wait_send()
    links.wait_sends()


def finish_kernel(
    extra, keep_a, keep_b, recv_a, recv_b, ga, part, gz1, sums_in,
    g_ff, g_attn, g_tok, sums,
    sa, sb, f2a, f2b, va, f3, f4, fe, a_in, a_mid, a_out, a_fin, a_two, ae, from_core, from_z, to_z, trade_out, trade_in, sum_in,
    send, recv, a_send, a_recv,
):
    me = Place()
    bits = [{"dp": me.p + bit - 2 * bit * ((me.p // bit) % 2)} for bit in extra]
    greet([me.sib, me.xn, me.yn, me.z1, me.z2, me.pair] + bits)
    links = Links(send, recv)

    def rows(ch):
        return pl.ds(ch * CHUNK, CHUNK)

    def add(*terms):
        return sum(t.astype(F32) for t in terms).astype(BF16)

    cores = [
        [links.start(part.at[shard, rows(ch)], from_core.at[i, rows(ch)], me.sib) for ch in range(CHUNKS)]
        for i, shard in ((1, me.slot3), (0, me.slot2))
    ]

    def half(oy, ox, h):
        return pl.ds(pl.multiple_of((oy * 2 + ox) * 192 + h * 96, 32), 96)

    attn_1 = []
    for o in range(2):
        attn_1.append(links.start(ga.at[half(1 - me.y, o, 0)], a_in.at[0, o], me.yn))
        attn_1.append(links.start(ga.at[half(o, 1 - me.x, 1)], a_in.at[1, o], me.xn))

    sums[...] = sums_in[...]
    around = [me.sib, me.xn, me.yn, me.z1, me.z2] + bits
    small = [links.start(sums, sum_in.at[0], around[0])]

    def small_step():
        n = len(small)
        small[-1].wait_recv()
        small[-1].wait_send()
        links.started = [copy for copy in links.started if copy is not small[n - 1]]
        sums[...] += sum_in[n - 1]
        if n < len(around):
            small.append(links.start(sums, sum_in.at[n], around[n]))

    order = (1, 3, 0, 2)
    ff_2 = {}

    def plane(ez):
        sa[ez] = add(keep_a[ez, 1 - me.x], recv_a[ez, 1 - me.x])
        sb[ez] = add(keep_b[ez, 1 - me.y], recv_b[ez, 1 - me.y])
        ff_2[ez] = (links.start(sa.at[ez], f2a.at[ez], me.xn), links.start(sb.at[ez], f2b.at[ez], me.yn))

    def planed(ez):
        ff_2[ez][0].wait_recv()
        va[ez, 0] = add(keep_a[ez, me.x], recv_a[ez, me.x], f2a[ez])
        ff_2[ez][1].wait_recv()
        va[ez, 1] = add(keep_b[ez, me.y], recv_b[ez, me.y], f2b[ez])

    plane(1)
    plane(3)
    zs = []
    for ch in range(CHUNKS):
        cores[0][ch].wait_recv()
        at = rows(ch)
        to_z[at] = add(part[me.slot1, at], from_core[1, at])
        zs.append(links.start(to_z.at[at], from_z.at[at], me.z1))
    plane(0)
    plane(2)
    small_step()
    for copy in attn_1:
        copy.wait_recv()
    a_mid[0] = add(ga[half(me.y, 1 - me.x, 0)], a_in[0, 1 - me.x])
    a_mid[1] = add(ga[half(1 - me.y, me.x, 1)], a_in[1, 1 - me.y])
    attn_2 = [links.start(a_mid.at[0], a_out.at[0], me.xn), links.start(a_mid.at[1], a_out.at[1], me.yn)]
    small_step()
    ff_3 = []
    for ez in (1, 3):
        planed(ez)
        ff_3.append(links.start(va.at[ez], f3.at[(ez - 1) // 2], me.z1))
    small_step()
    for copy in attn_2:
        copy.wait_recv()
    a_fin[:96] = add(ga[half(me.y, me.x, 0)], a_in[0, me.x], a_out[0])
    a_fin[96:] = add(ga[half(me.y, me.x, 1)], a_in[1, me.y], a_out[1])

    def attn_copy(n, src, dst, to):
        return pltpu.make_async_remote_copy(
            src_ref=src, dst_ref=dst, send_sem=a_send.at[n], recv_sem=a_recv.at[n], device_id=to, device_id_type=MESH
        )

    def quarter(oy, ox, first=0, size=192):
        return g_attn.at[pl.ds(pl.multiple_of((oy * 2 + ox) * 192 + first, 32), size)]

    def attn_over():
        return attn_copy(0, a_fin, a_two, me.z2)

    @pl.when(me.cross == 1)
    def _():
        attn_over().start()

    small_step()

    trades = [
        pltpu.make_async_remote_copy(
            src_ref=trade_out.at[rows(ch)], dst_ref=trade_in.at[rows(ch)], send_sem=a_send.at[8 + ch],
            recv_sem=a_recv.at[8 + ch], device_id=me.pair, device_id_type=MESH,
        )
        for ch in range(CHUNKS)
    ]
    for ch in range(CHUNKS):
        cores[1][ch].wait_recv()
        zs[ch].wait_recv()
        at = rows(ch)
        got = gz1[at] + (part[me.slot, at].astype(F32) + from_core[0, at].astype(F32) + from_z[at].astype(F32))

        @pl.when(me.cross == 0)
        def _(at=at, got=got):
            g_tok[at] = got

        @pl.when(me.cross == 1)
        def _(at=at, got=got, ch=ch):
            trade_out[at] = got.astype(BF16)
            trades[ch].start()

    planed(0)
    planed(2)
    ff_3[1].wait_recv()
    va[2] = add(va[2], f3[1])
    ff_4 = links.start(va.at[2], f4, me.z2)
    while len(small) < len(around):
        small_step()
    small_step()

    mine = quarter(me.y, me.x)

    def attn_send(n, src, to):
        return attn_copy(n, src, src, to)

    block_x, block_y = quarter(me.y, 1 - me.x), quarter(1 - me.y, me.x)
    low_x, high_y = quarter(me.y, 1 - me.x, 0, 96), quarter(1 - me.y, me.x, 96, 96)
    corner = quarter(1 - me.y, 1 - me.x)

    @pl.when(me.cross == 0)
    def _():
        attn_over().wait_recv()
        total = add(a_fin[...], a_two[...])
        for n, bit in enumerate(bits):
            ae[n, 0] = total
            step = attn_copy(16 + n, ae.at[n, 0], ae.at[n, 1], bit)
            step.start()
            step.wait()
            total = add(total, ae[n, 1])
        g_attn[pl.ds(pl.multiple_of((me.y * 2 + me.x) * 192, 32), 192)] = total
        attn_send(1, mine, me.xn).start()
        attn_send(2, mine, me.yn).start()
        attn_send(3, mine, me.sib).start()

    ff_3[0].wait_recv()
    va[0] = add(va[0], f3[0])
    ff_4.wait_recv()
    total = add(va[0], f4[...])
    for n, bit in enumerate(bits):
        fe[n, 0] = total
        step = links.start(fe.at[n, 0], fe.at[n, 1], bit)
        step.wait_recv()
        total = add(total, fe[n, 1])
    for h in range(2):
        g_ff[:, pl.ds(pl.multiple_of(me.place * 96 + h * 48, 16), 48)] = total[h]
    spread = Spread(me, links, view_3d(g_ff))

    @pl.when(me.cross == 0)
    def _():
        attn_send(1, block_x, me.xn).wait_recv()
        attn_send(4, low_x, me.yn).start()
        attn_send(5, block_x, me.sib).start()
        attn_send(2, block_y, me.yn).wait_recv()
        attn_send(6, high_y, me.xn).start()
        attn_send(7, block_y, me.sib).start()

    spread.second()

    @pl.when(me.cross == 0)
    def _():
        attn_send(4, low_x, me.yn).wait_recv()
        attn_send(6, high_y, me.xn).wait_recv()
        attn_send(12, corner, me.sib).start()
        for n, src, to in (
            (1, mine, me.xn), (2, mine, me.yn), (3, mine, me.sib), (4, low_x, me.yn), (5, block_x, me.sib),
            (6, high_y, me.xn), (7, block_y, me.sib), (12, corner, me.sib),
        ):
            attn_send(n, src, to).wait_send()

    @pl.when(me.cross == 1)
    def _():
        for ch in range(CHUNKS):
            trades[ch].wait_recv()
            g_tok[rows(ch)] = trade_in[rows(ch)].astype(F32)
        attn_over().wait_send()
        for n, src in ((3, mine), (5, block_x), (7, block_y), (12, corner)):
            attn_send(n, src, me.sib).wait_recv()
        for ch in range(CHUNKS):
            trades[ch].wait_send()

    spread.third()
    spread.last()
    links.wait_sends()


def solution(mesh):
    dp, tensor = mesh.shape["dp"], mesh.shape["tensor"]
    assert tensor == 4 and dp >= 8 and dp & (dp - 1) == 0
    extra = [1 << b for b in range(3, dp.bit_length() - 1)]
    both = ("dp", "tensor")

    def cell(i, k):
        return i * tensor + k

    def over(x, bit):
        return lax.ppermute(x, "dp", [(i, i ^ bit) for i in range(dp)])

    away = [(i, k) for i in range(dp) for k in range(tensor) if (i & 1) != (k >> 1)]

    def trade(x):
        return lax.ppermute(x, both, [(cell(i, k), cell(i ^ 1, k ^ 2)) for i, k in away])

    smem = pl.BlockSpec(memory_space=pltpu.SMEM)
    vmem = pl.BlockSpec(memory_space=pltpu.VMEM)
    hbm = pl.BlockSpec(memory_space=pl.ANY)

    def shape(*dims, dtype=BF16):
        return jax.ShapeDtypeStruct(dims, dtype)

    def dma(*dims):
        return pltpu.SemaphoreType.DMA(dims)

    def params(mib, number=None):
        if number is None:
            return pltpu.CompilerParams(vmem_limit_bytes=mib << 20)
        return pltpu.CompilerParams(vmem_limit_bytes=mib << 20, collective_id=number, has_side_effects=True)

    def on_device(tokens, segments, w_qkv, w_out, w_gate_up, w_down, norm_gain, norm_bias, cotangent):
        p, z = lax.axis_index("dp"), lax.axis_index("tensor")
        swapped = (p & 1) != (z >> 1)
        place = p & 7

        own = jnp.concatenate([w_qkv.transpose(1, 2, 0).reshape(576, 768), w_out])
        rows = lax.dynamic_slice(w_gate_up, (place * 96, 0, 0), (96, 2, 768))
        block = jnp.stack([rows[:, 0], rows[:, 1], lax.dynamic_slice(w_down, (place * 96, 0), (96, 768))])

        tok, wx, wf0, wf2, zb = pl.pallas_call(
            start_kernel,
            name="start",
            out_shape=(
                shape(4, 512, 768), shape(768, 768), shape(3, 768, 768), shape(3, 768, 768), shape(2, 3, 96, 768),
            ),
            in_specs=[hbm] * 3,
            out_specs=(hbm,) * 5,
            scratch_shapes=[dma(2, 4, CHUNKS), dma(4, CHUNKS), dma(40), dma(40), dma(4)],
            compiler_params=params(16, 0),
        )(tokens[0], own, block)

        row = jnp.where(swapped, over(segments, 1), segments)[0]
        length = row.shape[0]
        onehot = (row[None, :] == jnp.arange(SEGS, dtype=jnp.int32)[:, None]).astype(jnp.int32)
        counts = jnp.sum(onehot, axis=1)
        order = jnp.arange(SEGS, dtype=jnp.int32)
        starts = jnp.sum(jnp.where(order[None, :] < order[:, None], counts[None, :], 0), axis=1)
        first_place = jnp.sum(onehot * starts[:, None], axis=0)
        end_place = first_place + jnp.sum(onehot * counts[:, None], axis=0)
        lo = first_place.reshape(-1, BLK)[:, 0] // BLK
        hi = (end_place.reshape(-1, BLK)[:, -1] + (BLK - 1)) // BLK
        seg = row[None, :]
        places = (jnp.arange(length, dtype=jnp.int32) - first_place)[None, :].astype(F32)
        inverse = jnp.exp(-2.0 * jnp.arange(HEAD_DIM // 2, dtype=F32) / HEAD_DIM * log_base)
        angles = inverse[:, None] * places
        cos, sin = jnp.cos(angles), jnp.sin(angles)
        sc = jnp.concatenate([jnp.full((8,), swapped.astype(jnp.int32)), lo, hi]).astype(jnp.int32)

        zc = lax.ppermute(zb, "tensor", [(i, i ^ 1) for i in range(tensor)])
        cot, _ = lax.optimization_barrier((cotangent[0], zb))
        cot = jnp.where(swapped, trade(cot), cot)

        w, qa, ka, kt, vn, ot, logsum, part = pl.pallas_call(
            attend_forward_kernel,
            name="attend_forward",
            out_shape=(
                shape(768, 768), shape(3, 128, length), shape(3, length, 128), shape(192, length),
                shape(3, length, 64), shape(192, length), shape(8, length, dtype=F32), shape(4, 512, 768),
            ),
            in_specs=[smem, vmem, vmem, vmem, vmem, hbm, hbm],
            out_specs=(vmem,) * 8,
            scratch_shapes=[
                pltpu.VMEM((3, 80, length), BF16),
                pltpu.VMEM((3, 1, BLK), F32),
                pltpu.VMEM((3, 80, BLK), F32),
                dma(1),
            ],
            compiler_params=params(48),
            cost_estimate=pl.CostEstimate(flops=20_000_000_000, bytes_accessed=24_000_000, transcendentals=6_000_000),
        )(sc, tok, cos, sin, seg, own, wx)

        out, gz1, gb, sums, keep_a, keep_b, send_a, send_b = pl.pallas_call(
            feed_forward_kernel,
            name="feed_forward",
            out_shape=(
                shape(512, 768), shape(512, 768, dtype=F32), shape(4, 512, 768), shape(8, 768, dtype=F32),
                *(shape(4, 2, 3, 48, 768),) * 4,
            ),
            in_specs=[hbm] + [vmem] * 4 + [hbm] * 3,
            out_specs=(vmem,) * 4 + (hbm,) * 4,
            scratch_shapes=[
                pltpu.VMEM((4, 3, 768, 768), BF16),
                pltpu.VMEM((4, 512, 768), BF16),
                pltpu.VMEM((4, 512, 768), BF16),
                pltpu.VMEM((4, 512, 768), BF16),
                pltpu.VMEM((512, 768), BF16),
                pltpu.VMEM((768, 512), BF16),
                pltpu.VMEM((512, 768), BF16),
                pltpu.VMEM((768, 512), BF16),
                pltpu.VMEM((512, 768), F32),
                pltpu.VMEM((512, 768), F32),
                pltpu.VMEM((512, 128), F32),
                pltpu.VMEM((2, 3, 768, 768), BF16),
                pltpu.VMEM((4, 4, 3, 96, 768), BF16),
                pltpu.VMEM((512, 768), BF16),
                pltpu.VMEM((2, 512, 768), BF16),
                pltpu.VMEM((512, 768), BF16),
                pltpu.VMEM((512, 768), BF16),
                dma(64), dma(64), dma(5), dma(2, 8),
            ],
            compiler_params=params(62, 1),
            cost_estimate=pl.CostEstimate(flops=22_000_000_000, bytes_accessed=36_000_000, transcendentals=3_000_000),
        )(tok, part, cot, norm_gain, norm_bias, wf0, wf2, zc)

        recv_a, recv_b = over(send_a, 4), over(send_b, 2)
        output = jnp.where(swapped, trade(out), out)[None]

        grads, part = pl.pallas_call(
            attend_backward_kernel,
            name="attend_backward",
            out_shape=(shape(768, 768), shape(4, 512, 768)),
            in_specs=[smem] + [vmem] * 11,
            out_specs=(vmem,) * 2,
            scratch_shapes=[
                pltpu.VMEM((192, length), BF16),
                pltpu.VMEM((8, length), F32),
                pltpu.VMEM((192, length), F32),
                pltpu.VMEM((3, 64, BLK), F32),
                pltpu.VMEM((3, 64, BLK), F32),
                pltpu.VMEM((576, length), BF16),
            ],
            compiler_params=params(48),
            cost_estimate=pl.CostEstimate(flops=40_000_000_000, bytes_accessed=24_000_000, transcendentals=6_000_000),
        )(sc, gb, tok, w, qa, ka, kt, vn, ot, logsum, cos, sin)

        spare = max(len(extra), 1)
        half = (48, 768)
        g_ff, g_attn, g_tok, sums = pl.pallas_call(
            functools.partial(finish_kernel, extra),
            name="finish",
            out_shape=(shape(3, 768, 768), shape(768, 768), shape(512, 768, dtype=F32), shape(8, 768, dtype=F32)),
            in_specs=[vmem] * 8,
            out_specs=(vmem,) * 4,
            scratch_shapes=[
                pltpu.VMEM((4, 3, *half), BF16),
                pltpu.VMEM((4, 3, *half), BF16),
                pltpu.VMEM((4, 3, *half), BF16),
                pltpu.VMEM((4, 3, *half), BF16),
                pltpu.VMEM((4, 2, 3, *half), BF16),
                pltpu.VMEM((2, 2, 3, *half), BF16),
                pltpu.VMEM((2, 3, *half), BF16),
                pltpu.VMEM((spare, 2, 2, 3, *half), BF16),
                pltpu.VMEM((2, 2, 96, 768), BF16),
                pltpu.VMEM((2, 96, 768), BF16),
                pltpu.VMEM((2, 96, 768), BF16),
                pltpu.VMEM((192, 768), BF16),
                pltpu.VMEM((192, 768), BF16),
                pltpu.VMEM((spare, 2, 192, 768), BF16),
                pltpu.VMEM((2, 512, 768), BF16),
                pltpu.VMEM((512, 768), BF16),
                pltpu.VMEM((512, 768), BF16),
                pltpu.VMEM((512, 768), BF16),
                pltpu.VMEM((512, 768), BF16),
                pltpu.VMEM((5 + spare, 8, 768), F32),
                dma(64), dma(64), dma(16 + spare), dma(16 + spare),
            ],
            compiler_params=params(48, 2),
        )(keep_a, keep_b, recv_a, recv_b, grads, part, gz1, sums)

        full = g_attn.astype(F32)
        return (
            output,
            g_tok[None],
            full[:576].reshape(3, 192, 768).transpose(2, 0, 1),
            full[576:],
            g_ff[:2].transpose(1, 0, 2).astype(F32),
            g_ff[2].T.astype(F32),
            sums[0:2],
            sums[2:4],
        )

    placed = (
        P("dp", "tensor", None),
        P("dp", None),
        P(None, None, "tensor"),
        P("tensor", None),
        P(None, None, "tensor"),
        P("tensor", None),
        P(),
        P(),
        P("dp", "tensor", None),
    )
    return jax.shard_map(
        on_device,
        mesh=mesh,
        in_specs=placed,
        out_specs=(
            P("dp", "tensor", None),
            P("dp", "tensor", None),
            P(None, None, "tensor"),
            P("tensor", None),
            P(None, None, "tensor"),
            P("tensor", None),
            P(),
            P(),
        ),
        check_vma=False,
    )
```

time: 588 us -> 406 us (0.69); the launches traced: 576 us -> 402 us
  waiting for transfers between devices: 272 us -> 0.02 us
  Pallas kernels: 107 us -> 358 us
  starting transfers between devices: 88.1 us -> 4.88 us
  other arithmetic: 48.2 us -> 8.07 us
  local copies, waits for them, and re-layouts: 58 us -> 30.6 us
    pallas_call x0 -> x2, Pallas kernels: none -> 191 us  [the longest x1 122 us: on_device(): pl.pallas_call(functools.partial(finish_kernel, extra), name='finish', ou...]
    ppermute x14 -> x1, waiting for transfers between devices: 146 us -> 0.01 us  [on_device(): zc = lax.ppermute(zb, 'tensor', [(i, i ^ 1) for i in range(tensor)])]
    ppermute x56 -> x3, waiting for transfers between devices: 127 us -> 0.01 us  [over(): return lax.ppermute(x, 'dp', [(i, i ^ bit) for i in range(dp)])]
    ppermute x56 -> x3, starting transfers between devices: 69.4 us -> 2.62 us  [over(): return lax.ppermute(x, 'dp', [(i, i ^ bit) for i in range(dp)])]
    pallas_call x1, Pallas kernels: 37.9 us -> 99.8 us  [on_device(): pl.pallas_call(feed_forward_kernel, name='feed_forward', out_shape=(shape...]
    rev x7 -> x0, local copies, waits for them, and re-layouts: 16.5 us -> none  [unturn(): v.reshape(n // (2 << axis_index), 2, 1 << axis_index, *v.shape[1:])[:, ::-1]]
    ppermute x14 -> x1, starting transfers between devices: 14.5 us -> 0.01 us  [on_device(): zc = lax.ppermute(zb, 'tensor', [(i, i ^ 1) for i in range(tensor)])]
    select_n x8 -> x2, other arithmetic: 16.9 us -> 2.68 us  [the longest x1 2.67 us: on_device(): cot = jnp.where(swapped, trade(cot), cot)]
  transfers between devices with their start and end apart: 73 -> 6, of which waited for: 37 -> 0; matrix products, arithmetic and copies ran while one was open for 11% -> 2% of each run, Pallas kernels for 12% -> 34%
where the time goes in v3:
time: 406 us; the launch traced here: 402 us
  Pallas kernels  358 us (88%)
  local copies, waits for them, and re-layouts  30.6 us (8%)
  other arithmetic  8.07 us (2%)
  starting transfers between devices  4.88 us (1%)
    pallas_call x1, Pallas kernels, on_device(): pl.pallas_call(functools.partial(finish_kernel, extra), name='finish', ou...  122 us
    pallas_call x1, Pallas kernels, on_device(): pl.pallas_call(feed_forward_kernel, name='feed_forward', out_shape=(shape...  99.8 us
    pallas_call x1, Pallas kernels, on_device(): pl.pallas_call(start_kernel, name='start', out_shape=(shape(4, 512, 768),...  68.1 us
    pallas_call x1, Pallas kernels, on_device(): pl.pallas_call(attend_backward_kernel, name='attend_backward', out_shape=...  34.5 us
    pallas_call x1, Pallas kernels, on_device(): pl.pallas_call(attend_forward_kernel, name='attend_forward', out_shape=(s...  32.8 us
    unnamed x51, local copies, waits for them, and re-layouts  26.1 us
  transfers between devices with their start and end apart: 6, of which 0 were waited for; matrix products, arithmetic and copies ran while one was open for 2% of the time, Pallas kernels for 34%

profile of v3, /device:TPU:0, one launch (start us, length us, event | category | flops | bytes accessed | tf_op | source)
XLA Modules:
  0.0 402.4 jit_solution(11956835181888270925)
XLA Ops:
  0.6 0.0 copy-start
  0.7 0.0 copy-start.22
  0.7 0.0 copy-start.20
  0.7 0.5 collective-permute-start
  1.2 0.7 copy-done
  1.9 1.5 constant_dynamic-slice_fusion
  3.5 0.0 copy-start.5
  3.5 0.0 copy-done.22
  3.5 0.1 pad_maximum_fusion.wo.own
  3.6 0.0 copy-start.23
  3.6 0.1 pad_maximum_fusion.1.fb
  3.7 0.9 copy-done.5
  4.6 68.1 %start.1 = (bf16[4,512,768]{2,1,0:T(8,128)(2,1)S(1)}, bf16[768,768]{1,0:T(8,128)(2,1)S(1)}, bf16[3,768,768]{2,1,0:T(8,128)(2,1)S(1)}, bf16[3,768,768]{2,1,0:T(8,128)(2,1)S(1)}, bf16[2,3,96,768]{3,2,1,0:T(8,128)(2,1)}) custom-call(bf16[512,768]{1,0:T(8,128)(2,1)S(1)} %bitcast.26, bf16[768,768]{1,0:T(8,128)(2,1)S(1)} %pad_maximum_fusion.wo.own, ...), custom_call_target="tpu_custom_call" | custom-call | tf_op jit(solution)/shard_map/start/pallas_call | solution.py:838
  72.8 0.0 copy-start.7
  72.8 1.8 copy-done.7
  74.6 1.8 copy-done.8
  76.3 1.7 copy-done.9
  78.0 0.0 collective-permute-start.2
  78.0 1.5 collective-permute-start.1
  79.6 0.0 collective-permute-done
  79.6 0.0 copy-done.23
  79.6 0.1 convert_reduce_fusion
  79.7 0.1 select_reduce_fusion.2
  79.9 0.1 select_reduce_fusion.1
  80.0 0.2 slice_reduce_fusion
  80.2 1.0 multiply_sine_fusion
  81.2 0.1 pad_add_fusion.sc
  81.3 32.8 %attend_forward.1 = (bf16[768,768]{1,0:T(8,128)(2,1)S(1)}, bf16[3,128,2048]{2,1,0:T(8,128)(2,1)}, bf16[3,2048,128]{2,1,0:T(8,128)(2,1)}, bf16[192,2048]{1,0:T(8,...) custom-call(s32[24]{0:T(128)S(1)} %pad_add_fusion.sc, ...), custom_call_target="tpu_custom_call" | custom-call | flops 20000000000 | bytes 24000000 | tf_op jit(solution)/shard_map/attend_forward/pallas_call | solution.py:871
  114.1 0.0 copy-start.11
  114.2 1.0 copy-done.11
  115.2 0.0 collective-permute-done.1
  115.2 2.7 broadcast_select_fusion.cot
  117.9 0.0 collective-permute-done.2.zc
  117.9 0.0 copy-done.13
  117.9 99.8 %feed_forward.1 = (bf16[512,768]{1,0:T(8,128)(2,1)}, f32[512,768]{1,0:T(8,128)}, bf16[4,512,768]{2,1,0:T(8,128)(2,1)}, f32[8,768]{1,0:T(8,128)}, bf16[4,2,3,48,7...) custom-call(bf16[4,512,768]{2,1,0:T(8,128)(2,1)} %copy-done.9, ...), custom_call_target="tpu_custom_call" | custom-call | flops 22000001024 | bytes 36000000 | tf_op jit(solution)/shard_map/feed_forward/pallas_call | solution.py:890
  217.7 0.7 collective-permute-start.3
  218.4 1.0 collective-permute-start.4
  219.4 1.1 collective-permute-start.5
  220.5 0.0 copy-done.12
  220.5 1.4 copy-done.10
  221.9 1.1 copy-done.14
  223.1 1.1 copy-done.16
  224.2 34.5 %attend_backward.1 = (bf16[768,768]{1,0:T(8,128)(2,1)S(1)}, bf16[4,512,768]{2,1,0:T(8,128)(2,1)}) custom-call(s32[24]{0:T(128)S(1)} %pad_add_fusion.sc, bf16[4,512,768]{2,1,0:T(8,128)(2,1)} %get-tuple-element.48.gb, bf16[4,512,768]{2,1,0:T(8,128)(2,1)} %copy-done.9, bf16[768,768]{1,0:T(8,128)(2,1)S(1)} %copy-done.12, bf16[3,128,2048]{2,1,0:T(8,128)(2,1)S(1)} %copy-done.10, ...), custom_call_target="tpu_custom_call" | custom-call | flops 40000000000 | bytes 24000000 | tf_op jit(solution)/shard_map/attend_backward/pallas_call | solution.py:926
  258.7 0.0 copy-start.4
  258.7 0.0 copy-start.6
  258.7 0.0 collective-permute-done.3
  258.7 1.0 select_bitcast_fusion
  259.7 0.0 collective-permute-done.4.recv_a
  259.7 0.0 collective-permute-done.5.recv_b
  259.7 0.0 copy-start.19
  259.7 1.2 copy-done.18
  260.9 0.6 copy-done.19
  261.5 0.0 copy-done.6
  261.5 122.5 %finish.1 = (bf16[3,768,768]{2,1,0:T(8,128)(2,1)}, bf16[768,768]{1,0:T(8,128)(2,1)S(1)}, f32[512,768]{1,0:T(8,128)S(1)}, f32[8,768]{1,0:T(8,128)S(1)}) custom-call(bf16[4,2,3,48,768]{4,3,2,1,0:T(8,128)(2,1)} %get-tuple-element.44.keep_a, bf16[4,2,3,48,768]{4,3,2,1,0:T(8,128)(2,1)} %get-tuple-element.45.keep_b, bf16[4,2,3,48,768]{4,3,2,1,0:T(8,128)(2,1)} %copy-done.18, ...), custom_call_target="tpu_custom_call" | custom-call | tf_op jit(solution)/shard_map/finish/pallas_call | solution.py:946
  383.9 0.0 copy-start.2
  384.0 0.9 slice.44
  384.9 1.3 slice.43
  386.2 1.3 copy-done.17
  387.5 0.2 convert_bitcast_fusion.1
  387.7 2.5 convert_bitcast_fusion
  390.2 0.6 fusion.2
  390.8 1.9 copy.28
  392.7 8.3 %copy.27 = f32[768,2,768]{2,1,0:T(2,128)} copy(f32[768,2,768]{2,0,1:T(8,128)} %convert_bitcast_fusion) | data formatting | bytes 9437184
  401.0 1.1 copy.35
  (29 shorter events, 0.1 us)
Async XLA Ops:
  0.6 1.3 copy-start
  0.7 2.9 copy-start.22
  0.7 2.9 copy-start.20
  0.7 78.9 %collective-permute-start = (s32[1,2048]{1,0:T(1,128)}, s32[1,2048]{1,0:T(1,128)S(1)}, u32[]{:S(2)}, u32[]{:S(2)}) collective-permute-start(s32[1,2048]{1,0:T(1,128)} %param.10), channel_id=1, source_target_pairs={{0,4},{4,0},{8,12},{12,8},{16,20},{20,16},{24,28},{28,24},{1,5},{5... | collective-permute-start | bytes 24584 | tf_op jit(solution)/shard_map/ppermute | solution.py:807
  3.5 1.1 copy-start.5
  3.6 75.9 %copy-start.23 = (s32[1,2048]{1,0:T(1,128)S(1)}, s32[1,2048]{1,0:T(1,128)}, u32[]{:S(2)}) copy-start(s32[1,2048]{1,0:T(1,128)} %param.10) | copy-start | bytes 24580
  72.8 1.8 copy-start.7
  74.6 1.8 copy-start.8
  76.3 1.7 copy-start.9
  78.0 39.9 %collective-permute-start.2 = (bf16[2,3,96,768]{3,2,1,0:T(8,128)(2,1)}, bf16[2,3,96,768]{3,2,1,0:T(8,128)(2,1)}, u32[]{:S(2)}, u32[]{:S(2)}) collective-permute-start(bf16[2,3,96,768]{3,2,1,0:T(8,128)(2,1)} %get-tuple-element.39), channel_id=1, source_target_pairs={{0,1},{1,0},{2,3},{3,2},{4,5},{5,4},{6,7},{7,6},{8,9},{9,8},{10,11... | collective-permute-start | bytes 2654216 | tf_op jit(solution)/shard_map/ppermute | solution.py:867
  78.0 37.2 %collective-permute-start.1 = (bf16[512,768]{1,0:T(8,128)(2,1)}, bf16[512,768]{1,0:T(8,128)(2,1)}, u32[]{:S(2)}, u32[]{:S(2)}) collective-permute-start(bf16[512,768]{1,0:T(8,128)(2,1)} %bitcast.7), channel_id=1, source_target_pairs={{2,4},{3,5},{4,2},{5,3},{10,12},{11,13},{12,10},{13,11},{18,20},{1... | collective-permute-start | bytes 2359304 | tf_op jit(solution)/shard_map/ppermute | solution.py:812
  114.1 1.0 copy-start.11
  115.2 2.7 copy-start.13
  115.2 2.7 copy-start.15
  117.9 102.6 %copy-start.12 = (bf16[768,768]{1,0:T(8,128)(2,1)S(1)}, bf16[768,768]{1,0:T(8,128)(2,1)}, u32[]{:S(2)}) copy-start(bf16[768,768]{1,0:T(8,128)(2,1)} %copy-done.11) | copy-start | bytes 3538948
  217.7 41.0 %collective-permute-start.3 = (bf16[512,768]{1,0:T(8,128)(2,1)}, bf16[512,768]{1,0:T(8,128)(2,1)S(1)}, u32[]{:S(2)}, u32[]{:S(2)}) collective-permute-start(bf16[512,768]{1,0:T(8,128)(2,1)} %get-tuple-element.43), channel_id=1, source_target_pairs={{2,4},{3,5},{4,2},{5,3},{10,12},{11,13},{12,10},{13,11},{18,20},{1... | collective-permute-start | bytes 2359304 | tf_op jit(solution)/shard_map/ppermute | solution.py:812
  218.4 41.3 %collective-permute-start.4 = (bf16[4,2,3,48,768]{4,3,2,1,0:T(8,128)(2,1)}, bf16[4,2,3,48,768]{4,3,2,1,0:T(8,128)(2,1)S(1)}, u32[]{:S(2)}, u32[]{:S(2)}) collective-permute-start(bf16[4,2,3,48,768]{4,3,2,1,0:T(8,128)(2,1)} %get-tuple-element.46), channel_id=1, source_target_pairs={{0,16},{4,20},{8,24},{12,28},{16,0},{20,4},{24,8},{28,12},{1,17},{... | collective-permute-start | bytes 5308424 | tf_op jit(solution)/shard_map/ppermute | solution.py:807
  219.4 40.3 %collective-permute-start.5 = (bf16[4,2,3,48,768]{4,3,2,1,0:T(8,128)(2,1)}, bf16[4,2,3,48,768]{4,3,2,1,0:T(8,128)(2,1)S(1)}, u32[]{:S(2)}, u32[]{:S(2)}) collective-permute-start(bf16[4,2,3,48,768]{4,3,2,1,0:T(8,128)(2,1)} %get-tuple-element.47), channel_id=1, source_target_pairs={{0,8},{4,12},{8,0},{12,4},{16,24},{20,28},{24,16},{28,20},{1,9},{5... | collective-permute-start | bytes 5308424 | tf_op jit(solution)/shard_map/ppermute | solution.py:807
  220.5 1.4 copy-start.10
  221.9 1.1 copy-start.14
  223.1 1.1 copy-start.16
  224.2 34.5 %copy-start.21 = (bf16[512,768]{1,0:T(8,128)(2,1)S(1)}, bf16[512,768]{1,0:T(8,128)(2,1)}, u32[]{:S(2)}) copy-start(bf16[512,768]{1,0:T(8,128)(2,1)} %get-tuple-element.43) | copy-start | bytes 2359300
  258.7 2.8 copy-start.4
  258.7 2.8 copy-start.6
  259.7 1.2 copy-start.18
  259.7 1.8 copy-start.19
  383.9 2.3 copy-start.2
  384.9 2.6 copy-start.17
  392.7 8.3 %copy-start.3 = (f32[512,768]{1,0:T(8,128)S(1)}, f32[512,768]{1,0:T(8,128)}, u32[]{:S(2)}) copy-start(f32[512,768]{1,0:T(8,128)} %copy-done.2) | copy-start | bytes 4718596
  392.7 9.5 %copy-start.1 = (bf16[768,768]{1,0:T(8,128)(2,1)S(1)}, bf16[768,768]{1,0:T(8,128)(2,1)}, u32[]{:S(2)}) copy-start(bf16[768,768]{1,0:T(8,128)(2,1)} %param.14) | copy-start | bytes 3538948

commit v4 on v3

--- a/solution.py
+++ b/solution.py
@@ -87,10 +87,6 @@
             copy.wait_send()
 
 
-def rows_of(place, size=96, first=0):
-    return pl.ds(pl.multiple_of(place * size + first, 16), size - first if first == 0 else size // 2)
-
-
 class Spread:
     def __init__(self, me, links, view, src=None):
         self.me, self.links, self.view = me, links, view
@@ -125,6 +121,18 @@
             copy.wait_recv()
 
 
+class Corner(Spread):
+    def __init__(self, me, links, view, own, from_x, from_y):
+        self.me, self.links, self.view = me, links, view
+        first, last = pl.ds(0, 48), pl.ds(48, 48)
+        self.low = links.start(from_x.at[:, first], view(me.x_place, 0, 48), me.yn)
+        self.high = links.start(from_y.at[:, last], view(me.y_place, 48, 48), me.xn)
+        self.from_sib = [
+            links.start(src, view(place, 0, 96), me.sib)
+            for src, place in ((own, me.place), (from_x, me.x_place), (from_y, me.y_place))
+        ]
+
+
 def view_2d(ref):
     return lambda place, first, size: ref.at[pl.ds(pl.multiple_of(place * 96 + first, 16), size)]
 
@@ -133,7 +141,7 @@
     return lambda place, first, size: ref.at[:, pl.ds(pl.multiple_of(place * 96 + first, 16), size)]
 
 
-def start_kernel(x, wo, fb, tok, wx, wf0, wf2, zb, token_send, token_recv, send, recv, local):
+def start_kernel(x, wo, fb, tok, wx, wf0, zb, token_send, token_recv, send, recv, local):
     me = Place()
     c, z = me.c, me.z
     away = z + c * (3 - 2 * z)
@@ -182,7 +190,7 @@
 
     links = Links(send, recv)
     attn_z = links.start(view_2d(wo)(me.place, 0, 96), view_2d(wx)(me.place, 0, 96), me.z2)
-    ff_z = links.start(fb, view_3d(wf2)(me.place, 0, 96), me.z2)
+    ff_z = links.start(fb, zb.at[1], me.z2)
     ff0 = Spread(me, links, view_3d(wf0), fb)
     here = [
         pltpu.make_async_copy(fb, view_3d(wf0)(me.place, 0, 96), local.at[0]),
@@ -215,19 +223,13 @@
     attn_z.wait_recv()
     attn = Spread(me, links, view_2d(wx))
     forward(0)
+    ff0.second()
+    forward(1)
     attn.second()
-    ff0.second()
-    attn.third()
-    forward(1)
-    ff_z.wait_recv()
-    ff2 = Spread(me, links, view_3d(wf2))
-    keep = pltpu.make_async_copy(view_3d(wf2)(me.place, 0, 96), zb.at[1], local.at[3])
-    keep.start()
     ff0.third()
     forward(2)
-    ff2.second()
+    attn.third()
     forward(3)
-    ff2.third()
 
     @pl.when(away >= 2)
     def _():
@@ -238,11 +240,11 @@
                     recv_sem=token_recv.at[k, ch], device_id=me.sib, device_id_type=MESH,
                 ).wait_recv()
 
-    for spread in (attn, ff0, ff2):
+    for spread in (attn, ff0):
         spread.last()
+    ff_z.wait_recv()
     for h in here:
         h.wait()
-    keep.wait()
     links.wait_sends()
     for k, to in ((0, near), (1, far), (2, near), (3, near)):
 
@@ -415,21 +417,32 @@
 
 
 def feed_forward_kernel(
-    tok, part, cot, gain, bias, wf0, wf2, zc,
-    out, gz1, gb, sums, keep_a, keep_b, send_a, send_b,
-    w, slope_g, slope_u, hid, nb, nbt, gm, gmt, total, norm1, inv1, dw, lw, xs, from_core, from_z, to_z,
-    send, recv, local, out_sem,
+    tok, part, cot_in, gain, bias, wf0, zb, zx, zy, zc,
+    out, gz1, gb, sums, keep_a, keep_b, send_a, send_b, zs_out,
+    w, slope_g, slope_u, hid, nb, nbt, gm, gmt, total, norm1, inv1, dw, lw, xs, cot, from_core, from_z, to_z,
+    f1a, f1b, f2a, f2b, send, recv, local, out_sem, trade_sem,
 ):
     me = Place()
-    greet((me.sib, me.xn, me.yn, me.z1))
+    greet((me.sib, me.xn, me.yn, me.z1, me.pair))
     links = Links(send, recv)
     loads = [
         pltpu.make_async_copy(tok.at[me.slot], xs, local.at[0]),
         pltpu.make_async_copy(wf0, w.at[0], local.at[1]),
-        pltpu.make_async_copy(wf2, w.at[2], local.at[2]),
+        pltpu.make_async_copy(zb.at[1], view_3d(w.at[2])(me.place, 0, 96), local.at[2]),
         pltpu.make_async_copy(zc.at[0], view_3d(w.at[1])(me.place, 0, 96), local.at[3]),
         pltpu.make_async_copy(zc.at[1], view_3d(w.at[3])(me.place, 0, 96), local.at[4]),
+        pltpu.make_async_copy(zx, view_3d(w.at[2])(me.x_place, 0, 96), local.at[5]),
+        pltpu.make_async_copy(zy, view_3d(w.at[2])(me.y_place, 0, 96), local.at[6]),
     ]
+
+    def cot_here():
+        return pltpu.make_async_copy(cot_in, cot, local.at[7])
+
+    def cot_there():
+        return pltpu.make_async_remote_copy(
+            src_ref=cot_in, dst_ref=cot, send_sem=trade_sem.at[0], recv_sem=trade_sem.at[1], device_id=me.pair,
+            device_id_type=MESH,
+        )
 
     def rows(ch):
         return pl.ds(ch * CHUNK, CHUNK)
@@ -438,6 +451,7 @@
         [links.start(part.at[shard, rows(ch)], from_core.at[i, rows(ch)], me.sib) for ch in range(CHUNKS)]
         for i, shard in ((1, me.slot3), (0, me.slot2))
     ]
+    ff2 = Corner(me, links, view_3d(w.at[2]), zb.at[1], zx, zy)
     ff1 = Spread(me, links, view_3d(w.at[1]), zc.at[0])
     ff3 = Spread(me, links, view_3d(w.at[3]), zc.at[1])
     for load in loads:
@@ -448,6 +462,16 @@
         at = rows(ch)
         to_z[at] = (part[me.slot1, at].astype(F32) + from_core[1, at].astype(F32)).astype(BF16)
         zs.append(links.start(to_z.at[at], from_z.at[at], me.z1))
+
+    @pl.when(me.cross == 0)
+    def _():
+        cot_here().start()
+
+    @pl.when(me.cross == 1)
+    def _():
+        cot_there().start()
+
+    ff2.third()
     ff1.second()
     loads[0].wait()
     for ch in range(CHUNKS):
@@ -480,7 +504,9 @@
     loads[1].wait()
     forward(0)
     ff3.third()
-    loads[2].wait()
+    for load in (loads[2], loads[5], loads[6]):
+        load.wait()
+    ff2.last()
     forward(2)
     loads[3].wait()
     ff1.last()
@@ -490,6 +516,15 @@
     forward(3)
     n2, i2 = norm_forward(total[...])
     out[...] = (n2 * gain[1:2, :] + bias[1:2, :]).astype(BF16)
+
+    @pl.when(me.cross == 0)
+    def _():
+        cot_here().wait()
+
+    @pl.when(me.cross == 1)
+    def _():
+        cot_there().wait()
+
     g = cot[...].astype(F32)
     sums[1:2, :] = jnp.sum(g * n2, axis=0, keepdims=True)
     sums[3:4, :] = jnp.sum(g, axis=0, keepdims=True)
@@ -501,96 +536,135 @@
     def block(quad, core):
         return pl.ds(pl.multiple_of((quad * 2 + core) * 96, 32), 96)
 
-    def stores(ez, i):
+    order = (1, 3, 0, 2)
+    halves = []
+    first, last = pl.ds(0, 48), pl.ds(48, 48)
+
+    def slopes(ez):
+        grad_hidden = nt(gm[...], w[ez, 2])
+        gate = (grad_hidden * slope_g[ez].astype(F32)).astype(BF16)
+        up = (grad_hidden * slope_u[ez].astype(F32)).astype(BF16)
+        slope_g[ez] = gate
+        slope_u[ez] = up
+        total[...] += nt(gate, w[ez, 0]) + nt(up, w[ez, 1])
+
+    def weights(n):
+        i, ez = n % 2, order[n]
+        if n >= 2:
+            for copy in halves[n - 2]:
+                copy.wait_send()
+        dw[i, 2] = nn(gmt[...], hid[ez]).astype(BF16)
+        dw[i, 0] = nn(nbt[...], slope_g[ez]).astype(BF16)
+        dw[i, 1] = nn(nbt[...], slope_u[ez]).astype(BF16)
+        halves.append([links.make(dw.at[i, :, block(quad, 1 - me.c)], lw.at[n, quad], me.sib) for quad in range(4)])
+        for copy in halves[n]:
+            copy.start()
+
+    def settle(n):
+        for quad in range(4):
+            halves[n][quad].wait_recv()
+            for m in range(3):
+                lw[n, quad, m] = (lw[n, quad, m].astype(F32) + dw[n % 2, m, block(quad, me.c)].astype(F32)).astype(BF16)
+
+    plane_1, plane_2 = {}, {}
+
+    def plane_first(n):
+        plane_1[n] = [
+            (
+                links.start(lw.at[n, (1 - me.y) * 2 + o, :, first], f1a.at[n, o], me.yn),
+                links.start(lw.at[n, o * 2 + 1 - me.x, :, last], f1b.at[n, o], me.xn),
+            )
+            for o in range(2)
+        ]
+
+    def plane_second(n):
+        for o in range(2):
+            plane_1[n][o][0].wait_recv()
+            f1a[n, o] = (f1a[n, o].astype(F32) + lw[n, me.y * 2 + o, :, first].astype(F32)).astype(BF16)
+            plane_1[n][o][1].wait_recv()
+            f1b[n, o] = (f1b[n, o].astype(F32) + lw[n, o * 2 + me.x, :, last].astype(F32)).astype(BF16)
+        plane_2[n] = (
+            links.start(f1a.at[n, 1 - me.x], f2a.at[n], me.xn),
+            links.start(f1b.at[n, 1 - me.y], f2b.at[n], me.yn),
+        )
+
+    def plane_last(n):
+        plane_2[n][0].wait_recv()
+        zs_out[n, 0] = (f1a[n, me.x].astype(F32) + f2a[n].astype(F32)).astype(BF16)
+        plane_2[n][1].wait_recv()
+        zs_out[n, 1] = (f1b[n, me.y].astype(F32) + f2b[n].astype(F32)).astype(BF16)
+
+    def stores(n):
         made = []
         for oy in range(2):
             for ox in range(2):
-                row = pl.multiple_of(((oy * 2 + ox) * 2 + me.c) * 96, 32)
-                made.append((me.y == oy, dw.at[i, :, pl.ds(row, 48)], keep_a.at[ez, ox], send_a.at[ez, ox]))
-                row = pl.multiple_of(row + 48, 16)
-                made.append((me.x == ox, dw.at[i, :, pl.ds(row, 48)], keep_b.at[ez, oy], send_b.at[ez, oy]))
+                src = lw.at[n, oy * 2 + ox]
+                made.append((me.y == oy, src.at[:, first], keep_a.at[n - 2, ox], send_a.at[n - 2, ox]))
+                made.append((me.x == ox, src.at[:, last], keep_b.at[n - 2, oy], send_b.at[n - 2, oy]))
         return made
 
-    def store(ez, i):
-        for n, (here, src, kept, sent) in enumerate(stores(ez, i)):
+    def store(n):
+        for number, (here, src, kept, sent) in enumerate(stores(n)):
 
             @pl.when(here)
-            def _(n=n, src=src, kept=kept):
-                pltpu.make_async_copy(src, kept, out_sem.at[i, n]).start()
+            def _(number=number, src=src, kept=kept):
+                pltpu.make_async_copy(src, kept, out_sem.at[n - 2, number]).start()
 
             @pl.when(jnp.logical_not(here))
-            def _(n=n, src=src, sent=sent):
-                pltpu.make_async_copy(src, sent, out_sem.at[i, n]).start()
-
-    def stored(ez, i):
-        for n, (_, src, kept, _) in enumerate(stores(ez, i)):
-            pltpu.make_async_copy(src, kept, out_sem.at[i, n]).wait()
-
-    order = (1, 3, 0, 2)
-    halves = []
-
-    def settle(n):
-        i = n % 2
-        for quad in range(4):
-            halves[n][quad].wait_recv()
-            at = block(quad, me.c)
-            for m in range(3):
-                dw[i, m, at] = (dw[i, m, at].astype(F32) + lw[n, quad, m].astype(F32)).astype(BF16)
-        store(order[n], i)
-
-    for n, ez in enumerate(order):
-        i = n % 2
-        if n >= 2:
-            stored(order[n - 2], i)
-            for copy in halves[n - 2]:
-                copy.wait_send()
-        grad_hidden = nt(gm[...], w[ez, 2])
-        dw[i, 2] = nn(gmt[...], hid[ez]).astype(BF16)
-        gate = (grad_hidden * slope_g[ez].astype(F32)).astype(BF16)
-        dw[i, 0] = nn(nbt[...], gate).astype(BF16)
-        up = (grad_hidden * slope_u[ez].astype(F32)).astype(BF16)
-        dw[i, 1] = nn(nbt[...], up).astype(BF16)
-        halves.append(
-            [links.make(dw.at[i, :, block(quad, 1 - me.c)], lw.at[n, quad], me.sib) for quad in range(4)]
-        )
-        for copy in halves[n]:
-            copy.start()
-        total[...] += nt(gate, w[ez, 0]) + nt(up, w[ez, 1])
-        if n:
-            settle(n - 1)
-
+            def _(number=number, src=src, sent=sent):
+                pltpu.make_async_copy(src, sent, out_sem.at[n - 2, number]).start()
+
+    slopes(1)
+    weights(0)
+    slopes(3)
+    settle(0)
+    plane_first(0)
+    weights(1)
+    slopes(0)
+    settle(1)
+    plane_first(1)
+    slopes(2)
     g = total[...]
     sums[0:1, :] = jnp.sum(g * norm1[...], axis=0, keepdims=True)
     sums[2:3, :] = jnp.sum(g, axis=0, keepdims=True)
     sums[4:8, :] = jnp.zeros((4, 768), F32)
-    first, second, third = [], [], []
+    to_pair, to_core, on_core = [], [], []
     for ch in range(CHUNKS):
         at = rows(ch)
         made = norm_backward(total[at] * gain[0:1, :], norm1[at], inv1[at, 0:1])
         gz1[at] = made
         gb[me.slot, at] = made.astype(BF16)
         mine = gb.at[me.slot, at]
-        first.append(links.start(mine, mine, me.z1))
-        second.append(links.start(mine, mine, me.sib))
-    settle(len(order) - 1)
+        to_pair.append(links.start(mine, mine, me.z1))
+        to_core.append(links.start(mine, mine, me.sib))
+    weights(2)
+    plane_second(0)
+    weights(3)
+    settle(2)
+    store(2)
+    plane_second(1)
+    settle(3)
+    store(3)
     for ch in range(CHUNKS):
-        at = rows(ch)
-        first[ch].wait_recv()
-        other = gb.at[me.slot1, at]
-        third.append(links.start(other, other, me.sib))
-    for copy in second + third:
+        to_pair[ch].wait_recv()
+        other = gb.at[me.slot1, rows(ch)]
+        on_core.append(links.start(other, other, me.sib))
+    plane_last(0)
+    plane_last(1)
+    for copy in to_core + on_core:
         copy.wait_recv()
     for n in (2, 3):
-        stored(order[n], n % 2)
+        for number, (_, src, kept, _) in enumerate(stores(n)):
+            pltpu.make_async_copy(src, kept, out_sem.at[n - 2, number]).wait()
         for copy in halves[n]:
             copy.wait_send()
     links.wait_sends()
 
 
 def finish_kernel(
-    extra, keep_a, keep_b, recv_a, recv_b, ga, part, gz1, sums_in,
+    extra, keep_a, keep_b, recv_a, recv_b, zr, ga, part, gz1, sums_in,
     g_ff, g_attn, g_tok, sums,
-    sa, sb, f2a, f2b, va, f3, f4, fe, a_in, a_mid, a_out, a_fin, a_two, ae, from_core, from_z, to_z, trade_out, trade_in, sum_in,
+    sa, sb, f2a, f2b, va, f4, fe, a_in, a_mid, a_out, a_fin, a_two, ae, from_core, from_z, to_z, trade_out, trade_in, sum_in,
     send, recv, a_send, a_recv,
 ):
     me = Place()
@@ -630,7 +704,6 @@
         if n < len(around):
             small.append(links.start(sums, sum_in.at[n], around[n]))
 
-    order = (1, 3, 0, 2)
     ff_2 = {}
 
     def plane(ez):
@@ -640,12 +713,11 @@
 
     def planed(ez):
         ff_2[ez][0].wait_recv()
-        va[ez, 0] = add(keep_a[ez, me.x], recv_a[ez, me.x], f2a[ez])
+        va[ez, 0] = add(keep_a[ez, me.x], recv_a[ez, me.x], f2a[ez], zr[ez, 0])
         ff_2[ez][1].wait_recv()
-        va[ez, 1] = add(keep_b[ez, me.y], recv_b[ez, me.y], f2b[ez])
+        va[ez, 1] = add(keep_b[ez, me.y], recv_b[ez, me.y], f2b[ez], zr[ez, 1])
 
     plane(1)
-    plane(3)
     zs = []
     for ch in range(CHUNKS):
         cores[0][ch].wait_recv()
@@ -653,7 +725,8 @@
         to_z[at] = add(part[me.slot1, at], from_core[1, at])
         zs.append(links.start(to_z.at[at], from_z.at[at], me.z1))
     plane(0)
-    plane(2)
+    planed(1)
+    ff_4 = links.start(va.at[1], f4, me.z2)
     small_step()
     for copy in attn_1:
         copy.wait_recv()
@@ -661,10 +734,7 @@
     a_mid[1] = add(ga[half(1 - me.y, me.x, 1)], a_in[1, 1 - me.y])
     attn_2 = [links.start(a_mid.at[0], a_out.at[0], me.xn), links.start(a_mid.at[1], a_out.at[1], me.yn)]
     small_step()
-    ff_3 = []
-    for ez in (1, 3):
-        planed(ez)
-        ff_3.append(links.start(va.at[ez], f3.at[(ez - 1) // 2], me.z1))
+    planed(0)
     small_step()
     for copy in attn_2:
         copy.wait_recv()
@@ -710,11 +780,6 @@
             trade_out[at] = got.astype(BF16)
             trades[ch].start()
 
-    planed(0)
-    planed(2)
-    ff_3[1].wait_recv()
-    va[2] = add(va[2], f3[1])
-    ff_4 = links.start(va.at[2], f4, me.z2)
     while len(small) < len(around):
         small_step()
     small_step()
@@ -743,8 +808,6 @@
         attn_send(2, mine, me.yn).start()
         attn_send(3, mine, me.sib).start()
 
-    ff_3[0].wait_recv()
-    va[0] = add(va[0], f3[0])
     ff_4.wait_recv()
     total = add(va[0], f4[...])
     for n, bit in enumerate(bits):
@@ -794,6 +857,14 @@
     links.wait_sends()
 
 
+def widen_kernel(attn, out_rows, gate_up, down, g_qkv, g_out, g_gate_up, g_down):
+    g_qkv[...] = attn[...].astype(F32)
+    g_out[...] = out_rows[...].astype(F32)
+    g_gate_up[:, 0, :] = gate_up[0].astype(F32)
+    g_gate_up[:, 1, :] = gate_up[1].astype(F32)
+    g_down[...] = down[0].astype(F32).T
+
+
 def solution(mesh):
     dp, tensor = mesh.shape["dp"], mesh.shape["tensor"]
     assert tensor == 4 and dp >= 8 and dp & (dp - 1) == 0
@@ -835,14 +906,14 @@
         rows = lax.dynamic_slice(w_gate_up, (place * 96, 0, 0), (96, 2, 768))
         block = jnp.stack([rows[:, 0], rows[:, 1], lax.dynamic_slice(w_down, (place * 96, 0), (96, 768))])
 
-        tok, wx, wf0, wf2, zb = pl.pallas_call(
+        tok, wx, wf0, zb = pl.pallas_call(
             start_kernel,
             name="start",
             out_shape=(
-                shape(4, 512, 768), shape(768, 768), shape(3, 768, 768), shape(3, 768, 768), shape(2, 3, 96, 768),
+                shape(4, 512, 768), shape(768, 768), shape(3, 768, 768), shape(2, 3, 96, 768),
             ),
             in_specs=[hbm] * 3,
-            out_specs=(hbm,) * 5,
+            out_specs=(hbm,) * 4,
             scratch_shapes=[dma(2, 4, CHUNKS), dma(4, CHUNKS), dma(40), dma(40), dma(4)],
             compiler_params=params(16, 0),
         )(tokens[0], own, block)
@@ -865,8 +936,7 @@
         sc = jnp.concatenate([jnp.full((8,), swapped.astype(jnp.int32)), lo, hi]).astype(jnp.int32)
 
         zc = lax.ppermute(zb, "tensor", [(i, i ^ 1) for i in range(tensor)])
-        cot, _ = lax.optimization_barrier((cotangent[0], zb))
-        cot = jnp.where(swapped, trade(cot), cot)
+        zx, zy = over(zb[1], 2), over(zb[1], 4)
 
         w, qa, ka, kt, vn, ot, logsum, part = pl.pallas_call(
             attend_forward_kernel,
@@ -887,15 +957,15 @@
             cost_estimate=pl.CostEstimate(flops=20_000_000_000, bytes_accessed=24_000_000, transcendentals=6_000_000),
         )(sc, tok, cos, sin, seg, own, wx)
 
-        out, gz1, gb, sums, keep_a, keep_b, send_a, send_b = pl.pallas_call(
+        out, gz1, gb, sums, keep_a, keep_b, send_a, send_b, zs = pl.pallas_call(
             feed_forward_kernel,
             name="feed_forward",
             out_shape=(
                 shape(512, 768), shape(512, 768, dtype=F32), shape(4, 512, 768), shape(8, 768, dtype=F32),
-                *(shape(4, 2, 3, 48, 768),) * 4,
+                *(shape(2, 2, 3, 48, 768),) * 5,
             ),
-            in_specs=[hbm] + [vmem] * 4 + [hbm] * 3,
-            out_specs=(vmem,) * 4 + (hbm,) * 4,
+            in_specs=[hbm, vmem, hbm, vmem, vmem] + [hbm] * 5,
+            out_specs=(vmem,) * 4 + (hbm,) * 4 + (vmem,),
             scratch_shapes=[
                 pltpu.VMEM((4, 3, 768, 768), BF16),
                 pltpu.VMEM((4, 512, 768), BF16),
@@ -911,16 +981,22 @@
                 pltpu.VMEM((2, 3, 768, 768), BF16),
                 pltpu.VMEM((4, 4, 3, 96, 768), BF16),
                 pltpu.VMEM((512, 768), BF16),
+                pltpu.VMEM((512, 768), BF16),
                 pltpu.VMEM((2, 512, 768), BF16),
                 pltpu.VMEM((512, 768), BF16),
                 pltpu.VMEM((512, 768), BF16),
-                dma(64), dma(64), dma(5), dma(2, 8),
+                pltpu.VMEM((2, 2, 3, 48, 768), BF16),
+                pltpu.VMEM((2, 2, 3, 48, 768), BF16),
+                pltpu.VMEM((2, 3, 48, 768), BF16),
+                pltpu.VMEM((2, 3, 48, 768), BF16),
+                dma(80), dma(80), dma(8), dma(2, 8), dma(2),
             ],
             compiler_params=params(62, 1),
             cost_estimate=pl.CostEstimate(flops=22_000_000_000, bytes_accessed=36_000_000, transcendentals=3_000_000),
-        )(tok, part, cot, norm_gain, norm_bias, wf0, wf2, zc)
+        )(tok, part, cotangent[0], norm_gain, norm_bias, wf0, zb, zx, zy, zc)
 
         recv_a, recv_b = over(send_a, 4), over(send_b, 2)
+        zr = lax.ppermute(zs, "tensor", [(i, i ^ 1) for i in range(tensor)])
         output = jnp.where(swapped, trade(out), out)[None]
 
         grads, part = pl.pallas_call(
@@ -947,14 +1023,10 @@
             functools.partial(finish_kernel, extra),
             name="finish",
             out_shape=(shape(3, 768, 768), shape(768, 768), shape(512, 768, dtype=F32), shape(8, 768, dtype=F32)),
-            in_specs=[vmem] * 8,
+            in_specs=[vmem] * 9,
             out_specs=(vmem,) * 4,
             scratch_shapes=[
-                pltpu.VMEM((4, 3, *half), BF16),
-                pltpu.VMEM((4, 3, *half), BF16),
-                pltpu.VMEM((4, 3, *half), BF16),
-                pltpu.VMEM((4, 3, *half), BF16),
-                pltpu.VMEM((4, 2, 3, *half), BF16),
+                *[pltpu.VMEM((2, 3, *half), BF16)] * 4,
                 pltpu.VMEM((2, 2, 3, *half), BF16),
                 pltpu.VMEM((2, 3, *half), BF16),
                 pltpu.VMEM((spare, 2, 2, 3, *half), BF16),
@@ -973,18 +1045,34 @@
                 dma(64), dma(64), dma(16 + spare), dma(16 + spare),
             ],
             compiler_params=params(48, 2),
-        )(keep_a, keep_b, recv_a, recv_b, grads, part, gz1, sums)
-
-        full = g_attn.astype(F32)
+        )(keep_a, keep_b, recv_a, recv_b, zr, grads, part, gz1, sums)
+
+        g_qkv, g_out, g_gate_up, g_down = pl.pallas_call(
+            widen_kernel,
+            name="widen",
+            grid=(3,),
+            out_shape=(
+                shape(576, 768, dtype=F32), shape(192, 768, dtype=F32), shape(768, 2, 768, dtype=F32),
+                shape(768, 768, dtype=F32),
+            ),
+            in_specs=[
+                pl.BlockSpec((192, 768), lambda i: (i, 0)),
+                pl.BlockSpec((64, 768), lambda i: (9 + i, 0)),
+                pl.BlockSpec((2, 256, 768), lambda i: (0, i, 0)),
+                pl.BlockSpec((1, 768, 256), lambda i: (2, 0, i)),
+            ],
+            out_specs=(
+                pl.BlockSpec((192, 768), lambda i: (i, 0)),
+                pl.BlockSpec((64, 768), lambda i: (i, 0)),
+                pl.BlockSpec((256, 2, 768), lambda i: (i, 0, 0)),
+                pl.BlockSpec((256, 768), lambda i: (i, 0)),
+            ),
+            compiler_params=params(32),
+            cost_estimate=pl.CostEstimate(flops=0, bytes_accessed=16_000_000, transcendentals=0),
+        )(g_attn, g_attn, g_ff, g_ff)
         return (
-            output,
-            g_tok[None],
-            full[:576].reshape(3, 192, 768).transpose(2, 0, 1),
-            full[576:],
-            g_ff[:2].transpose(1, 0, 2).astype(F32),
-            g_ff[2].T.astype(F32),
-            sums[0:2],
-            sums[2:4],
+            output, g_tok[None], g_qkv.reshape(3, 192, 768).transpose(2, 0, 1), g_out, g_gate_up, g_down,
+            sums[0:2], sums[2:4],
         )
 
     placed = (

time: 406 us -> 357 us (0.88)
  Pallas kernels: 358 us -> 318 us
  local copies, waits for them, and re-layouts: 30.6 us -> 24 us
  other arithmetic: 8.07 us -> 2.76 us
    pallas_call x1, Pallas kernels: 122 us -> 81.7 us  [on_device(): pl.pallas_call(functools.partial(finish_kernel, extra), name='finish', ou...]
    pallas_call x1, Pallas kernels: 99.8 us -> 91 us  [on_device(): pl.pallas_call(feed_forward_kernel, name='feed_forward', out_shape=(shape...]
    pallas_call x1, Pallas kernels: 68.1 us -> 60 us  [on_device(): pl.pallas_call(start_kernel, name='start', out_shape=(shape(4, 512, 768),...]
    pallas_call x1, Pallas kernels: 34.5 us -> 41.6 us  [on_device(): pl.pallas_call(attend_backward_kernel, name='attend_backward', out_shape=...]
    pallas_call x1, Pallas kernels: 32.8 us -> 39.9 us  [on_device(): pl.pallas_call(attend_forward_kernel, name='attend_forward', out_shape=(s...]
    unnamed x51 -> x47, local copies, waits for them, and re-layouts: 26.1 us -> 19.9 us
  transfers between devices with their start and end apart: 6 -> 8, of which waited for: 0 -> 1; matrix products, arithmetic and copies ran while one was open for 2% -> 1% of each run, Pallas kernels for 34% -> 23%
where the time goes in v4:
time: 357 us; the launch traced here: 355 us
  Pallas kernels  318 us (89%)
  local copies, waits for them, and re-layouts  24 us (7%)
  starting transfers between devices  7.35 us (2%)
    pallas_call x1, Pallas kernels, on_device(): pl.pallas_call(feed_forward_kernel, name='feed_forward', out_shape=(shape...  91 us
    pallas_call x1, Pallas kernels, on_device(): pl.pallas_call(functools.partial(finish_kernel, extra), name='finish', ou...  81.7 us
    pallas_call x1, Pallas kernels, on_device(): pl.pallas_call(start_kernel, name='start', out_shape=(shape(4, 512, 768),...  60 us
    pallas_call x1, Pallas kernels, on_device(): pl.pallas_call(attend_backward_kernel, name='attend_backward', out_shape=...  41.6 us
    pallas_call x1, Pallas kernels, on_device(): pl.pallas_call(attend_forward_kernel, name='attend_forward', out_shape=(s...  39.9 us
    unnamed x47, local copies, waits for them, and re-layouts  19.9 us
  transfers between devices with their start and end apart: 8, of which 1 were waited for; matrix products, arithmetic and copies ran while one was open for 1% of the time, Pallas kernels for 23%

profile of v4, /device:TPU:0, one launch (start us, length us, event | category | flops | bytes accessed | tf_op | source)
XLA Modules:
  0.0 354.6 jit_solution(4151470384196094265)
XLA Ops:
  0.6 0.0 copy-start
  0.6 0.0 copy-start.21
  0.7 1.2 copy-done
  1.9 1.6 constant_dynamic-slice_fusion
  3.6 0.0 copy-done.21
  3.6 0.0 copy-done.19
  3.6 0.0 copy-start.5
  3.6 0.1 pad_maximum_fusion.wo.own
  3.7 0.1 pad_maximum_fusion.1.fb
  3.8 1.0 copy-done.5
  4.7 60.0 %start.1 = (bf16[4,512,768]{2,1,0:T(8,128)(2,1)S(1)}, bf16[768,768]{1,0:T(8,128)(2,1)S(1)}, bf16[3,768,768]{2,1,0:T(8,128)(2,1)S(1)}, bf16[2,3,96,768]{3,2,1,0:T(8,128)(2,1)}) custom-call(bf16[512,768]{1,0:T(8,128)(2,1)S(1)} %bitcast.20, bf16[768,768]{1,0:T(8,128)(2,1)S(1)} %pad_maximum_fusion.wo.own, bf16[3,96,768]{2,1,0:T(8,128)(2,1)S(1)} %pad_maximum_fusion.1.fb), custom_call_target="tpu_custom_call" | custom-call | tf_op jit(solution)/shard_map/start/pallas_call | solution.py:909
  64.7 0.0 copy-start.7
  64.7 1.8 copy-done.7
  66.5 1.6 copy-done.8
  68.1 1.0 copy-done.9
  69.2 1.8 slice_bitcast_fusion
  71.0 1.5 collective-permute-start.2
  72.5 1.5 collective-permute-start.1
  74.0 0.0 collective-permute-start.3
  74.0 0.0 copy-done.22
  74.0 0.0 collective-permute-start
  74.0 1.1 collective-permute-done
  75.2 0.1 convert_reduce_fusion
  75.3 0.1 select_reduce_fusion.2
  75.4 0.1 select_reduce_fusion.1
  75.6 0.2 slice_reduce_fusion
  75.8 1.0 multiply_sine_fusion
  76.8 0.1 pad_add_fusion.sc
  76.8 1.3 copy-done.10
  78.1 39.9 %attend_forward.1 = (bf16[768,768]{1,0:T(8,128)(2,1)S(1)}, bf16[3,128,2048]{2,1,0:T(8,128)(2,1)}, bf16[3,2048,128]{2,1,0:T(8,128)(2,1)}, bf16[192,2048]{1,0:T(8,...) custom-call(s32[24]{0:T(128)S(1)} %pad_add_fusion.sc, ...), custom_call_target="tpu_custom_call" | custom-call | flops 20000000000 | bytes 24000000 | tf_op jit(solution)/shard_map/attend_forward/pallas_call | solution.py:941
  118.1 0.0 copy-start.12
  118.1 1.0 copy-done.12
  119.1 0.9 copy-done.14
  120.0 0.9 copy-done.16
  120.8 0.0 collective-permute-done.2.zy
  120.8 0.0 collective-permute-done.1.zx
  120.8 0.0 collective-permute-done.3.zc
  120.9 91.0 %feed_forward.1 = (bf16[512,768]{1,0:T(8,128)(2,1)}, f32[512,768]{1,0:T(8,128)}, bf16[4,512,768]{2,1,0:T(8,128)(2,1)}, f32[8,768]{1,0:T(8,128)}, bf16[2,2,3,48,7...) custom-call(bf16[4,512,768]{2,1,0:T(8,128)(2,1)} %copy-done.8, ...), custom_call_target="tpu_custom_call" | custom-call | flops 22000001024 | bytes 36000000 | tf_op jit(solution)/shard_map/feed_forward/pallas_call | solution.py:960
  211.8 0.7 collective-permute-start.4
  212.6 1.6 collective-permute-start.5
  214.1 0.5 collective-permute-start.6
  214.7 1.5 collective-permute-start.7
  216.2 1.4 copy-done.11
  217.6 1.3 copy-done.13
  218.9 1.1 copy-done.15
  220.0 1.1 copy-done.17
  221.1 41.6 %attend_backward.1 = (bf16[768,768]{1,0:T(8,128)(2,1)S(1)}, bf16[4,512,768]{2,1,0:T(8,128)(2,1)}) custom-call(s32[24]{0:T(128)S(1)} %pad_add_fusion.sc, bf16[4,512,768]{2,1,0:T(8,128)(2,1)} %get-tuple-element.50.gb, bf16[4,512,768]{2,1,0:T(8,128)(2,1)} %copy-done.8, bf16[768,768]{1,0:T(8,128)(2,1)S(1)} %copy-done.13, bf16[3,128,2048]{2,1,0:T(8,128)(2,1)S(1)} %copy-done.11, ...), custom_call_target="tpu_custom_call" | custom-call | flops 40000000000 | bytes 24000000 | tf_op jit(solution)/shard_map/attend_backward/pallas_call | solution.py:1002
  262.8 0.0 copy-start.2
  262.8 0.0 copy-start.3
  262.8 0.0 copy-start.4
  262.8 0.0 copy-start.6
  262.8 0.0 collective-permute-done.4
  262.9 1.0 select_bitcast_fusion
  263.9 0.0 collective-permute-done.5.recv_a
  263.9 0.0 collective-permute-done.6.recv_b
  263.9 0.0 collective-permute-done.7.zr
  263.9 0.2 copy-done.2
  264.1 0.5 copy-done.3
  264.6 0.3 copy-done.4
  265.0 81.7 %finish.1 = (bf16[3,768,768]{2,1,0:T(8,128)(2,1)}, bf16[768,768]{1,0:T(8,128)(2,1)S(1)}, f32[512,768]{1,0:T(8,128)}, f32[8,768]{1,0:T(8,128)S(1)}) custom-call(bf16[2,2,3,48,768]{4,3,2,1,0:T(8,128)(2,1)S(1)} %copy-done.3, bf16[2,2,3,48,768]{4,3,2,1,0:T(8,128)(2,1)S(1)} %copy-done.4, bf16[2,2,3,48,768]{4,3,2,1,0:T(8,128)(2,1)S(1)} %collective-permute-done.5.recv_a, ...), custom_call_target="tpu_custom_call" | custom-call | tf_op jit(solution)/shard_map/finish/pallas_call | solution.py:1022
  346.6 0.6 fusion.2
  347.2 2.0 copy-done.1
  349.2 4.1 %widen.1 = (f32[576,768]{1,0:T(8,128)}, f32[192,768]{1,0:T(8,128)}, f32[768,2,768]{2,1,0:T(2,128)}, f32[768,768]{1,0:T(8,128)}) custom-call(bf16[768,768]{1,0:T(8,128)(2,1)S(1)} %get-tuple-element.63.attn.out_rows, bf16[768,768]{1,0:T(8,128)(2,1)S(1)} %get-tuple-element.63.attn.out_rows, bf16[3,768,768]{2,1,0:T(8,128)(2,1)S(1)} %copy-done.1, ...), custom_call_target="tpu_custom_call" | custom-call | bytes 16000000 | tf_op jit(solution)/shard_map/widen/pallas_call | solution.py:1050
  353.3 1.1 copy.27
  (26 shorter events, 0.1 us)
Async XLA Ops:
  0.6 1.3 copy-start
  0.6 2.9 copy-start.21
  1.9 1.7 copy-start.19
  3.6 1.1 copy-start.5
  4.7 69.2 %copy-start.22 = (s32[1,2048]{1,0:T(1,128)S(1)}, s32[1,2048]{1,0:T(1,128)}, u32[]{:S(2)}) copy-start(s32[1,2048]{1,0:T(1,128)} %param.10) | copy-start | bytes 24580
  64.7 1.8 copy-start.7
  66.5 1.6 copy-start.8
  68.1 1.0 copy-start.9
  71.0 49.9 %collective-permute-start.2 = (bf16[3,96,768]{2,1,0:T(8,128)(2,1)}, bf16[3,96,768]{2,1,0:T(8,128)(2,1)}, u32[]{:S(2)}, u32[]{:S(2)}) collective-permute-start(bf16[3,96,768]{2,1,0:T(8,128)(2,1)} %slice_bitcast_fusion), channel_id=1, source_target_pairs={{0,16},{4,20},{8,24},{12,28},{16,0},{20,4},{24,8},{28,12},{1,17},{... | collective-permute-start | bytes 1327112 | tf_op jit(solution)/shard_map/ppermute | solution.py:878
  72.5 48.4 %collective-permute-start.1 = (bf16[3,96,768]{2,1,0:T(8,128)(2,1)}, bf16[3,96,768]{2,1,0:T(8,128)(2,1)}, u32[]{:S(2)}, u32[]{:S(2)}) collective-permute-start(bf16[3,96,768]{2,1,0:T(8,128)(2,1)} %slice_bitcast_fusion), channel_id=1, source_target_pairs={{0,8},{4,12},{8,0},{12,4},{16,24},{20,28},{24,16},{28,20},{1,9},{5... | collective-permute-start | bytes 1327112 | tf_op jit(solution)/shard_map/ppermute | solution.py:878
  74.0 46.9 %collective-permute-start.3 = (bf16[2,3,96,768]{3,2,1,0:T(8,128)(2,1)}, bf16[2,3,96,768]{3,2,1,0:T(8,128)(2,1)}, u32[]{:S(2)}, u32[]{:S(2)}) collective-permute-start(bf16[2,3,96,768]{3,2,1,0:T(8,128)(2,1)} %get-tuple-element.43.zb), channel_id=1, source_target_pairs={{0,1},{1,0},{2,3},{3,2},{4,5},{5,4},{6,7},{7,6},{8,9},{9,8},{10,11... | collective-permute-start | bytes 2654216 | tf_op jit(solution)/shard_map/ppermute | solution.py:938
  74.0 1.2 collective-permute-start
  76.8 1.3 copy-start.10
  118.1 1.0 copy-start.12
  119.1 0.9 copy-start.14
  120.0 0.9 copy-start.16
  211.8 51.0 %collective-permute-start.4 = (bf16[512,768]{1,0:T(8,128)(2,1)}, bf16[512,768]{1,0:T(8,128)(2,1)S(1)}, u32[]{:S(2)}, u32[]{:S(2)}) collective-permute-start(bf16[512,768]{1,0:T(8,128)(2,1)} %get-tuple-element.44), channel_id=1, source_target_pairs={{2,4},{3,5},{4,2},{5,3},{10,12},{11,13},{12,10},{13,11},{18,20},{1... | collective-permute-start | bytes 2359304 | tf_op jit(solution)/shard_map/ppermute | solution.py:883
  212.6 51.3 %collective-permute-start.5 = (bf16[2,2,3,48,768]{4,3,2,1,0:T(8,128)(2,1)}, bf16[2,2,3,48,768]{4,3,2,1,0:T(8,128)(2,1)S(1)}, u32[]{:S(2)}, u32[]{:S(2)}) collective-permute-start(bf16[2,2,3,48,768]{4,3,2,1,0:T(8,128)(2,1)} %get-tuple-element.47), channel_id=1, source_target_pairs={{0,16},{4,20},{8,24},{12,28},{16,0},{20,4},{24,8},{28,12},{1,17},{... | collective-permute-start | bytes 2654216 | tf_op jit(solution)/shard_map/ppermute | solution.py:878
  214.1 49.7 %collective-permute-start.6 = (bf16[2,2,3,48,768]{4,3,2,1,0:T(8,128)(2,1)}, bf16[2,2,3,48,768]{4,3,2,1,0:T(8,128)(2,1)S(1)}, u32[]{:S(2)}, u32[]{:S(2)}) collective-permute-start(bf16[2,2,3,48,768]{4,3,2,1,0:T(8,128)(2,1)} %get-tuple-element.48), channel_id=1, source_target_pairs={{0,8},{4,12},{8,0},{12,4},{16,24},{20,28},{24,16},{28,20},{1,9},{5... | collective-permute-start | bytes 2654216 | tf_op jit(solution)/shard_map/ppermute | solution.py:878
  214.7 49.2 %collective-permute-start.7 = (bf16[2,2,3,48,768]{4,3,2,1,0:T(8,128)(2,1)}, bf16[2,2,3,48,768]{4,3,2,1,0:T(8,128)(2,1)S(1)}, u32[]{:S(2)}, u32[]{:S(2)}) collective-permute-start(bf16[2,2,3,48,768]{4,3,2,1,0:T(8,128)(2,1)} %get-tuple-element.49), channel_id=1, source_target_pairs={{0,1},{1,0},{2,3},{3,2},{4,5},{5,4},{6,7},{7,6},{8,9},{9,8},{10,11... | collective-permute-start | bytes 2654216 | tf_op jit(solution)/shard_map/ppermute | solution.py:999
  216.2 1.4 copy-start.11
  217.6 1.3 copy-start.13
  218.9 1.1 copy-start.15
  220.0 1.1 copy-start.17
  221.1 41.7 %copy-start.20 = (bf16[512,768]{1,0:T(8,128)(2,1)S(1)}, bf16[512,768]{1,0:T(8,128)(2,1)}, u32[]{:S(2)}) copy-start(bf16[512,768]{1,0:T(8,128)(2,1)} %get-tuple-element.44) | copy-start | bytes 2359300
  262.8 1.3 copy-start.2
  262.8 1.8 copy-start.3
  262.8 2.1 copy-start.4
  262.8 2.1 copy-start.6
  347.2 2.0 copy-start.1
  349.2 4.1 %copy-start.18 = (f32[512,768]{1,0:T(8,128)S(1)}, f32[512,768]{1,0:T(8,128)}, u32[]{:S(2)}) copy-start(f32[512,768]{1,0:T(8,128)} %get-tuple-element.62) | copy-start | bytes 4718596

commit v5 on v4

--- a/solution.py
+++ b/solution.py
@@ -169,7 +169,8 @@
 
     def copy(kind, k, ch, src, to):
         return pltpu.make_async_remote_copy(
-            src_ref=src, dst_ref=tok.at[line(k), part(ch)], send_sem=token_send.at[kind, k, ch],
+            src_ref=src, dst_ref=tok.at[line(k), part(ch)],
+            send_sem=token_send.at[kind, k, ch],
             recv_sem=token_recv.at[k, ch], device_id=to, device_id_type=MESH,
         )
 
@@ -190,7 +191,7 @@
 
     links = Links(send, recv)
     attn_z = links.start(view_2d(wo)(me.place, 0, 96), view_2d(wx)(me.place, 0, 96), me.z2)
-    ff_z = links.start(fb, zb.at[1], me.z2)
+    ff_z = links.make(fb, zb.at[1], me.z2)
     ff0 = Spread(me, links, view_3d(wf0), fb)
     here = [
         pltpu.make_async_copy(fb, view_3d(wf0)(me.place, 0, 96), local.at[0]),
@@ -228,6 +229,15 @@
     attn.second()
     ff0.third()
     forward(2)
+
+    for k in (2, 3):
+
+        @pl.when(away == k)
+        def _(k=k):
+            copy(0, k, 2, own(2), near).wait_send()
+
+    ff_z.start()
+    links.started.append(ff_z)
     attn.third()
     forward(3)
 
@@ -251,7 +261,8 @@
         @pl.when(away == k)
         def _(k=k, to=to):
             for ch in range(CHUNKS):
-                copy(0, k, ch, own(ch), to).wait_send()
+                if k < 2 or ch != 2:
+                    copy(0, k, ch, own(ch), to).wait_send()
                 if k == 1:
                     for j in (2, 3):
                         copy(0, j, ch, held(j, ch), to).wait_send()
@@ -260,8 +271,44 @@
                         copy(1, j, ch, own(ch) if j == k else held(j, ch), me.sib).wait_send()
 
 
+FIRST, LAST = 256, 512
+
+
+def list_pairs(sc, pairs):
+    idle = 8 * 16 + 8
+    pairs[0] = idle
+
+    def of_query(i, n):
+        lo, hi = sc[8 + i], sc[16 + i]
+
+        def of_key(j, n):
+            first = jnp.where(j == lo, FIRST, 0)
+            last = jnp.where(j == hi - 1, LAST, 0)
+            pairs[n] = i * 16 + j + first + last
+            return n + 1
+
+        return lax.fori_loop(lo, hi, of_key, n)
+
+    n = lax.fori_loop(0, 2048 // BLK, of_query, 1)
+    for more in range(3):
+        pairs[n + more] = idle
+    return n - 1
+
+
+def split_pair(code):
+    return (code // 16) % 16, code % 16
+
+
+def columns(block):
+    return pl.ds(pl.multiple_of(block * BLK, BLK), BLK)
+
+
+def real(block):
+    return jnp.where(block == 8, 0, block)
+
+
 def attend_forward_kernel(
-    sc, tok, cos, sin, seg, own, other, w, qa, ka, kt, vn, ot, logsum, part, va, mx, acc, sem
+    sc, tok, cos, sin, seg, own, other, w, qa, ka, kt, vn, ot, logsum, part, va, mx, acc, s0, s1, p0, p1, al0, al1, pairs, sem
 ):
     heads = 3
     width = heads * HEAD_DIM
@@ -303,37 +350,60 @@
 
     lax.fori_loop(0, 4, project, 0)
 
-    def query_block(i, _):
-        at = pl.ds(pl.multiple_of(i * BLK, BLK), BLK)
+    count = list_pairs(sc, pairs)
+
+    def score(t, s):
+        i, j = split_pair(pairs[t])
+        at, here = columns(real(i)), columns(real(j))
         for h in range(heads):
-            mx[h] = jnp.full((1, BLK), -3e38, F32)
-            acc[h] = jnp.zeros((80, BLK), F32)
-
-        def key_block(j, _):
-            here = pl.ds(pl.multiple_of(j * BLK, BLK), BLK)
+            s[h] = nn(ka[h, here, :], qa[h, :, at])
+
+    def weigh(t, s, p, al):
+        fresh = pairs[t] & FIRST
+        for h in range(heads):
+            scores = s[h]
+            before = jnp.where(fresh > 0, -3e38, mx[h])
+            largest = jnp.maximum(before, jnp.max(scores, axis=0, keepdims=True))
+            p[h] = jnp.exp(scores - largest).astype(BF16)
+            al[h] = jnp.exp(before - largest)
+            mx[h] = largest
+
+    def gather(t, p, al):
+        code = pairs[t]
+        i, j = split_pair(code)
+        here = columns(real(j))
+        for h in range(heads):
+            acc[h] = acc[h] * al[h] + nn(va[h, :, here], p[h])
+
+        @pl.when((code & LAST) > 0)
+        def _():
+            at = columns(i)
             for h in range(heads):
-                scores = nn(ka[h, here, :], qa[h, :, at])
-                before = mx[h]
-                largest = jnp.maximum(before, jnp.max(scores, axis=0, keepdims=True))
-                weights = jnp.exp(scores - largest).astype(BF16)
-                acc[h] = acc[h] * jnp.exp(before - largest) + nn(va[h, :, here], weights)
-                mx[h] = largest
-            return 0
-
-        lax.fori_loop(sc[8 + i], sc[16 + i], key_block, 0)
-        for h in range(heads):
-            total = acc[h, 64:65, :]
-            ot[h * HEAD_DIM : (h + 1) * HEAD_DIM, at] = (acc[h, :64, :] / total).astype(BF16)
-            logsum[pl.ds(h, 1), at] = mx[h] + jnp.log(total)
+                total = acc[h, 64:65, :]
+                ot[h * HEAD_DIM : (h + 1) * HEAD_DIM, at] = (acc[h, :64, :] / total).astype(BF16)
+                logsum[pl.ds(h, 1), at] = mx[h] + jnp.log(total)
+
+    def step(u, _):
+        t = 2 * u + 1
+        gather(t - 1, p1, al1)
+        weigh(t, s0, p0, al0)
+        score(t + 1, s1)
+        gather(t, p0, al0)
+        weigh(t + 1, s1, p1, al1)
+        score(t + 2, s0)
         return 0
 
-    lax.fori_loop(0, 2048 // BLK, query_block, 0)
+    acc[...] = jnp.zeros_like(acc)
+    p1[...] = jnp.zeros_like(p1)
+    al1[...] = jnp.zeros_like(al1)
+    score(1, s0)
+    lax.fori_loop(0, (count + 2) // 2, step, 0)
     for e in range(4):
         part[e] = tn(ot[:, e * 512 : (e + 1) * 512], w[3 * width :]).astype(BF16)
 
 
 def attend_backward_kernel(
-    sc, gb, tok, w, qa, ka, kt, vn, ot, logsum, cos, sin, grads, part, dot_, inner, dq, dk, dv, gp
+    sc, gb, tok, w, qa, ka, kt, vn, ot, logsum, cos, sin, grads, part, dot_, inner, dq, dk, dv, gp, s0, s1, r0, r1, p0, p1, d0, d1, pairs
 ):
     heads = 3
     width = heads * HEAD_DIM
@@ -348,46 +418,59 @@
         return 0
 
     lax.fori_loop(0, 4, begin, 0)
-    dq[...] = jnp.zeros_like(dq)
-
-    def key_block(j, _):
-        here = pl.ds(pl.multiple_of(j * BLK, BLK), BLK)
+    for total in (dq, dk, dv, p1, d1):
+        total[...] = jnp.zeros_like(total)
+    count = list_pairs(sc, pairs)
+
+    def score(t, s, r):
+        i, j = split_pair(pairs[t])
+        at, here = columns(real(i)), columns(real(j))
         for h in range(heads):
-            dk[h] = jnp.zeros((HEAD_DIM, BLK), F32)
-            dv[h] = jnp.zeros((HEAD_DIM, BLK), F32)
-
-        def query_block(i, _):
-            at = pl.ds(pl.multiple_of(i * BLK, BLK), BLK)
-            for h in range(heads):
-                rows = slice(h * HEAD_DIM, (h + 1) * HEAD_DIM)
-                scores = nn(ka[h, here, :], qa[h, :, at])
-                probability = jnp.exp(scores - logsum[pl.ds(h, 1), at])
-                rise = nn(vn[h, here, :], dot_[rows, at])
-                slope = (probability * (rise - inner[pl.ds(h, 1), at])).astype(BF16)
-                dv[h] += nt(dot_[rows, at], probability.astype(BF16))
-                dk[h] += nt(qa[h, :HEAD_DIM, at], slope)
-                dq[rows, at] += nn(kt[rows, here], slope)
-            return 0
-
-        lax.fori_loop(sc[8 + j], sc[16 + j], query_block, 0)
-        c, s = cos[:, here], sin[:, here]
+            rows = slice(h * HEAD_DIM, (h + 1) * HEAD_DIM)
+            s[h] = nn(ka[h, here, :], qa[h, :, at])
+            r[h] = nn(vn[h, here, :], dot_[rows, at])
+
+    def weigh(t, s, r, p, d):
+        at = columns(real(split_pair(pairs[t])[0]))
         for h in range(heads):
-            d1, d2 = dk[h, :32, :], dk[h, 32:, :]
-            r = width + h * HEAD_DIM
-            gp[r : r + 64, here] = jnp.concatenate([d1 * c + d2 * s, d2 * c - d1 * s], axis=0).astype(BF16)
-            r += width
-            gp[r : r + 64, here] = dv[h].astype(BF16)
+            probability = jnp.exp(s[h] - logsum[pl.ds(h, 1), at])
+            p[h] = probability.astype(BF16)
+            d[h] = (probability * (r[h] - inner[pl.ds(h, 1), at])).astype(BF16)
+
+    def gather(t, p, d):
+        i, j = split_pair(pairs[t])
+        at, here = columns(real(i)), columns(real(j))
+        to_query, to_key = columns(i), columns(j)
+        for h in range(heads):
+            rows = slice(h * HEAD_DIM, (h + 1) * HEAD_DIM)
+            dv[rows, to_key] += nt(dot_[rows, at], p[h])
+            dk[rows, to_key] += nt(qa[h, :HEAD_DIM, at], d[h])
+            dq[rows, to_query] += nn(kt[rows, here], d[h])
+
+    def step(u, _):
+        t = 2 * u + 1
+        gather(t - 1, p1, d1)
+        weigh(t, s0, r0, p0, d0)
+        score(t + 1, s1, r1)
+        gather(t, p0, d0)
+        weigh(t + 1, s1, r1, p1, d1)
+        score(t + 2, s0, r0)
         return 0
 
-    lax.fori_loop(0, 2048 // BLK, key_block, 0)
+    score(1, s0, r0)
+    lax.fori_loop(0, (count + 2) // 2, step, 0)
 
     def turn(e, _):
         at = pl.ds(pl.multiple_of(e * 512, 512), 512)
-        c, s = cos[:, at] * 0.125, sin[:, at] * 0.125
+        c, s = cos[:, at], sin[:, at]
         for h in range(heads):
             r = h * HEAD_DIM
-            d1, d2 = dq[r : r + 32, at], dq[r + 32 : r + 64, at]
-            gp[r : r + 64, at] = jnp.concatenate([d1 * c + d2 * s, d2 * c - d1 * s], axis=0).astype(BF16)
+            for first, total, scale in ((0, dq, 0.125), (width, dk, 1.0)):
+                d1_, d2_ = total[r : r + 32, at] * scale, total[r + 32 : r + 64, at] * scale
+                gp[first + r : first + r + 64, at] = jnp.concatenate(
+                    [d1_ * c + d2_ * s, d2_ * c - d1_ * s], axis=0
+                ).astype(BF16)
+        gp[2 * width :, at] = dv[:, at].astype(BF16)
         return 0
 
     lax.fori_loop(0, 4, turn, 0)
@@ -718,24 +801,22 @@
         va[ez, 1] = add(keep_b[ez, me.y], recv_b[ez, me.y], f2b[ez], zr[ez, 1])
 
     plane(1)
+    plane(0)
     zs = []
     for ch in range(CHUNKS):
         cores[0][ch].wait_recv()
         at = rows(ch)
         to_z[at] = add(part[me.slot1, at], from_core[1, at])
         zs.append(links.start(to_z.at[at], from_z.at[at], me.z1))
-    plane(0)
+    small_step()
     planed(1)
     ff_4 = links.start(va.at[1], f4, me.z2)
-    small_step()
     for copy in attn_1:
         copy.wait_recv()
     a_mid[0] = add(ga[half(me.y, 1 - me.x, 0)], a_in[0, 1 - me.x])
     a_mid[1] = add(ga[half(1 - me.y, me.x, 1)], a_in[1, 1 - me.y])
     attn_2 = [links.start(a_mid.at[0], a_out.at[0], me.xn), links.start(a_mid.at[1], a_out.at[1], me.yn)]
-    small_step()
     planed(0)
-    small_step()
     for copy in attn_2:
         copy.wait_recv()
     a_fin[:96] = add(ga[half(me.y, me.x, 0)], a_in[0, me.x], a_out[0])
@@ -756,6 +837,7 @@
     def _():
         attn_over().start()
 
+    small_step()
     small_step()
 
     trades = [
@@ -778,11 +860,6 @@
         @pl.when(me.cross == 1)
         def _(at=at, got=got, ch=ch):
             trade_out[at] = got.astype(BF16)
-            trades[ch].start()
-
-    while len(small) < len(around):
-        small_step()
-    small_step()
 
     mine = quarter(me.y, me.x)
 
@@ -809,6 +886,12 @@
         attn_send(3, mine, me.sib).start()
 
     ff_4.wait_recv()
+
+    @pl.when(me.cross == 1)
+    def _():
+        for ch in range(CHUNKS):
+            trades[ch].start()
+
     total = add(va[0], f4[...])
     for n, bit in enumerate(bits):
         fe[n, 0] = total
@@ -818,6 +901,9 @@
     for h in range(2):
         g_ff[:, pl.ds(pl.multiple_of(me.place * 96 + h * 48, 16), 48)] = total[h]
     spread = Spread(me, links, view_3d(g_ff))
+    while len(small) < len(around):
+        small_step()
+    small_step()
 
     @pl.when(me.cross == 0)
     def _():
@@ -951,6 +1037,10 @@
                 pltpu.VMEM((3, 80, length), BF16),
                 pltpu.VMEM((3, 1, BLK), F32),
                 pltpu.VMEM((3, 80, BLK), F32),
+                *[pltpu.VMEM((3, BLK, BLK), F32)] * 2,
+                *[pltpu.VMEM((3, BLK, BLK), BF16)] * 2,
+                *[pltpu.VMEM((3, 1, BLK), F32)] * 2,
+                pltpu.SMEM((72,), jnp.int32),
                 dma(1),
             ],
             compiler_params=params(48),
@@ -1008,10 +1098,11 @@
             scratch_shapes=[
                 pltpu.VMEM((192, length), BF16),
                 pltpu.VMEM((8, length), F32),
-                pltpu.VMEM((192, length), F32),
-                pltpu.VMEM((3, 64, BLK), F32),
-                pltpu.VMEM((3, 64, BLK), F32),
+                *[pltpu.VMEM((192, length + BLK), F32)] * 3,
                 pltpu.VMEM((576, length), BF16),
+                *[pltpu.VMEM((3, BLK, BLK), F32)] * 4,
+                *[pltpu.VMEM((3, BLK, BLK), BF16)] * 4,
+                pltpu.SMEM((72,), jnp.int32),
             ],
             compiler_params=params(48),
             cost_estimate=pl.CostEstimate(flops=40_000_000_000, bytes_accessed=24_000_000, transcendentals=6_000_000),

time: 357 us -> 334 us (0.936)
  the two profiles are of different devices: /device:TPU:0 before, /device:TPU:25 now
where the time goes in v5:
time: 334 us; the launch traced here: 329 us
  Pallas kernels  289 us (87%)
  local copies, waits for them, and re-layouts  24 us (7%)
  starting transfers between devices  11.5 us (3%)
    pallas_call x1, Pallas kernels, on_device(): pl.pallas_call(feed_forward_kernel, name='feed_forward', out_shape=(shape...  89.9 us
    pallas_call x1, Pallas kernels, on_device(): pl.pallas_call(functools.partial(finish_kernel, extra), name='finish', ou...  81.7 us
    pallas_call x1, Pallas kernels, on_device(): pl.pallas_call(start_kernel, name='start', out_shape=(shape(4, 512, 768),...  53.8 us
    pallas_call x1, Pallas kernels, on_device(): pl.pallas_call(attend_backward_kernel, name='attend_backward', out_shape=...  33.4 us
    pallas_call x1, Pallas kernels, on_device(): pl.pallas_call(attend_forward_kernel, name='attend_forward', out_shape=(s...  25.9 us
    unnamed x47, local copies, waits for them, and re-layouts  19.9 us
    ppermute x5, starting transfers between devices, over(): return lax.ppermute(x, 'dp', [(i, i ^ bit) for i in range(dp)])  10.7 us
  transfers between devices with their start and end apart: 8, of which 1 were waited for; matrix products, arithmetic and copies ran while one was open for 1% of the time, Pallas kernels for 18%

profile of v5, /device:TPU:25, one launch (start us, length us, event | category | flops | bytes accessed | tf_op | source)
XLA Modules:
  0.0 328.9 jit_solution(10737118142470976306)
XLA Ops:
  0.6 0.0 copy-start
  0.6 0.0 copy-start.21
  0.7 1.2 copy-done
  1.9 1.6 constant_dynamic-slice_fusion
  3.6 0.0 copy-done.21
  3.6 0.0 copy-done.19
  3.6 0.0 copy-start.5
  3.6 0.1 pad_maximum_fusion.wo.own
  3.7 0.1 pad_maximum_fusion.1.fb
  3.8 1.0 copy-done.5
  4.7 53.8 %start.1 = (bf16[4,512,768]{2,1,0:T(8,128)(2,1)S(1)}, bf16[768,768]{1,0:T(8,128)(2,1)S(1)}, bf16[3,768,768]{2,1,0:T(8,128)(2,1)S(1)}, bf16[2,3,96,768]{3,2,1,0:T(8,128)(2,1)}) custom-call(bf16[512,768]{1,0:T(8,128)(2,1)S(1)} %bitcast.20, bf16[768,768]{1,0:T(8,128)(2,1)S(1)} %pad_maximum_fusion.wo.own, bf16[3,96,768]{2,1,0:T(8,128)(2,1)S(1)} %pad_maximum_fusion.1.fb), custom_call_target="tpu_custom_call" | custom-call | tf_op jit(solution)/shard_map/start/pallas_call | solution.py:995
  58.5 0.0 copy-start.7
  58.5 1.8 copy-done.7
  60.3 1.6 copy-done.8
  62.0 1.0 copy-done.9
  63.0 1.8 slice_bitcast_fusion
  64.8 1.2 collective-permute-start.2
  66.0 1.2 collective-permute-start.1
  67.2 0.0 collective-permute-start.3
  67.2 0.0 copy-done.22
  67.2 6.7 %collective-permute-start = (s32[1,2048]{1,0:T(1,128)S(1)}, s32[1,2048]{1,0:T(1,128)S(1)}, u32[]{:S(2)}, u32[]{:S(2)}) collective-permute-start(s32[1,2048]{1,0:T(1,128)S(1)} %copy-done.22), channel_id=1, source_target_pairs={{0,4},{4,0},{8,12},{12,8},{16,20},{20,16},{24,28},{28,24},{1,5},{5... | collective-permute-start | bytes 24584 | tf_op jit(solution)/shard_map/ppermute | solution.py:964
  73.9 0.8 collective-permute-done
  74.8 0.1 convert_reduce_fusion
  74.9 0.1 select_reduce_fusion.2
  75.0 0.1 select_reduce_fusion.1
  75.2 0.2 slice_reduce_fusion
  75.4 1.0 multiply_sine_fusion
  76.4 0.1 pad_add_fusion.sc
  76.5 1.3 copy-done.10
  77.7 25.9 %attend_forward.1 = (bf16[768,768]{1,0:T(8,128)(2,1)S(1)}, bf16[3,128,2048]{2,1,0:T(8,128)(2,1)}, bf16[3,2048,128]{2,1,0:T(8,128)(2,1)}, bf16[192,2048]{1,0:T(8,...) custom-call(s32[24]{0:T(128)S(1)} %pad_add_fusion.sc, ...), custom_call_target="tpu_custom_call" | custom-call | flops 20000000000 | bytes 24000000 | tf_op jit(solution)/shard_map/attend_forward/pallas_call | solution.py:1027
  103.6 0.0 copy-start.12
  103.6 1.0 copy-done.12
  104.6 0.9 copy-done.14
  105.5 0.9 copy-done.16
  106.4 0.0 collective-permute-done.2.zy
  106.4 0.0 collective-permute-done.1.zx
  106.4 0.0 collective-permute-done.3.zc
  106.4 89.9 %feed_forward.1 = (bf16[512,768]{1,0:T(8,128)(2,1)}, f32[512,768]{1,0:T(8,128)}, bf16[4,512,768]{2,1,0:T(8,128)(2,1)}, f32[8,768]{1,0:T(8,128)}, bf16[2,2,3,48,7...) custom-call(bf16[4,512,768]{2,1,0:T(8,128)(2,1)} %copy-done.8, ...), custom_call_target="tpu_custom_call" | custom-call | flops 22000001024 | bytes 36000000 | tf_op jit(solution)/shard_map/feed_forward/pallas_call | solution.py:1050
  196.3 0.7 collective-permute-start.4
  197.0 0.9 collective-permute-start.5
  198.0 0.6 collective-permute-start.6
  198.6 0.1 collective-permute-start.7
  198.7 1.4 copy-done.11
  200.1 1.3 copy-done.13
  201.4 1.1 copy-done.15
  202.5 1.1 copy-done.17
  203.6 33.4 %attend_backward.1 = (bf16[768,768]{1,0:T(8,128)(2,1)S(1)}, bf16[4,512,768]{2,1,0:T(8,128)(2,1)}) custom-call(s32[24]{0:T(128)S(1)} %pad_add_fusion.sc, bf16[4,512,768]{2,1,0:T(8,128)(2,1)} %get-tuple-element.50.gb, bf16[4,512,768]{2,1,0:T(8,128)(2,1)} %copy-done.8, bf16[768,768]{1,0:T(8,128)(2,1)S(1)} %copy-done.13, bf16[3,128,2048]{2,1,0:T(8,128)(2,1)S(1)} %copy-done.11, ...), custom_call_target="tpu_custom_call" | custom-call | flops 40000000000 | bytes 24000000 | tf_op jit(solution)/shard_map/attend_backward/pallas_call | solution.py:1092
  237.0 0.0 copy-start.2
  237.0 0.0 copy-start.3
  237.0 0.0 collective-permute-done.4
  237.1 1.0 select_bitcast_fusion
  238.1 0.0 collective-permute-done.5.recv_a
  238.1 0.0 collective-permute-done.6.recv_b
  238.1 0.0 collective-permute-done.7.zr
  238.1 0.2 copy-done.2
  238.3 0.5 copy-done.3
  238.8 0.3 copy-done.4
  239.2 0.0 copy-done.6
  239.2 81.7 %finish.1 = (bf16[3,768,768]{2,1,0:T(8,128)(2,1)}, bf16[768,768]{1,0:T(8,128)(2,1)S(1)}, f32[512,768]{1,0:T(8,128)}, f32[8,768]{1,0:T(8,128)S(1)}) custom-call(bf16[2,2,3,48,768]{4,3,2,1,0:T(8,128)(2,1)S(1)} %copy-done.3, bf16[2,2,3,48,768]{4,3,2,1,0:T(8,128)(2,1)S(1)} %copy-done.4, bf16[2,2,3,48,768]{4,3,2,1,0:T(8,128)(2,1)S(1)} %collective-permute-done.5.recv_a, ...), custom_call_target="tpu_custom_call" | custom-call | tf_op jit(solution)/shard_map/finish/pallas_call | solution.py:1113
  320.9 0.6 fusion.2
  321.5 2.0 copy-done.1
  323.5 4.1 %widen.1 = (f32[576,768]{1,0:T(8,128)}, f32[192,768]{1,0:T(8,128)}, f32[768,2,768]{2,1,0:T(2,128)}, f32[768,768]{1,0:T(8,128)}) custom-call(bf16[768,768]{1,0:T(8,128)(2,1)S(1)} %get-tuple-element.63.attn.out_rows, bf16[768,768]{1,0:T(8,128)(2,1)S(1)} %get-tuple-element.63.attn.out_rows, bf16[3,768,768]{2,1,0:T(8,128)(2,1)S(1)} %copy-done.1, ...), custom_call_target="tpu_custom_call" | custom-call | bytes 16000000 | tf_op jit(solution)/shard_map/widen/pallas_call | solution.py:1141
  327.5 0.0 copy-done.18
  327.5 1.1 copy.27
  (26 shorter events, 0.1 us)
Async XLA Ops:
  0.6 1.3 copy-start
  0.6 2.9 copy-start.21
  1.9 1.7 copy-start.19
  3.6 1.1 copy-start.5
  4.7 62.5 %copy-start.22 = (s32[1,2048]{1,0:T(1,128)S(1)}, s32[1,2048]{1,0:T(1,128)}, u32[]{:S(2)}) copy-start(s32[1,2048]{1,0:T(1,128)} %param.10) | copy-start | bytes 24580
  58.5 1.8 copy-start.7
  60.3 1.6 copy-start.8
  62.0 1.0 copy-start.9
  64.8 41.6 %collective-permute-start.2 = (bf16[3,96,768]{2,1,0:T(8,128)(2,1)}, bf16[3,96,768]{2,1,0:T(8,128)(2,1)}, u32[]{:S(2)}, u32[]{:S(2)}) collective-permute-start(bf16[3,96,768]{2,1,0:T(8,128)(2,1)} %slice_bitcast_fusion), channel_id=1, source_target_pairs={{0,16},{4,20},{8,24},{12,28},{16,0},{20,4},{24,8},{28,12},{1,17},{... | collective-permute-start | bytes 1327112 | tf_op jit(solution)/shard_map/ppermute | solution.py:964
  66.0 40.4 %collective-permute-start.1 = (bf16[3,96,768]{2,1,0:T(8,128)(2,1)}, bf16[3,96,768]{2,1,0:T(8,128)(2,1)}, u32[]{:S(2)}, u32[]{:S(2)}) collective-permute-start(bf16[3,96,768]{2,1,0:T(8,128)(2,1)} %slice_bitcast_fusion), channel_id=1, source_target_pairs={{0,8},{4,12},{8,0},{12,4},{16,24},{20,28},{24,16},{28,20},{1,9},{5... | collective-permute-start | bytes 1327112 | tf_op jit(solution)/shard_map/ppermute | solution.py:964
  67.2 39.2 %collective-permute-start.3 = (bf16[2,3,96,768]{3,2,1,0:T(8,128)(2,1)}, bf16[2,3,96,768]{3,2,1,0:T(8,128)(2,1)}, u32[]{:S(2)}, u32[]{:S(2)}) collective-permute-start(bf16[2,3,96,768]{3,2,1,0:T(8,128)(2,1)} %get-tuple-element.43.zb), channel_id=1, source_target_pairs={{0,1},{1,0},{2,3},{3,2},{4,5},{5,4},{6,7},{7,6},{8,9},{9,8},{10,11... | collective-permute-start | bytes 2654216 | tf_op jit(solution)/shard_map/ppermute | solution.py:1024
  67.2 7.5 %collective-permute-start = (s32[1,2048]{1,0:T(1,128)S(1)}, s32[1,2048]{1,0:T(1,128)S(1)}, u32[]{:S(2)}, u32[]{:S(2)}) collective-permute-start(s32[1,2048]{1,0:T(1,128)S(1)} %copy-done.22), channel_id=1, source_target_pairs={{0,4},{4,0},{8,12},{12,8},{16,20},{20,16},{24,28},{28,24},{1,5},{5... | collective-permute-start | bytes 24584 | tf_op jit(solution)/shard_map/ppermute | solution.py:964
  76.5 1.3 copy-start.10
  103.6 1.0 copy-start.12
  104.6 0.9 copy-start.14
  105.5 0.9 copy-start.16
  196.3 40.7 %collective-permute-start.4 = (bf16[512,768]{1,0:T(8,128)(2,1)}, bf16[512,768]{1,0:T(8,128)(2,1)S(1)}, u32[]{:S(2)}, u32[]{:S(2)}) collective-permute-start(bf16[512,768]{1,0:T(8,128)(2,1)} %get-tuple-element.44), channel_id=1, source_target_pairs={{2,4},{3,5},{4,2},{5,3},{10,12},{11,13},{12,10},{13,11},{18,20},{1... | collective-permute-start | bytes 2359304 | tf_op jit(solution)/shard_map/ppermute | solution.py:969
  197.0 41.0 %collective-permute-start.5 = (bf16[2,2,3,48,768]{4,3,2,1,0:T(8,128)(2,1)}, bf16[2,2,3,48,768]{4,3,2,1,0:T(8,128)(2,1)S(1)}, u32[]{:S(2)}, u32[]{:S(2)}) collective-permute-start(bf16[2,2,3,48,768]{4,3,2,1,0:T(8,128)(2,1)} %get-tuple-element.47), channel_id=1, source_target_pairs={{0,16},{4,20},{8,24},{12,28},{16,0},{20,4},{24,8},{28,12},{1,17},{... | collective-permute-start | bytes 2654216 | tf_op jit(solution)/shard_map/ppermute | solution.py:964
  198.0 40.1 %collective-permute-start.6 = (bf16[2,2,3,48,768]{4,3,2,1,0:T(8,128)(2,1)}, bf16[2,2,3,48,768]{4,3,2,1,0:T(8,128)(2,1)S(1)}, u32[]{:S(2)}, u32[]{:S(2)}) collective-permute-start(bf16[2,2,3,48,768]{4,3,2,1,0:T(8,128)(2,1)} %get-tuple-element.48), channel_id=1, source_target_pairs={{0,8},{4,12},{8,0},{12,4},{16,24},{20,28},{24,16},{28,20},{1,9},{5... | collective-permute-start | bytes 2654216 | tf_op jit(solution)/shard_map/ppermute | solution.py:964
  198.6 39.4 %collective-permute-start.7 = (bf16[2,2,3,48,768]{4,3,2,1,0:T(8,128)(2,1)}, bf16[2,2,3,48,768]{4,3,2,1,0:T(8,128)(2,1)S(1)}, u32[]{:S(2)}, u32[]{:S(2)}) collective-permute-start(bf16[2,2,3,48,768]{4,3,2,1,0:T(8,128)(2,1)} %get-tuple-element.49), channel_id=1, source_target_pairs={{0,1},{1,0},{2,3},{3,2},{4,5},{5,4},{6,7},{7,6},{8,9},{9,8},{10,11... | collective-permute-start | bytes 2654216 | tf_op jit(solution)/shard_map/ppermute | solution.py:1089
  198.7 1.4 copy-start.11
  200.1 1.3 copy-start.13
  201.4 1.1 copy-start.15
  202.5 1.1 copy-start.17
  203.6 33.4 %copy-start.20 = (bf16[512,768]{1,0:T(8,128)(2,1)S(1)}, bf16[512,768]{1,0:T(8,128)(2,1)}, u32[]{:S(2)}) copy-start(bf16[512,768]{1,0:T(8,128)(2,1)} %get-tuple-element.44) | copy-start | bytes 2359300
  237.0 1.3 copy-start.2
  237.0 1.8 copy-start.3
  237.0 2.1 copy-start.4
  237.0 2.1 copy-start.6
  321.5 2.0 copy-start.1
  323.5 4.1 %copy-start.18 = (f32[512,768]{1,0:T(8,128)S(1)}, f32[512,768]{1,0:T(8,128)}, u32[]{:S(2)}) copy-start(f32[512,768]{1,0:T(8,128)} %get-tuple-element.62) | copy-start | bytes 4718596

commit v6 on v5

--- a/solution.py
+++ b/solution.py
@@ -3,6 +3,7 @@
 
 import jax
 import jax.numpy as jnp
+import numpy as np
 from jax import lax
 from jax.experimental import pallas as pl
 from jax.experimental.pallas import tpu as pltpu
@@ -141,8 +142,24 @@
     return lambda place, first, size: ref.at[:, pl.ds(pl.multiple_of(place * 96 + first, 16), size)]
 
 
-def start_kernel(x, wo, fb, tok, wx, wf0, zb, token_send, token_recv, send, recv, local):
+class Moves:
+    def __init__(self, sems):
+        self.sems, self.count = sems, 0
+
+    def start(self, src, dst):
+        copy = pltpu.make_async_copy(src, dst, self.sems.at[self.count])
+        self.count += 1
+        copy.start()
+        return copy
+
+
+def start_kernel(
+    x, wo, fb, near_row, inverse,
+    tok, w, wf0, zb, zl, qa_out, ka_out, kt_out, vn_out, va_out, cos_out, sin_out, seg, first, end,
+    tv, wx, wv, far_row, cos, sin, qa, ka, kt, vn, va, token_send, token_recv, send, recv, local,
+):
     me = Place()
+    moves = Moves(local)
     c, z = me.c, me.z
     away = z + c * (3 - 2 * z)
 
@@ -169,7 +186,7 @@
 
     def copy(kind, k, ch, src, to):
         return pltpu.make_async_remote_copy(
-            src_ref=src, dst_ref=tok.at[line(k), part(ch)],
+            src_ref=src, dst_ref=tv.at[line(k), part(ch)],
             send_sem=token_send.at[kind, k, ch],
             recv_sem=token_recv.at[k, ch], device_id=to, device_id_type=MESH,
         )
@@ -178,8 +195,13 @@
         return x.at[part(ch)]
 
     def held(k, ch):
-        return tok.at[line(k), part(ch)]
-
+        return tv.at[line(k), part(ch)]
+
+    links = Links(send, recv)
+    rows_far = links.start(near_row, far_row, me.sib)
+    attn_z = links.start(view_2d(wo)(me.place, 0, 96), view_2d(wx)(me.place, 0, 96), me.z2)
+    ff_z1 = links.make(fb, zb.at[0], me.z1)
+    ff_z2 = links.make(fb, zb.at[1], me.z2)
     for k, to in ((0, near), (1, far), (2, near), (3, near)):
 
         @pl.when(away == k)
@@ -189,20 +211,16 @@
                 if k < 2:
                     copy(1, k, ch, own(ch), me.sib).start()
 
-    links = Links(send, recv)
-    attn_z = links.start(view_2d(wo)(me.place, 0, 96), view_2d(wx)(me.place, 0, 96), me.z2)
-    ff_z = links.make(fb, zb.at[1], me.z2)
+    ff_z1.start()
+    links.started.append(ff_z1)
+    ff_z2.start()
+    links.started.append(ff_z2)
     ff0 = Spread(me, links, view_3d(wf0), fb)
-    here = [
-        pltpu.make_async_copy(fb, view_3d(wf0)(me.place, 0, 96), local.at[0]),
-        pltpu.make_async_copy(fb, zb.at[0], local.at[1]),
-    ]
-    for h in here:
-        h.start()
+    here = moves.start(fb, view_3d(wf0)(me.place, 0, 96))
 
     @pl.when(away < 2)
     def _():
-        mine = pltpu.make_async_copy(x, tok.at[z], local.at[2])
+        mine = pltpu.make_async_copy(x, tv.at[z], local.at[30])
         mine.start()
         mine.wait()
 
@@ -221,125 +239,82 @@
                     copy(0, k, ch, held(k, ch), far).start()
                 copy(1, k, ch, held(k, ch), me.sib).start()
 
+    def documents():
+        rows_far.wait_recv()
+        row = jnp.where(me.cross == 1, far_row[...], near_row[...])
+        seg[...] = row
+        opened = jnp.zeros(row.shape, F32)
+        closed = jnp.zeros(row.shape, F32)
+        before = jnp.zeros((1, 1), F32)
+        for d in range(SEGS):
+            here = (row == d).astype(F32)
+            opened += here * before
+            before = before + jnp.sum(here, axis=1, keepdims=True)
+            closed += here * before
+        first[...] = opened.astype(jnp.int32)
+        end[...] = closed.astype(jnp.int32)
+        places = lax.broadcasted_iota(jnp.int32, row.shape, 1).astype(F32) - opened
+        for e in range(4):
+            at = slice(e * 512, (e + 1) * 512)
+            angles = inverse[...] * places[:, at]
+            cos[:, at] = jnp.cos(angles)
+            sin[:, at] = jnp.sin(angles)
+
     attn_z.wait_recv()
     attn = Spread(me, links, view_2d(wx))
+    documents()
     forward(0)
+    attn.second()
+    forward(1)
+    attn.third()
     ff0.second()
-    forward(1)
-    attn.second()
+    forward(2)
+    forward(3)
     ff0.third()
-    forward(2)
-
-    for k in (2, 3):
-
-        @pl.when(away == k)
-        def _(k=k):
-            copy(0, k, 2, own(2), near).wait_send()
-
-    ff_z.start()
-    links.started.append(ff_z)
-    attn.third()
-    forward(3)
 
     @pl.when(away >= 2)
     def _():
         for ch in range(CHUNKS):
             for k in range(4):
                 pltpu.make_async_remote_copy(
-                    src_ref=own(ch), dst_ref=tok.at[line_sib(k), part(ch)], send_sem=token_send.at[0, k, ch],
+                    src_ref=own(ch), dst_ref=tv.at[line_sib(k), part(ch)], send_sem=token_send.at[0, k, ch],
                     recv_sem=token_recv.at[k, ch], device_id=me.sib, device_id_type=MESH,
                 ).wait_recv()
 
-    for spread in (attn, ff0):
-        spread.last()
-    ff_z.wait_recv()
-    for h in here:
-        h.wait()
-    links.wait_sends()
-    for k, to in ((0, near), (1, far), (2, near), (3, near)):
-
-        @pl.when(away == k)
-        def _(k=k, to=to):
-            for ch in range(CHUNKS):
-                if k < 2 or ch != 2:
-                    copy(0, k, ch, own(ch), to).wait_send()
-                if k == 1:
-                    for j in (2, 3):
-                        copy(0, j, ch, held(j, ch), to).wait_send()
-                if k < 2:
-                    for j in range(4):
-                        copy(1, j, ch, own(ch) if j == k else held(j, ch), me.sib).wait_send()
-
-
-FIRST, LAST = 256, 512
-
-
-def list_pairs(sc, pairs):
-    idle = 8 * 16 + 8
-    pairs[0] = idle
-
-    def of_query(i, n):
-        lo, hi = sc[8 + i], sc[16 + i]
-
-        def of_key(j, n):
-            first = jnp.where(j == lo, FIRST, 0)
-            last = jnp.where(j == hi - 1, LAST, 0)
-            pairs[n] = i * 16 + j + first + last
-            return n + 1
-
-        return lax.fori_loop(lo, hi, of_key, n)
-
-    n = lax.fori_loop(0, 2048 // BLK, of_query, 1)
-    for more in range(3):
-        pairs[n + more] = idle
-    return n - 1
-
-
-def split_pair(code):
-    return (code // 16) % 16, code % 16
-
-
-def columns(block):
-    return pl.ds(pl.multiple_of(block * BLK, BLK), BLK)
-
-
-def real(block):
-    return jnp.where(block == 8, 0, block)
-
-
-def attend_forward_kernel(
-    sc, tok, cos, sin, seg, own, other, w, qa, ka, kt, vn, ot, logsum, part, va, mx, acc, s0, s1, p0, p1, al0, al1, pairs, sem
-):
+    attn.last()
+
+    def chosen(src):
+        return pltpu.make_async_copy(src, wv, local.at[31])
+
+    @pl.when(me.cross == 0)
+    def _():
+        chosen(wo).start()
+
+    @pl.when(me.cross == 1)
+    def _():
+        chosen(wx).start()
+
+    chosen(wx).wait()
+    moved = [here, moves.start(tv, tok), moves.start(wv, w), moves.start(cos, cos_out), moves.start(sin, sin_out)]
+
     heads = 3
     width = heads * HEAD_DIM
 
-    @pl.when(sc[0] == 0)
-    def _():
-        copy = pltpu.make_async_copy(own, w, sem.at[0])
-        copy.start()
-        copy.wait()
-
-    @pl.when(sc[0] == 1)
-    def _():
-        copy = pltpu.make_async_copy(other, w, sem.at[0])
-        copy.start()
-        copy.wait()
-
     def project(e, _):
         at = pl.ds(pl.multiple_of(e * 512, 512), 512)
-        made = nt(w[: 3 * width], tok[e])
-        c, s = cos[:, at], sin[:, at]
+        made = nt(wv[: 3 * width], tv[e])
+        c_, s_ = cos[:, at], sin[:, at]
         hot = (seg[:, at] == lax.broadcasted_iota(jnp.int32, (SEGS, 512), 0)).astype(F32)
         rest = jnp.zeros((64 - SEGS, 512), F32)
         one_row = (lax.broadcasted_iota(jnp.int32, (16, 512), 0) == 0).astype(F32)
         for h in range(heads):
             r = h * HEAD_DIM
             a1, a2 = made[r : r + 32], made[r + 32 : r + 64]
-            q = jnp.concatenate([a1 * c - a2 * s, a2 * c + a1 * s], axis=0).astype(BF16).astype(F32)
+            q = jnp.concatenate([a1 * c_ - a2 * s_, a2 * c_ + a1 * s_], axis=0).astype(BF16).astype(F32)
             qa[h, :, at] = jnp.concatenate([q * 0.125, hot, rest], axis=0).astype(BF16)
             r += width
             a1, a2 = made[r : r + 32], made[r + 32 : r + 64]
-            k = jnp.concatenate([a1 * c - a2 * s, a2 * c + a1 * s], axis=0)
+            k = jnp.concatenate([a1 * c_ - a2 * s_, a2 * c_ + a1 * s_], axis=0)
             kt[h * HEAD_DIM : (h + 1) * HEAD_DIM, at] = k.astype(BF16)
             ka[h, at, :] = jnp.concatenate([k, (1.0 - hot) * far_below, rest], axis=0).T.astype(BF16)
             r += width
@@ -349,8 +324,73 @@
         return 0
 
     lax.fori_loop(0, 4, project, 0)
-
-    count = list_pairs(sc, pairs)
+    for src, dst in ((qa, qa_out), (ka, ka_out), (kt, kt_out), (vn, vn_out), (va, va_out)):
+        moved.append(moves.start(src, dst))
+    ff0.last()
+    ff_z2.wait_recv()
+    moved.append(moves.start(zb.at[1], zl))
+    ff_z1.wait_recv()
+    for move in moved:
+        move.wait()
+    links.wait_sends()
+    for k, to in ((0, near), (1, far), (2, near), (3, near)):
+
+        @pl.when(away == k)
+        def _(k=k, to=to):
+            for ch in range(CHUNKS):
+                copy(0, k, ch, own(ch), to).wait_send()
+                if k == 1:
+                    for j in (2, 3):
+                        copy(0, j, ch, held(j, ch), to).wait_send()
+                if k < 2:
+                    for j in range(4):
+                        copy(1, j, ch, own(ch) if j == k else held(j, ch), me.sib).wait_send()
+
+
+FIRST, LAST = 256, 512
+
+
+def list_pairs(first, end, pairs):
+    idle = 8 * 16 + 8
+    pairs[0] = idle
+
+    def of_query(i, n):
+        lo = first[0, i * BLK] // BLK
+        hi = (end[0, i * BLK + BLK - 1] + (BLK - 1)) // BLK
+
+        def of_key(j, n):
+            pairs[n] = i * 16 + j + jnp.where(j == lo, FIRST, 0) + jnp.where(j == hi - 1, LAST, 0)
+            return n + 1
+
+        return lax.fori_loop(lo, hi, of_key, n)
+
+    n = lax.fori_loop(0, 2048 // BLK, of_query, 1)
+    for more in range(3):
+        pairs[n + more] = idle
+    return n - 1
+
+
+def split_pair(code):
+    return (code // 16) % 16, code % 16
+
+
+def columns(block):
+    return pl.ds(pl.multiple_of(block * BLK, BLK), BLK)
+
+
+def real(block):
+    return jnp.where(block == 8, 0, block)
+
+
+def attend_forward_kernel(
+    first, end, w_in, qa_in, ka_in, va_in, ot, logsum, part,
+    w, qa, ka, va, mx, acc, s0, s1, p0, p1, al0, al1, pairs, sem,
+):
+    heads = 3
+    width = heads * HEAD_DIM
+    moves = Moves(sem)
+    loads = [moves.start(src, dst) for src, dst in ((qa_in, qa), (ka_in, ka), (va_in, va), (w_in.at[pl.ds(3 * width, width)], w))]
+    count = list_pairs(first, end, pairs)
 
     def score(t, s):
         i, j = split_pair(pairs[t])
@@ -396,17 +436,33 @@
     acc[...] = jnp.zeros_like(acc)
     p1[...] = jnp.zeros_like(p1)
     al1[...] = jnp.zeros_like(al1)
+    for load in loads:
+        load.wait()
     score(1, s0)
     lax.fori_loop(0, (count + 2) // 2, step, 0)
     for e in range(4):
-        part[e] = tn(ot[:, e * 512 : (e + 1) * 512], w[3 * width :]).astype(BF16)
+        part[e] = tn(ot[:, e * 512 : (e + 1) * 512], w[...]).astype(BF16)
 
 
 def attend_backward_kernel(
-    sc, gb, tok, w, qa, ka, kt, vn, ot, logsum, cos, sin, grads, part, dot_, inner, dq, dk, dv, gp, s0, s1, r0, r1, p0, p1, d0, d1, pairs
+    first, end, gb_in, tok_in, w_in, qa_in, ka_in, kt_in, vn_in, ot_in, logsum, cos_in, sin_in, grads, part,
+    gb, tok, w, qa, ka, kt, vn, ot, cos, sin, dot_, inner, dq, dk, dv, gp, s0, s1, r0, r1, p0, p1, d0, d1, pairs, sem,
 ):
     heads = 3
     width = heads * HEAD_DIM
+    moves = Moves(sem)
+    loads = [
+        moves.start(src, dst)
+        for src, dst in (
+            (w_in, w), (ot_in, ot), (gb_in, gb), (qa_in, qa), (ka_in, ka), (vn_in, vn), (kt_in, kt), (cos_in, cos),
+            (sin_in, sin), (tok_in, tok),
+        )
+    ]
+    for total in (dq, dk, dv, p1, d1):
+        total[...] = jnp.zeros_like(total)
+    count = list_pairs(first, end, pairs)
+    for load in loads[:3]:
+        load.wait()
 
     def begin(e, _):
         at = pl.ds(pl.multiple_of(e * 512, 512), 512)
@@ -418,9 +474,8 @@
         return 0
 
     lax.fori_loop(0, 4, begin, 0)
-    for total in (dq, dk, dv, p1, d1):
-        total[...] = jnp.zeros_like(total)
-    count = list_pairs(sc, pairs)
+    for load in loads[3:]:
+        load.wait()
 
     def score(t, s, r):
         i, j = split_pair(pairs[t])
@@ -500,26 +555,24 @@
 
 
 def feed_forward_kernel(
-    tok, part, cot_in, gain, bias, wf0, zb, zx, zy, zc,
+    tok, part_in, cot_in, gain, bias, wf0, zb, zx, zy, zc,
     out, gz1, gb, sums, keep_a, keep_b, send_a, send_b, zs_out,
-    w, slope_g, slope_u, hid, nb, nbt, gm, gmt, total, norm1, inv1, dw, lw, xs, cot, from_core, from_z, to_z,
+    part, own_g, w, slope_g, slope_u, hid, nb, nbt, gm, gmt, total, norm1, inv1, dw, lw, xs, cot, from_core, from_z, to_z,
     f1a, f1b, f2a, f2b, send, recv, local, out_sem, trade_sem,
 ):
     me = Place()
     greet((me.sib, me.xn, me.yn, me.z1, me.pair))
     links = Links(send, recv)
-    loads = [
-        pltpu.make_async_copy(tok.at[me.slot], xs, local.at[0]),
-        pltpu.make_async_copy(wf0, w.at[0], local.at[1]),
-        pltpu.make_async_copy(zb.at[1], view_3d(w.at[2])(me.place, 0, 96), local.at[2]),
-        pltpu.make_async_copy(zc.at[0], view_3d(w.at[1])(me.place, 0, 96), local.at[3]),
-        pltpu.make_async_copy(zc.at[1], view_3d(w.at[3])(me.place, 0, 96), local.at[4]),
-        pltpu.make_async_copy(zx, view_3d(w.at[2])(me.x_place, 0, 96), local.at[5]),
-        pltpu.make_async_copy(zy, view_3d(w.at[2])(me.y_place, 0, 96), local.at[6]),
-    ]
+    moves = Moves(local)
+    partial = moves.start(part_in, part)
+    loads = [moves.start(tok.at[me.slot], xs), moves.start(wf0, w.at[0])]
+    for ez in (2, 1):
+        for place, src in ((me.place, zb), (me.x_place, zx), (me.y_place, zy)):
+            loads.append(moves.start(src.at[ez - 1], view_3d(w.at[ez])(place, 0, 96)))
+    loads.append(moves.start(zc, view_3d(w.at[3])(me.place, 0, 96)))
 
     def cot_here():
-        return pltpu.make_async_copy(cot_in, cot, local.at[7])
+        return pltpu.make_async_copy(cot_in, cot, local.at[15])
 
     def cot_there():
         return pltpu.make_async_remote_copy(
@@ -530,15 +583,13 @@
     def rows(ch):
         return pl.ds(ch * CHUNK, CHUNK)
 
+    partial.wait()
     cores = [
         [links.start(part.at[shard, rows(ch)], from_core.at[i, rows(ch)], me.sib) for ch in range(CHUNKS)]
         for i, shard in ((1, me.slot3), (0, me.slot2))
     ]
-    ff2 = Corner(me, links, view_3d(w.at[2]), zb.at[1], zx, zy)
-    ff1 = Spread(me, links, view_3d(w.at[1]), zc.at[0])
-    ff3 = Spread(me, links, view_3d(w.at[3]), zc.at[1])
-    for load in loads:
-        load.start()
+    ff2, ff1 = [Corner(me, links, view_3d(w.at[ez]), *(src.at[ez - 1] for src in (zb, zx, zy))) for ez in (2, 1)]
+    ff3 = Spread(me, links, view_3d(w.at[3]), zc)
     zs = []
     for ch in range(CHUNKS):
         cores[0][ch].wait_recv()
@@ -555,7 +606,7 @@
         cot_there().start()
 
     ff2.third()
-    ff1.second()
+    ff1.third()
     loads[0].wait()
     for ch in range(CHUNKS):
         if ch == CHUNKS - 1:
@@ -571,7 +622,6 @@
         total[at] = normed
         nb[at] = normed.astype(BF16)
         nbt[:, ch * CHUNK : (ch + 1) * CHUNK] = normed.T.astype(BF16)
-    ff1.third()
 
     def forward(ez):
         gate = nn(nb[...], w[ez, 0])
@@ -586,15 +636,13 @@
 
     loads[1].wait()
     forward(0)
-    ff3.third()
-    for load in (loads[2], loads[5], loads[6]):
+    for load in loads[2:]:
         load.wait()
     ff2.last()
     forward(2)
-    loads[3].wait()
+    ff3.third()
     ff1.last()
     forward(1)
-    loads[4].wait()
     ff3.last()
     forward(3)
     n2, i2 = norm_forward(total[...])
@@ -619,7 +667,7 @@
     def block(quad, core):
         return pl.ds(pl.multiple_of((quad * 2 + core) * 96, 32), 96)
 
-    order = (1, 3, 0, 2)
+    order = (3, 1, 0, 2)
     halves = []
     first, last = pl.ds(0, 48), pl.ds(48, 48)
 
@@ -649,41 +697,36 @@
             for m in range(3):
                 lw[n, quad, m] = (lw[n, quad, m].astype(F32) + dw[n % 2, m, block(quad, me.c)].astype(F32)).astype(BF16)
 
-    plane_1, plane_2 = {}, {}
-
-    def plane_first(n):
-        plane_1[n] = [
+    def plane_first():
+        return [
             (
-                links.start(lw.at[n, (1 - me.y) * 2 + o, :, first], f1a.at[n, o], me.yn),
-                links.start(lw.at[n, o * 2 + 1 - me.x, :, last], f1b.at[n, o], me.xn),
+                links.start(lw.at[0, (1 - me.y) * 2 + o, :, first], f1a.at[o], me.yn),
+                links.start(lw.at[0, o * 2 + 1 - me.x, :, last], f1b.at[o], me.xn),
             )
             for o in range(2)
         ]
 
-    def plane_second(n):
+    def plane_second(plane_1):
         for o in range(2):
-            plane_1[n][o][0].wait_recv()
-            f1a[n, o] = (f1a[n, o].astype(F32) + lw[n, me.y * 2 + o, :, first].astype(F32)).astype(BF16)
-            plane_1[n][o][1].wait_recv()
-            f1b[n, o] = (f1b[n, o].astype(F32) + lw[n, o * 2 + me.x, :, last].astype(F32)).astype(BF16)
-        plane_2[n] = (
-            links.start(f1a.at[n, 1 - me.x], f2a.at[n], me.xn),
-            links.start(f1b.at[n, 1 - me.y], f2b.at[n], me.yn),
-        )
-
-    def plane_last(n):
-        plane_2[n][0].wait_recv()
-        zs_out[n, 0] = (f1a[n, me.x].astype(F32) + f2a[n].astype(F32)).astype(BF16)
-        plane_2[n][1].wait_recv()
-        zs_out[n, 1] = (f1b[n, me.y].astype(F32) + f2b[n].astype(F32)).astype(BF16)
+            plane_1[o][0].wait_recv()
+            f1a[o] = (f1a[o].astype(F32) + lw[0, me.y * 2 + o, :, first].astype(F32)).astype(BF16)
+            plane_1[o][1].wait_recv()
+            f1b[o] = (f1b[o].astype(F32) + lw[0, o * 2 + me.x, :, last].astype(F32)).astype(BF16)
+        return links.start(f1a.at[1 - me.x], f2a, me.xn), links.start(f1b.at[1 - me.y], f2b, me.yn)
+
+    def plane_last(plane_2):
+        plane_2[0].wait_recv()
+        zs_out[0] = (f1a[me.x].astype(F32) + f2a[...].astype(F32)).astype(BF16)
+        plane_2[1].wait_recv()
+        zs_out[1] = (f1b[me.y].astype(F32) + f2b[...].astype(F32)).astype(BF16)
 
     def stores(n):
         made = []
         for oy in range(2):
             for ox in range(2):
                 src = lw.at[n, oy * 2 + ox]
-                made.append((me.y == oy, src.at[:, first], keep_a.at[n - 2, ox], send_a.at[n - 2, ox]))
-                made.append((me.x == ox, src.at[:, last], keep_b.at[n - 2, oy], send_b.at[n - 2, oy]))
+                made.append((me.y == oy, src.at[:, first], keep_a.at[n - 1, ox], send_a.at[n - 1, ox]))
+                made.append((me.x == ox, src.at[:, last], keep_b.at[n - 1, oy], send_b.at[n - 1, oy]))
         return made
 
     def store(n):
@@ -691,21 +734,18 @@
 
             @pl.when(here)
             def _(number=number, src=src, kept=kept):
-                pltpu.make_async_copy(src, kept, out_sem.at[n - 2, number]).start()
+                pltpu.make_async_copy(src, kept, out_sem.at[n - 1, number]).start()
 
             @pl.when(jnp.logical_not(here))
             def _(number=number, src=src, sent=sent):
-                pltpu.make_async_copy(src, sent, out_sem.at[n - 2, number]).start()
-
+                pltpu.make_async_copy(src, sent, out_sem.at[n - 1, number]).start()
+
+    slopes(3)
+    weights(0)
     slopes(1)
-    weights(0)
-    slopes(3)
+    slopes(0)
     settle(0)
-    plane_first(0)
-    weights(1)
-    slopes(0)
-    settle(1)
-    plane_first(1)
+    plane_1 = plane_first()
     slopes(2)
     g = total[...]
     sums[0:1, :] = jnp.sum(g * norm1[...], axis=0, keepdims=True)
@@ -716,29 +756,33 @@
         at = rows(ch)
         made = norm_backward(total[at] * gain[0:1, :], norm1[at], inv1[at, 0:1])
         gz1[at] = made
-        gb[me.slot, at] = made.astype(BF16)
+        own_g[at] = made.astype(BF16)
         mine = gb.at[me.slot, at]
-        to_pair.append(links.start(mine, mine, me.z1))
-        to_core.append(links.start(mine, mine, me.sib))
+        to_pair.append(links.start(own_g.at[at], mine, me.z1))
+        to_core.append(links.start(own_g.at[at], mine, me.sib))
+    kept_g = moves.start(own_g, gb.at[me.slot])
+    weights(1)
     weights(2)
-    plane_second(0)
+    settle(1)
+    store(1)
+    plane_2 = plane_second(plane_1)
     weights(3)
     settle(2)
     store(2)
-    plane_second(1)
     settle(3)
     store(3)
     for ch in range(CHUNKS):
         to_pair[ch].wait_recv()
         other = gb.at[me.slot1, rows(ch)]
         on_core.append(links.start(other, other, me.sib))
-    plane_last(0)
-    plane_last(1)
+    plane_last(plane_2)
+    kept_g.wait()
     for copy in to_core + on_core:
         copy.wait_recv()
+    for n in (1, 2, 3):
+        for number, (_, src, kept, _) in enumerate(stores(n)):
+            pltpu.make_async_copy(src, kept, out_sem.at[n - 1, number]).wait()
     for n in (2, 3):
-        for number, (_, src, kept, _) in enumerate(stores(n)):
-            pltpu.make_async_copy(src, kept, out_sem.at[n - 2, number]).wait()
         for copy in halves[n]:
             copy.wait_send()
     links.wait_sends()
@@ -747,7 +791,7 @@
 def finish_kernel(
     extra, keep_a, keep_b, recv_a, recv_b, zr, ga, part, gz1, sums_in,
     g_ff, g_attn, g_tok, sums,
-    sa, sb, f2a, f2b, va, f4, fe, a_in, a_mid, a_out, a_fin, a_two, ae, from_core, from_z, to_z, trade_out, trade_in, sum_in,
+    sa, sb, f2a, f2b, va, f3, f4, fe, a_in, a_mid, a_out, a_fin, a_two, ae, from_core, from_z, to_z, trade_out, trade_in, sum_in,
     send, recv, a_send, a_recv,
 ):
     me = Place()
@@ -796,29 +840,28 @@
 
     def planed(ez):
         ff_2[ez][0].wait_recv()
-        va[ez, 0] = add(keep_a[ez, me.x], recv_a[ez, me.x], f2a[ez], zr[ez, 0])
+        va[ez, 0] = add(keep_a[ez, me.x], recv_a[ez, me.x], f2a[ez], *([zr[0]] if ez == 2 else []))
         ff_2[ez][1].wait_recv()
-        va[ez, 1] = add(keep_b[ez, me.y], recv_b[ez, me.y], f2b[ez], zr[ez, 1])
-
-    plane(1)
-    plane(0)
+        va[ez, 1] = add(keep_b[ez, me.y], recv_b[ez, me.y], f2b[ez], *([zr[1]] if ez == 2 else []))
+
+    plane(2)
     zs = []
     for ch in range(CHUNKS):
         cores[0][ch].wait_recv()
         at = rows(ch)
         to_z[at] = add(part[me.slot1, at], from_core[1, at])
         zs.append(links.start(to_z.at[at], from_z.at[at], me.z1))
-    small_step()
-    planed(1)
-    ff_4 = links.start(va.at[1], f4, me.z2)
     for copy in attn_1:
         copy.wait_recv()
+    small_step()
     a_mid[0] = add(ga[half(me.y, 1 - me.x, 0)], a_in[0, 1 - me.x])
     a_mid[1] = add(ga[half(1 - me.y, me.x, 1)], a_in[1, 1 - me.y])
     attn_2 = [links.start(a_mid.at[0], a_out.at[0], me.xn), links.start(a_mid.at[1], a_out.at[1], me.yn)]
-    planed(0)
+    planed(2)
+    ff_4 = links.start(va.at[2], f4, me.z2)
     for copy in attn_2:
         copy.wait_recv()
+    small_step()
     a_fin[:96] = add(ga[half(me.y, me.x, 0)], a_in[0, me.x], a_out[0])
     a_fin[96:] = add(ga[half(me.y, me.x, 1)], a_in[1, me.y], a_out[1])
 
@@ -837,7 +880,11 @@
     def _():
         attn_over().start()
 
-    small_step()
+    plane(0)
+    plane(1)
+    planed(0)
+    ff_3 = links.start(va.at[0], f3, me.z1)
+    planed(1)
     small_step()
 
     trades = [
@@ -847,20 +894,6 @@
         )
         for ch in range(CHUNKS)
     ]
-    for ch in range(CHUNKS):
-        cores[1][ch].wait_recv()
-        zs[ch].wait_recv()
-        at = rows(ch)
-        got = gz1[at] + (part[me.slot, at].astype(F32) + from_core[0, at].astype(F32) + from_z[at].astype(F32))
-
-        @pl.when(me.cross == 0)
-        def _(at=at, got=got):
-            g_tok[at] = got
-
-        @pl.when(me.cross == 1)
-        def _(at=at, got=got, ch=ch):
-            trade_out[at] = got.astype(BF16)
-
     mine = quarter(me.y, me.x)
 
     def attn_send(n, src, to):
@@ -885,14 +918,35 @@
         attn_send(2, mine, me.yn).start()
         attn_send(3, mine, me.sib).start()
 
+    for ch in range(CHUNKS):
+        cores[1][ch].wait_recv()
+        zs[ch].wait_recv()
+        at = rows(ch)
+        got = gz1[at] + (part[me.slot, at].astype(F32) + from_core[0, at].astype(F32) + from_z[at].astype(F32))
+
+        @pl.when(me.cross == 0)
+        def _(at=at, got=got):
+            g_tok[at] = got
+
+        @pl.when(me.cross == 1)
+        def _(at=at, got=got, ch=ch):
+            trade_out[at] = got.astype(BF16)
+
+    small_step()
+
+
+    @pl.when(me.cross == 0)
+    def _():
+        attn_send(1, block_x, me.xn).wait_recv()
+        attn_send(4, low_x, me.yn).start()
+        attn_send(5, block_x, me.sib).start()
+        attn_send(2, block_y, me.yn).wait_recv()
+        attn_send(6, high_y, me.xn).start()
+        attn_send(7, block_y, me.sib).start()
+
+    ff_3.wait_recv()
     ff_4.wait_recv()
-
-    @pl.when(me.cross == 1)
-    def _():
-        for ch in range(CHUNKS):
-            trades[ch].start()
-
-    total = add(va[0], f4[...])
+    total = add(va[1], f3[...], f4[...])
     for n, bit in enumerate(bits):
         fe[n, 0] = total
         step = links.start(fe.at[n, 0], fe.at[n, 1], bit)
@@ -901,20 +955,16 @@
     for h in range(2):
         g_ff[:, pl.ds(pl.multiple_of(me.place * 96 + h * 48, 16), 48)] = total[h]
     spread = Spread(me, links, view_3d(g_ff))
+
+    @pl.when(me.cross == 1)
+    def _():
+        for ch in range(CHUNKS):
+            trades[ch].start()
+
     while len(small) < len(around):
         small_step()
+    spread.second()
     small_step()
-
-    @pl.when(me.cross == 0)
-    def _():
-        attn_send(1, block_x, me.xn).wait_recv()
-        attn_send(4, low_x, me.yn).start()
-        attn_send(5, block_x, me.sib).start()
-        attn_send(2, block_y, me.yn).wait_recv()
-        attn_send(6, high_y, me.xn).start()
-        attn_send(7, block_y, me.sib).start()
-
-    spread.second()
 
     @pl.when(me.cross == 0)
     def _():
@@ -975,6 +1025,11 @@
     def shape(*dims, dtype=BF16):
         return jax.ShapeDtypeStruct(dims, dtype)
 
+    far = pl.BlockSpec(memory_space=pltpu.HBM)
+
+    def held(*dims, dtype=BF16):
+        return pltpu.HBM(dims, dtype)
+
     def dma(*dims):
         return pltpu.SemaphoreType.DMA(dims)
 
@@ -992,48 +1047,49 @@
         rows = lax.dynamic_slice(w_gate_up, (place * 96, 0, 0), (96, 2, 768))
         block = jnp.stack([rows[:, 0], rows[:, 1], lax.dynamic_slice(w_down, (place * 96, 0), (96, 768))])
 
-        tok, wx, wf0, zb = pl.pallas_call(
+        length = segments.shape[1]
+        inverse = jnp.asarray(np.exp(-2.0 * np.arange(HEAD_DIM // 2) / HEAD_DIM * log_base).astype(np.float32)[:, None])
+        tok, w, wf0, zb, zl, qa, ka, kt, vn, va, cos, sin, seg, first, end = pl.pallas_call(
             start_kernel,
             name="start",
             out_shape=(
-                shape(4, 512, 768), shape(768, 768), shape(3, 768, 768), shape(2, 3, 96, 768),
+                held(4, 512, 768), held(768, 768), held(3, 768, 768), held(2, 3, 96, 768), held(3, 96, 768),
+                held(3, 128, length), held(3, length, 128), held(192, length), held(3, length, 64), held(3, 80, length),
+                held(32, length, dtype=F32), held(32, length, dtype=F32),
+                *(shape(1, length, dtype=jnp.int32),) * 3,
             ),
-            in_specs=[hbm] * 3,
-            out_specs=(hbm,) * 4,
-            scratch_shapes=[dma(2, 4, CHUNKS), dma(4, CHUNKS), dma(40), dma(40), dma(4)],
-            compiler_params=params(16, 0),
-        )(tokens[0], own, block)
-
-        row = jnp.where(swapped, over(segments, 1), segments)[0]
-        length = row.shape[0]
-        onehot = (row[None, :] == jnp.arange(SEGS, dtype=jnp.int32)[:, None]).astype(jnp.int32)
-        counts = jnp.sum(onehot, axis=1)
-        order = jnp.arange(SEGS, dtype=jnp.int32)
-        starts = jnp.sum(jnp.where(order[None, :] < order[:, None], counts[None, :], 0), axis=1)
-        first_place = jnp.sum(onehot * starts[:, None], axis=0)
-        end_place = first_place + jnp.sum(onehot * counts[:, None], axis=0)
-        lo = first_place.reshape(-1, BLK)[:, 0] // BLK
-        hi = (end_place.reshape(-1, BLK)[:, -1] + (BLK - 1)) // BLK
-        seg = row[None, :]
-        places = (jnp.arange(length, dtype=jnp.int32) - first_place)[None, :].astype(F32)
-        inverse = jnp.exp(-2.0 * jnp.arange(HEAD_DIM // 2, dtype=F32) / HEAD_DIM * log_base)
-        angles = inverse[:, None] * places
-        cos, sin = jnp.cos(angles), jnp.sin(angles)
-        sc = jnp.concatenate([jnp.full((8,), swapped.astype(jnp.int32)), lo, hi]).astype(jnp.int32)
-
-        zc = lax.ppermute(zb, "tensor", [(i, i ^ 1) for i in range(tensor)])
-        zx, zy = over(zb[1], 2), over(zb[1], 4)
-
-        w, qa, ka, kt, vn, ot, logsum, part = pl.pallas_call(
+            in_specs=[hbm] * 3 + [vmem] * 2,
+            out_specs=(far,) * 12 + (vmem,) * 3,
+            scratch_shapes=[
+                pltpu.VMEM((4, 512, 768), BF16),
+                pltpu.VMEM((768, 768), BF16),
+                pltpu.VMEM((768, 768), BF16),
+                pltpu.VMEM((1, length), jnp.int32),
+                pltpu.VMEM((32, length), F32),
+                pltpu.VMEM((32, length), F32),
+                pltpu.VMEM((3, 128, length), BF16),
+                pltpu.VMEM((3, length, 128), BF16),
+                pltpu.VMEM((192, length), BF16),
+                pltpu.VMEM((3, length, 64), BF16),
+                pltpu.VMEM((3, 80, length), BF16),
+                dma(2, 4, CHUNKS), dma(4, CHUNKS), dma(40), dma(40), dma(32),
+            ],
+            compiler_params=params(62, 0),
+        )(tokens[0], own, block, segments, inverse)
+
+        zc = lax.ppermute(zl, "tensor", [(i, i ^ 1) for i in range(tensor)])
+        zx, zy = over(zb, 2), over(zb, 4)
+
+        ot, logsum, part = pl.pallas_call(
             attend_forward_kernel,
             name="attend_forward",
-            out_shape=(
-                shape(768, 768), shape(3, 128, length), shape(3, length, 128), shape(192, length),
-                shape(3, length, 64), shape(192, length), shape(8, length, dtype=F32), shape(4, 512, 768),
-            ),
-            in_specs=[smem, vmem, vmem, vmem, vmem, hbm, hbm],
-            out_specs=(vmem,) * 8,
+            out_shape=(held(192, length), shape(8, length, dtype=F32), held(4, 512, 768)),
+            in_specs=[smem] * 2 + [far] * 4,
+            out_specs=(vmem,) * 3,
             scratch_shapes=[
+                pltpu.VMEM((192, 768), BF16),
+                pltpu.VMEM((3, 128, length), BF16),
+                pltpu.VMEM((3, length, 128), BF16),
                 pltpu.VMEM((3, 80, length), BF16),
                 pltpu.VMEM((3, 1, BLK), F32),
                 pltpu.VMEM((3, 80, BLK), F32),
@@ -1041,22 +1097,25 @@
                 *[pltpu.VMEM((3, BLK, BLK), BF16)] * 2,
                 *[pltpu.VMEM((3, 1, BLK), F32)] * 2,
                 pltpu.SMEM((72,), jnp.int32),
-                dma(1),
+                dma(4),
             ],
-            compiler_params=params(48),
+            compiler_params=params(62),
             cost_estimate=pl.CostEstimate(flops=20_000_000_000, bytes_accessed=24_000_000, transcendentals=6_000_000),
-        )(sc, tok, cos, sin, seg, own, wx)
-
+        )(first, end, w, qa, ka, va)
+
+        plane = (3, 2, 3, 48, 768)
         out, gz1, gb, sums, keep_a, keep_b, send_a, send_b, zs = pl.pallas_call(
             feed_forward_kernel,
             name="feed_forward",
             out_shape=(
-                shape(512, 768), shape(512, 768, dtype=F32), shape(4, 512, 768), shape(8, 768, dtype=F32),
-                *(shape(2, 2, 3, 48, 768),) * 5,
+                shape(512, 768), shape(512, 768, dtype=F32), held(4, 512, 768), shape(8, 768, dtype=F32),
+                *(held(*plane),) * 4, shape(2, 3, 48, 768),
             ),
-            in_specs=[hbm, vmem, hbm, vmem, vmem] + [hbm] * 5,
-            out_specs=(vmem,) * 4 + (hbm,) * 4 + (vmem,),
+            in_specs=[far, far, hbm, vmem, vmem] + [far] * 5,
+            out_specs=(vmem, vmem, far, vmem) + (far,) * 4 + (vmem,),
             scratch_shapes=[
+                pltpu.VMEM((4, 512, 768), BF16),
+                pltpu.VMEM((512, 768), BF16),
                 pltpu.VMEM((4, 3, 768, 768), BF16),
                 pltpu.VMEM((4, 512, 768), BF16),
                 pltpu.VMEM((4, 512, 768), BF16),
@@ -1075,11 +1134,11 @@
                 pltpu.VMEM((2, 512, 768), BF16),
                 pltpu.VMEM((512, 768), BF16),
                 pltpu.VMEM((512, 768), BF16),
-                pltpu.VMEM((2, 2, 3, 48, 768), BF16),
-                pltpu.VMEM((2, 2, 3, 48, 768), BF16),
                 pltpu.VMEM((2, 3, 48, 768), BF16),
                 pltpu.VMEM((2, 3, 48, 768), BF16),
-                dma(80), dma(80), dma(8), dma(2, 8), dma(2),
+                pltpu.VMEM((3, 48, 768), BF16),
+                pltpu.VMEM((3, 48, 768), BF16),
+                dma(80), dma(80), dma(16), dma(3, 8), dma(2),
             ],
             compiler_params=params(62, 1),
             cost_estimate=pl.CostEstimate(flops=22_000_000_000, bytes_accessed=36_000_000, transcendentals=3_000_000),
@@ -1093,9 +1152,19 @@
             attend_backward_kernel,
             name="attend_backward",
             out_shape=(shape(768, 768), shape(4, 512, 768)),
-            in_specs=[smem] + [vmem] * 11,
+            in_specs=[smem] * 2 + [far] * 8 + [vmem] + [far] * 2,
             out_specs=(vmem,) * 2,
             scratch_shapes=[
+                pltpu.VMEM((4, 512, 768), BF16),
+                pltpu.VMEM((4, 512, 768), BF16),
+                pltpu.VMEM((768, 768), BF16),
+                pltpu.VMEM((3, 128, length), BF16),
+                pltpu.VMEM((3, length, 128), BF16),
+                pltpu.VMEM((192, length), BF16),
+                pltpu.VMEM((3, length, 64), BF16),
+                pltpu.VMEM((192, length), BF16),
+                pltpu.VMEM((32, length), F32),
+                pltpu.VMEM((32, length), F32),
                 pltpu.VMEM((192, length), BF16),
                 pltpu.VMEM((8, length), F32),
                 *[pltpu.VMEM((192, length + BLK), F32)] * 3,
@@ -1103,10 +1172,11 @@
                 *[pltpu.VMEM((3, BLK, BLK), F32)] * 4,
                 *[pltpu.VMEM((3, BLK, BLK), BF16)] * 4,
                 pltpu.SMEM((72,), jnp.int32),
+                dma(10),
             ],
-            compiler_params=params(48),
+            compiler_params=params(62),
             cost_estimate=pl.CostEstimate(flops=40_000_000_000, bytes_accessed=24_000_000, transcendentals=6_000_000),
-        )(sc, gb, tok, w, qa, ka, kt, vn, ot, logsum, cos, sin)
+        )(first, end, gb, tok, w, qa, ka, kt, vn, ot, logsum, cos, sin)
 
         spare = max(len(extra), 1)
         half = (48, 768)
@@ -1117,8 +1187,9 @@
             in_specs=[vmem] * 9,
             out_specs=(vmem,) * 4,
             scratch_shapes=[
-                *[pltpu.VMEM((2, 3, *half), BF16)] * 4,
-                pltpu.VMEM((2, 2, 3, *half), BF16),
+                *[pltpu.VMEM((3, 3, *half), BF16)] * 4,
+                pltpu.VMEM((3, 2, 3, *half), BF16),
+                pltpu.VMEM((2, 3, *half), BF16),
                 pltpu.VMEM((2, 3, *half), BF16),
                 pltpu.VMEM((spare, 2, 2, 3, *half), BF16),
                 pltpu.VMEM((2, 2, 96, 768), BF16),
@@ -1135,7 +1206,7 @@
                 pltpu.VMEM((5 + spare, 8, 768), F32),
                 dma(64), dma(64), dma(16 + spare), dma(16 + spare),
             ],
-            compiler_params=params(48, 2),
+            compiler_params=params(62, 2),
         )(keep_a, keep_b, recv_a, recv_b, zr, grads, part, gz1, sums)
 
         g_qkv, g_out, g_gate_up, g_down = pl.pallas_call(
@@ -1158,7 +1229,7 @@
                 pl.BlockSpec((256, 2, 768), lambda i: (i, 0, 0)),
                 pl.BlockSpec((256, 768), lambda i: (i, 0)),
             ),
-            compiler_params=params(32),
+            compiler_params=params(62),
             cost_estimate=pl.CostEstimate(flops=0, bytes_accessed=16_000_000, transcendentals=0),
         )(g_attn, g_attn, g_ff, g_ff)
         return (

time: 334 us -> 321 us (0.961)
  the two profiles are of different devices: /device:TPU:25 before, /device:TPU:0 now
where the time goes in v6:
time: 321 us; the launch traced here: 317 us
  Pallas kernels  292 us (91%)
  starting transfers between devices  9.88 us (3%)
  local copies, waits for them, and re-layouts  7.02 us (2%)
  waiting for transfers between devices  4.42 us (1%)
    pallas_call x1, Pallas kernels, on_device(): pl.pallas_call(functools.partial(finish_kernel, extra), name='finish', ou...  84.5 us
    pallas_call x1, Pallas kernels, on_device(): pl.pallas_call(feed_forward_kernel, name='feed_forward', out_shape=(shape...  78.9 us
    pallas_call x1, Pallas kernels, on_device(): pl.pallas_call(start_kernel, name='start', out_shape=(held(4, 512, 768),...  76 us
    pallas_call x1, Pallas kernels, on_device(): pl.pallas_call(attend_backward_kernel, name='attend_backward', out_shape=...  28.4 us
    pallas_call x1, Pallas kernels, on_device(): pl.pallas_call(attend_forward_kernel, name='attend_forward', out_shape=(h...  17.5 us
    pallas_call x1, Pallas kernels, on_device(): pl.pallas_call(widen_kernel, name='widen', grid=(3,), out_shape=(shape(57...  6.6 us
  transfers between devices with their start and end apart: 7, of which 4 were waited for; matrix products, arithmetic and copies ran while one was open for 0% of the time, Pallas kernels for 14%

profile of v6, /device:TPU:0, one launch (start us, length us, event | category | flops | bytes accessed | tf_op | source)
XLA Modules:
  0.0 317.0 jit_solution(7808344553138867987)
XLA Ops:
  0.6 0.0 copy-start
  0.7 0.0 copy-start.4
  0.7 0.0 copy-start.2
  0.7 1.2 copy-done
  1.9 1.5 constant_dynamic-slice_fusion
  3.5 0.0 copy-done.4
  3.5 0.0 copy-done.2
  3.5 1.1 pad_maximum_fusion.wo
  4.6 0.8 pad_maximum_fusion.1.fb
  5.4 76.0 %start.1 = (bf16[4,512,768]{2,1,0:T(8,128)(2,1)}, bf16[768,768]{1,0:T(8,128)(2,1)}, bf16[3,768,768]{2,1,0:T(8,128)(2,1)}, bf16[2,3,96,768]{3,2,1,0:T(8,128)(2,1)...) custom-call(bf16[512,768]{1,0:T(8,128)(2,1)} %bitcast.19, ...), custom_call_target="tpu_custom_call" | custom-call | tf_op jit(solution)/shard_map/start/pallas_call | solution.py:1052
  81.4 1.6 collective-permute-start.1
  83.0 1.5 collective-permute-start
  84.5 0.0 collective-permute-start.2
  84.5 17.5 %attend_forward.1 = (bf16[192,2048]{1,0:T(8,128)(2,1)}, f32[8,2048]{1,0:T(8,128)}, bf16[4,512,768]{2,1,0:T(8,128)(2,1)}) custom-call(s32[1,2048]{1,0:T(1,128)} %get-tuple-element.45.first, s32[1,2048]{1,0:T(1,128)} %get-tuple-element.46.end, bf16[768,768]{1,0:T(8,128)(2,1)} %get-tuple-element.47.w_in, bf16[3,128,2048]{2,1,0:T(8,128)(2,1)} %get-tuple-element.48.qa_in, ...), custom_call_target="tpu_custom_call" | custom-call | flops 20000000000 | bytes 24000000 | tf_op jit(solution)/shard_map/attend_forward/pallas_call | solution.py:1083
  102.0 0.0 collective-permute-done.2.zc
  102.0 0.0 copy-start.6
  102.0 1.8 collective-permute-done.1.zy
  103.9 0.0 copy-start.5
  103.9 1.3 collective-permute-done.zx
  105.2 0.0 copy-done.6
  105.2 0.0 copy-done.5
  105.2 78.9 %feed_forward.1 = (bf16[512,768]{1,0:T(8,128)(2,1)}, f32[512,768]{1,0:T(8,128)}, bf16[4,512,768]{2,1,0:T(8,128)(2,1)}, f32[8,768]{1,0:T(8,128)}, bf16[3,2,3,48,7...) custom-call(bf16[4,512,768]{2,1,0:T(8,128)(2,1)} %get-tuple-element., ...), custom_call_target="tpu_custom_call" | custom-call | flops 22000001024 | bytes 36000000 | tf_op jit(solution)/shard_map/feed_forward/pallas_call | solution.py:1107
  184.1 4.1 %collective-permute-start.6 = (bf16[2,3,48,768]{3,2,1,0:T(8,128)(2,1)}, bf16[2,3,48,768]{3,2,1,0:T(8,128)(2,1)}, u32[]{:S(2)}, u32[]{:S(2)}) collective-permute-start(bf16[2,3,48,768]{3,2,1,0:T(8,128)(2,1)} %get-tuple-element.60), channel_id=1, source_target_pairs={{0,1},{1,0},{2,3},{3,2},{4,5},{5,4},{6,7},{7,6},{8,9},{9,8},{10,11... | collective-permute-start | bytes 1327112 | tf_op jit(solution)/shard_map/ppermute | solution.py:1148
  188.2 0.7 collective-permute-start.3
  188.9 0.5 collective-permute-start.4
  189.5 1.5 collective-permute-start.5
  190.9 0.0 copy-start.3
  190.9 28.4 %attend_backward.1 = (bf16[768,768]{1,0:T(8,128)(2,1)}, bf16[4,512,768]{2,1,0:T(8,128)(2,1)}) custom-call(s32[1,2048]{1,0:T(1,128)} %get-tuple-element.45.first, s32[1,2048]{1,0:T(1,128)} %get-tuple-element.46.end, bf16[4,512,768]{2,1,0:T(8,128)(2,1)} %get-tuple-element.61.gb_in, bf16[4,512,768]{2,1,0:T(8,128)(2,1)} %get-tuple-element.44.tok.tok_in, ...), custom_call_target="tpu_custom_call" | custom-call | flops 40000000000 | bytes 24000000 | tf_op jit(solution)/shard_map/attend_backward/pallas_call | solution.py:1151
  219.4 0.0 collective-permute-done.3
  219.4 0.0 copy-done.3
  219.4 1.0 select_bitcast_fusion
  220.4 0.0 collective-permute-done.6.zr
  220.4 0.5 collective-permute-done.4.recv_a
  220.9 0.7 collective-permute-done.5.recv_b
  221.6 84.5 %finish.1 = (bf16[3,768,768]{2,1,0:T(8,128)(2,1)}, bf16[768,768]{1,0:T(8,128)(2,1)}, f32[512,768]{1,0:T(8,128)}, f32[8,768]{1,0:T(8,128)}) custom-call(bf16[3,2,3,48,768]{4,3,2,1,0:T(8,128)(2,1)} %get-tuple-element.56.keep_a, bf16[3,2,3,48,768]{4,3,2,1,0:T(8,128)(2,1)} %get-tuple-element.57.keep_b, ...), custom_call_target="tpu_custom_call" | custom-call | tf_op jit(solution)/shard_map/finish/pallas_call | solution.py:1183
  306.1 1.4 fusion
  307.5 6.6 %widen.1 = (f32[576,768]{1,0:T(8,128)}, f32[192,768]{1,0:T(8,128)}, f32[768,2,768]{2,1,0:T(2,128)}, f32[768,768]{1,0:T(8,128)}) custom-call(bf16[768,768]{1,0:T(8,128)(2,1)} %get-tuple-element.73.attn.out_rows, bf16[768,768]{1,0:T(8,128)(2,1)} %get-tuple-element.73.attn.out_rows, bf16[3,768,768]{2,1,0:T(8,128)(2,1)} %get-tuple-element.74.gate_up.down, ...), custom_call_target="tpu_custom_call" | custom-call | bytes 16000000 | tf_op jit(solution)/shard_map/widen/pallas_call | solution.py:1212
  314.1 0.0 copy-start.1
  314.1 2.7 copy.25
  316.8 0.0 copy-done.1
  (2 shorter events, 0.0 us)
Async XLA Ops:
  0.6 1.3 copy-start
  0.7 2.9 copy-start.4
  0.7 2.9 copy-start.2
  81.4 22.5 %collective-permute-start.1 = (bf16[2,3,96,768]{3,2,1,0:T(8,128)(2,1)}, bf16[2,3,96,768]{3,2,1,0:T(8,128)(2,1)S(1)}, u32[]{:S(2)}, u32[]{:S(2)}) collective-permute-start(bf16[2,3,96,768]{3,2,1,0:T(8,128)(2,1)} %get-tuple-element.53.zb), channel_id=1, source_target_pairs={{0,16},{4,20},{8,24},{12,28},{16,0},{20,4},{24,8},{28,12},{1,17},{... | collective-permute-start | bytes 2654216 | tf_op jit(solution)/shard_map/ppermute | solution.py:1014
  83.0 22.2 %collective-permute-start = (bf16[2,3,96,768]{3,2,1,0:T(8,128)(2,1)}, bf16[2,3,96,768]{3,2,1,0:T(8,128)(2,1)}, u32[]{:S(2)}, u32[]{:S(2)}) collective-permute-start(bf16[2,3,96,768]{3,2,1,0:T(8,128)(2,1)} %get-tuple-element.53.zb), channel_id=1, source_target_pairs={{0,8},{4,12},{8,0},{12,4},{16,24},{20,28},{24,16},{28,20},{1,9},{5... | collective-permute-start | bytes 2654216 | tf_op jit(solution)/shard_map/ppermute | solution.py:1014
  84.5 17.5 %collective-permute-start.2 = (bf16[3,96,768]{2,1,0:T(8,128)(2,1)}, bf16[3,96,768]{2,1,0:T(8,128)(2,1)S(1)}, u32[]{:S(2)}, u32[]{:S(2)}) collective-permute-start(bf16[3,96,768]{2,1,0:T(8,128)(2,1)} %get-tuple-element.54), channel_id=1, source_target_pairs={{0,1},{1,0},{2,3},{3,2},{4,5},{5,4},{6,7},{7,6},{8,9},{9,8},{10,11... | collective-permute-start | bytes 1327112 | tf_op jit(solution)/shard_map/ppermute | solution.py:1080
  102.0 3.2 %copy-start.6 = (bf16[3,96,768]{2,1,0:T(8,128)(2,1)}, bf16[3,96,768]{2,1,0:T(8,128)(2,1)S(1)}, u32[]{:S(2)}) copy-start(bf16[3,96,768]{2,1,0:T(8,128)(2,1)S(1)} %collective-permute-done.2.zc) | copy-start | bytes 1327108
  103.9 1.3 copy-start.5
  184.1 36.2 %collective-permute-start.6 = (bf16[2,3,48,768]{3,2,1,0:T(8,128)(2,1)}, bf16[2,3,48,768]{3,2,1,0:T(8,128)(2,1)}, u32[]{:S(2)}, u32[]{:S(2)}) collective-permute-start(bf16[2,3,48,768]{3,2,1,0:T(8,128)(2,1)} %get-tuple-element.60), channel_id=1, source_target_pairs={{0,1},{1,0},{2,3},{3,2},{4,5},{5,4},{6,7},{7,6},{8,9},{9,8},{10,11... | collective-permute-start | bytes 1327112 | tf_op jit(solution)/shard_map/ppermute | solution.py:1148
  188.2 31.2 %collective-permute-start.3 = (bf16[512,768]{1,0:T(8,128)(2,1)}, bf16[512,768]{1,0:T(8,128)(2,1)S(1)}, u32[]{:S(2)}, u32[]{:S(2)}) collective-permute-start(bf16[512,768]{1,0:T(8,128)(2,1)} %get-tuple-element.55), channel_id=1, source_target_pairs={{2,4},{3,5},{4,2},{5,3},{10,12},{11,13},{12,10},{13,11},{18,20},{1... | collective-permute-start | bytes 2359304 | tf_op jit(solution)/shard_map/ppermute | solution.py:1019
  188.9 32.0 %collective-permute-start.4 = (bf16[3,2,3,48,768]{4,3,2,1,0:T(8,128)(2,1)}, bf16[3,2,3,48,768]{4,3,2,1,0:T(8,128)(2,1)}, u32[]{:S(2)}, u32[]{:S(2)}) collective-permute-start(bf16[3,2,3,48,768]{4,3,2,1,0:T(8,128)(2,1)} %get-tuple-element.58), channel_id=1, source_target_pairs={{0,16},{4,20},{8,24},{12,28},{16,0},{20,4},{24,8},{28,12},{1,17},{... | collective-permute-start | bytes 3981320 | tf_op jit(solution)/shard_map/ppermute | solution.py:1014
  189.5 32.1 %collective-permute-start.5 = (bf16[3,2,3,48,768]{4,3,2,1,0:T(8,128)(2,1)}, bf16[3,2,3,48,768]{4,3,2,1,0:T(8,128)(2,1)}, u32[]{:S(2)}, u32[]{:S(2)}) collective-permute-start(bf16[3,2,3,48,768]{4,3,2,1,0:T(8,128)(2,1)} %get-tuple-element.59), channel_id=1, source_target_pairs={{0,8},{4,12},{8,0},{12,4},{16,24},{20,28},{24,16},{28,20},{1,9},{5... | collective-permute-start | bytes 3981320 | tf_op jit(solution)/shard_map/ppermute | solution.py:1014
  190.9 28.5 %copy-start.3 = (bf16[512,768]{1,0:T(8,128)(2,1)S(1)}, bf16[512,768]{1,0:T(8,128)(2,1)}, u32[]{:S(2)}) copy-start(bf16[512,768]{1,0:T(8,128)(2,1)} %get-tuple-element.55) | copy-start | bytes 2359300
  314.1 2.8 copy-start.1

commit v7 on v6

--- a/solution.py
+++ b/solution.py
@@ -154,12 +154,13 @@
 
 
 def start_kernel(
-    x, wo, fb, near_row, inverse,
+    x, w_qkv, w_out, fb, near_row, inverse,
     tok, w, wf0, zb, zl, qa_out, ka_out, kt_out, vn_out, va_out, cos_out, sin_out, seg, first, end,
-    tv, wx, wv, far_row, cos, sin, qa, ka, kt, vn, va, token_send, token_recv, send, recv, local,
+    wo, zv, tv, wx, wv, far_row, cos, sin, qa, ka, kt, vn, va, token_send, token_recv, send, recv, local,
 ):
     me = Place()
     moves = Moves(local)
+    wo_here = [moves.start(w_qkv, wo.at[pl.ds(0, 576)]), moves.start(w_out, wo.at[pl.ds(576, 192)])]
     c, z = me.c, me.z
     away = z + c * (3 - 2 * z)
 
@@ -199,9 +200,11 @@
 
     links = Links(send, recv)
     rows_far = links.start(near_row, far_row, me.sib)
+    for load in wo_here:
+        load.wait()
     attn_z = links.start(view_2d(wo)(me.place, 0, 96), view_2d(wx)(me.place, 0, 96), me.z2)
     ff_z1 = links.make(fb, zb.at[0], me.z1)
-    ff_z2 = links.make(fb, zb.at[1], me.z2)
+    ff_z2 = links.make(fb, zv, me.z2)
     for k, to in ((0, near), (1, far), (2, near), (3, near)):
 
         @pl.when(away == k)
@@ -328,7 +331,7 @@
         moved.append(moves.start(src, dst))
     ff0.last()
     ff_z2.wait_recv()
-    moved.append(moves.start(zb.at[1], zl))
+    moved += [moves.start(zv, zb.at[1]), moves.start(zv, zl)]
     ff_z1.wait_recv()
     for move in moved:
         move.wait()
@@ -789,12 +792,20 @@
 
 
 def finish_kernel(
-    extra, keep_a, keep_b, recv_a, recv_b, zr, ga, part, gz1, sums_in,
+    extra, keep_a_in, keep_b_in, recv_a_in, recv_b_in, zr_in, ga_in, part_in, gz1_in, sums_in,
     g_ff, g_attn, g_tok, sums,
+    keep_a, keep_b, recv_a, recv_b, zr, ga, part, gz1, block,
     sa, sb, f2a, f2b, va, f3, f4, fe, a_in, a_mid, a_out, a_fin, a_two, ae, from_core, from_z, to_z, trade_out, trade_in, sum_in,
-    send, recv, a_send, a_recv,
+    send, recv, a_send, a_recv, local,
 ):
     me = Place()
+    moves = Moves(local)
+    part_here, ga_here = moves.start(part_in, part), moves.start(ga_in, ga)
+    ff_here = [
+        moves.start(src, dst)
+        for src, dst in ((keep_a_in, keep_a), (recv_a_in, recv_a), (keep_b_in, keep_b), (recv_b_in, recv_b), (zr_in, zr))
+    ]
+    gz1_here = moves.start(gz1_in, gz1)
     bits = [{"dp": me.p + bit - 2 * bit * ((me.p // bit) % 2)} for bit in extra]
     greet([me.sib, me.xn, me.yn, me.z1, me.z2, me.pair] + bits)
     links = Links(send, recv)
@@ -805,6 +816,7 @@
     def add(*terms):
         return sum(t.astype(F32) for t in terms).astype(BF16)
 
+    part_here.wait()
     cores = [
         [links.start(part.at[shard, rows(ch)], from_core.at[i, rows(ch)], me.sib) for ch in range(CHUNKS)]
         for i, shard in ((1, me.slot3), (0, me.slot2))
@@ -814,6 +826,7 @@
         return pl.ds(pl.multiple_of((oy * 2 + ox) * 192 + h * 96, 32), 96)
 
     attn_1 = []
+    ga_here.wait()
     for o in range(2):
         attn_1.append(links.start(ga.at[half(1 - me.y, o, 0)], a_in.at[0, o], me.yn))
         attn_1.append(links.start(ga.at[half(o, 1 - me.x, 1)], a_in.at[1, o], me.xn))
@@ -844,6 +857,8 @@
         ff_2[ez][1].wait_recv()
         va[ez, 1] = add(keep_b[ez, me.y], recv_b[ez, me.y], f2b[ez], *([zr[1]] if ez == 2 else []))
 
+    for load in ff_here:
+        load.wait()
     plane(2)
     zs = []
     for ch in range(CHUNKS):
@@ -918,6 +933,7 @@
         attn_send(2, mine, me.yn).start()
         attn_send(3, mine, me.sib).start()
 
+    gz1_here.wait()
     for ch in range(CHUNKS):
         cores[1][ch].wait_recv()
         zs[ch].wait_recv()
@@ -953,8 +969,9 @@
         step.wait_recv()
         total = add(total, fe[n, 1])
     for h in range(2):
-        g_ff[:, pl.ds(pl.multiple_of(me.place * 96 + h * 48, 16), 48)] = total[h]
-    spread = Spread(me, links, view_3d(g_ff))
+        block[:, h * 48 : (h + 1) * 48] = total[h]
+    spread = Spread(me, links, view_3d(g_ff), block)
+    kept = moves.start(block, view_3d(g_ff)(me.place, 0, 96))
 
     @pl.when(me.cross == 1)
     def _():
@@ -990,15 +1007,19 @@
 
     spread.third()
     spread.last()
+    kept.wait()
     links.wait_sends()
 
 
-def widen_kernel(attn, out_rows, gate_up, down, g_qkv, g_out, g_gate_up, g_down):
+def widen_kernel(attn, out_rows, gate_up, down, tok, sums, g_qkv, g_out, g_gate_up, g_down, g_tok, gains, biases):
     g_qkv[...] = attn[...].astype(F32)
     g_out[...] = out_rows[...].astype(F32)
     g_gate_up[:, 0, :] = gate_up[0].astype(F32)
     g_gate_up[:, 1, :] = gate_up[1].astype(F32)
     g_down[...] = down[0].astype(F32).T
+    g_tok[0] = tok[...]
+    gains[...] = sums[0:2, :]
+    biases[...] = sums[2:4, :]
 
 
 def solution(mesh):
@@ -1043,7 +1064,6 @@
         swapped = (p & 1) != (z >> 1)
         place = p & 7
 
-        own = jnp.concatenate([w_qkv.transpose(1, 2, 0).reshape(576, 768), w_out])
         rows = lax.dynamic_slice(w_gate_up, (place * 96, 0, 0), (96, 2, 768))
         block = jnp.stack([rows[:, 0], rows[:, 1], lax.dynamic_slice(w_down, (place * 96, 0), (96, 768))])
 
@@ -1058,9 +1078,11 @@
                 held(32, length, dtype=F32), held(32, length, dtype=F32),
                 *(shape(1, length, dtype=jnp.int32),) * 3,
             ),
-            in_specs=[hbm] * 3 + [vmem] * 2,
+            in_specs=[hbm] * 3 + [vmem] * 3,
             out_specs=(far,) * 12 + (vmem,) * 3,
             scratch_shapes=[
+                pltpu.VMEM((768, 768), BF16),
+                pltpu.VMEM((3, 96, 768), BF16),
                 pltpu.VMEM((4, 512, 768), BF16),
                 pltpu.VMEM((768, 768), BF16),
                 pltpu.VMEM((768, 768), BF16),
@@ -1075,7 +1097,7 @@
                 dma(2, 4, CHUNKS), dma(4, CHUNKS), dma(40), dma(40), dma(32),
             ],
             compiler_params=params(62, 0),
-        )(tokens[0], own, block, segments, inverse)
+        )(tokens[0], w_qkv.transpose(1, 2, 0).reshape(576, 768), w_out, block, segments, inverse)
 
         zc = lax.ppermute(zl, "tensor", [(i, i ^ 1) for i in range(tensor)])
         zx, zy = over(zb, 2), over(zb, 4)
@@ -1183,10 +1205,16 @@
         g_ff, g_attn, g_tok, sums = pl.pallas_call(
             functools.partial(finish_kernel, extra),
             name="finish",
-            out_shape=(shape(3, 768, 768), shape(768, 768), shape(512, 768, dtype=F32), shape(8, 768, dtype=F32)),
-            in_specs=[vmem] * 9,
-            out_specs=(vmem,) * 4,
+            out_shape=(held(3, 768, 768), shape(768, 768), shape(512, 768, dtype=F32), shape(8, 768, dtype=F32)),
+            in_specs=[far] * 8 + [vmem],
+            out_specs=(far, vmem, vmem, vmem),
             scratch_shapes=[
+                *[pltpu.VMEM((3, 2, 3, *half), BF16)] * 4,
+                pltpu.VMEM((2, 3, *half), BF16),
+                pltpu.VMEM((768, 768), BF16),
+                pltpu.VMEM((4, 512, 768), BF16),
+                pltpu.VMEM((512, 768), F32),
+                pltpu.VMEM((3, 96, 768), BF16),
                 *[pltpu.VMEM((3, 3, *half), BF16)] * 4,
                 pltpu.VMEM((3, 2, 3, *half), BF16),
                 pltpu.VMEM((2, 3, *half), BF16),
@@ -1204,38 +1232,40 @@
                 pltpu.VMEM((512, 768), BF16),
                 pltpu.VMEM((512, 768), BF16),
                 pltpu.VMEM((5 + spare, 8, 768), F32),
-                dma(64), dma(64), dma(16 + spare), dma(16 + spare),
+                dma(64), dma(64), dma(16 + spare), dma(16 + spare), dma(9),
             ],
             compiler_params=params(62, 2),
         )(keep_a, keep_b, recv_a, recv_b, zr, grads, part, gz1, sums)
 
-        g_qkv, g_out, g_gate_up, g_down = pl.pallas_call(
+        g_qkv, g_out, g_gate_up, g_down, g_tok, gains, biases = pl.pallas_call(
             widen_kernel,
             name="widen",
-            grid=(3,),
+            grid=(6,),
             out_shape=(
                 shape(576, 768, dtype=F32), shape(192, 768, dtype=F32), shape(768, 2, 768, dtype=F32),
-                shape(768, 768, dtype=F32),
+                shape(768, 768, dtype=F32), shape(1, 512, 768, dtype=F32), *(shape(2, 768, dtype=F32),) * 2,
             ),
             in_specs=[
-                pl.BlockSpec((192, 768), lambda i: (i, 0)),
-                pl.BlockSpec((64, 768), lambda i: (9 + i, 0)),
-                pl.BlockSpec((2, 256, 768), lambda i: (0, i, 0)),
-                pl.BlockSpec((1, 768, 256), lambda i: (2, 0, i)),
+                pl.BlockSpec((96, 768), lambda i: (i, 0)),
+                pl.BlockSpec((32, 768), lambda i: (18 + i, 0)),
+                pl.BlockSpec((2, 128, 768), lambda i: (0, i, 0)),
+                pl.BlockSpec((1, 768, 128), lambda i: (2, 0, i)),
+                pl.BlockSpec((128, 768), lambda i: (jnp.minimum(i, 3), 0)),
+                pl.BlockSpec((8, 768), lambda i: (0, 0)),
             ],
             out_specs=(
-                pl.BlockSpec((192, 768), lambda i: (i, 0)),
-                pl.BlockSpec((64, 768), lambda i: (i, 0)),
-                pl.BlockSpec((256, 2, 768), lambda i: (i, 0, 0)),
-                pl.BlockSpec((256, 768), lambda i: (i, 0)),
+                pl.BlockSpec((96, 768), lambda i: (i, 0)),
+                pl.BlockSpec((32, 768), lambda i: (i, 0)),
+                pl.BlockSpec((128, 2, 768), lambda i: (i, 0, 0)),
+                pl.BlockSpec((128, 768), lambda i: (i, 0)),
+                pl.BlockSpec((1, 128, 768), lambda i: (0, jnp.minimum(i, 3), 0)),
+                pl.BlockSpec((2, 768), lambda i: (0, 0)),
+                pl.BlockSpec((2, 768), lambda i: (0, 0)),
             ),
             compiler_params=params(62),
-            cost_estimate=pl.CostEstimate(flops=0, bytes_accessed=16_000_000, transcendentals=0),
-        )(g_attn, g_attn, g_ff, g_ff)
-        return (
-            output, g_tok[None], g_qkv.reshape(3, 192, 768).transpose(2, 0, 1), g_out, g_gate_up, g_down,
-            sums[0:2], sums[2:4],
-        )
+            cost_estimate=pl.CostEstimate(flops=0, bytes_accessed=18_000_000, transcendentals=0),
+        )(g_attn, g_attn, g_ff, g_ff, g_tok, sums)
+        return output, g_tok, g_qkv.reshape(3, 192, 768).transpose(2, 0, 1), g_out, g_gate_up, g_down, gains, biases
 
     placed = (
         P("dp", "tensor", None),

time: 321 us -> 301 us (0.938)
  Pallas kernels: 292 us -> 274 us
    pallas_call x1, Pallas kernels: 76 us -> 63.5 us  [on_device(): pl.pallas_call(start_kernel, name='start', out_shape=(held(4, 512, 768),...]
    pallas_call x1, Pallas kernels: 84.5 us -> 77.3 us  [on_device(): pl.pallas_call(functools.partial(finish_kernel, extra), name='finish', ou...]
  transfers between devices with their start and end apart: 7 -> 7, of which waited for: 4 -> 2; matrix products, arithmetic and copies ran while one was open for 0% -> 1% of each run, Pallas kernels for 14% -> 16%
where the time goes in v7:
time: 301 us; the launch traced here: 296 us
  Pallas kernels  274 us (91%)
  starting transfers between devices  10.8 us (4%)
  local copies, waits for them, and re-layouts  4.95 us (2%)
    pallas_call x1, Pallas kernels, on_device(): pl.pallas_call(feed_forward_kernel, name='feed_forward', out_shape=(shape...  77.4 us
    pallas_call x1, Pallas kernels, on_device(): pl.pallas_call(functools.partial(finish_kernel, extra), name='finish', ou...  77.3 us
    pallas_call x1, Pallas kernels, on_device(): pl.pallas_call(start_kernel, name='start', out_shape=(held(4, 512, 768),...  63.5 us
    pallas_call x1, Pallas kernels, on_device(): pl.pallas_call(attend_backward_kernel, name='attend_backward', out_shape=...  29.5 us
    pallas_call x1, Pallas kernels, on_device(): pl.pallas_call(attend_forward_kernel, name='attend_forward', out_shape=(h...  18.3 us
    pallas_call x1, Pallas kernels, on_device(): pl.pallas_call(widen_kernel, name='widen', grid=(6,), out_shape=(shape(57...  8.12 us
  transfers between devices with their start and end apart: 7, of which 2 were waited for; matrix products, arithmetic and copies ran while one was open for 1% of the time, Pallas kernels for 16%

profile of v7, /device:TPU:0, one launch (start us, length us, event | category | flops | bytes accessed | tf_op | source)
XLA Modules:
  0.0 296.3 jit_solution(16636983445664009683)
XLA Ops:
  0.6 0.0 copy-start
  0.7 1.3 copy-done
  1.9 1.5 constant_dynamic-slice_fusion
  3.5 0.8 pad_maximum_fusion.fb
  4.3 63.5 %start.1 = (bf16[4,512,768]{2,1,0:T(8,128)(2,1)}, bf16[768,768]{1,0:T(8,128)(2,1)}, bf16[3,768,768]{2,1,0:T(8,128)(2,1)}, bf16[2,3,96,768]{3,2,1,0:T(8,128)(2,1)...) custom-call(bf16[512,768]{1,0:T(8,128)(2,1)} %bitcast.17, ...), custom_call_target="tpu_custom_call" | custom-call | tf_op jit(solution)/shard_map/start/pallas_call | solution.py:1072
  67.8 1.6 collective-permute-start.1
  69.4 1.5 collective-permute-start
  70.9 0.0 collective-permute-start.2
  70.9 18.3 %attend_forward.1 = (bf16[192,2048]{1,0:T(8,128)(2,1)}, f32[8,2048]{1,0:T(8,128)}, bf16[4,512,768]{2,1,0:T(8,128)(2,1)}) custom-call(s32[1,2048]{1,0:T(1,128)} %get-tuple-element.48.first, s32[1,2048]{1,0:T(1,128)} %get-tuple-element.49.end, bf16[768,768]{1,0:T(8,128)(2,1)} %get-tuple-element.50.w_in, bf16[3,128,2048]{2,1,0:T(8,128)(2,1)} %get-tuple-element.51.qa_in, ...), custom_call_target="tpu_custom_call" | custom-call | flops 20000000000 | bytes 24000000 | tf_op jit(solution)/shard_map/attend_forward/pallas_call | solution.py:1105
  89.2 0.0 collective-permute-done.2.zc
  89.2 0.7 collective-permute-done.1.zy
  89.9 0.0 copy-start.4
  89.9 1.8 collective-permute-done.zx
  91.8 0.0 copy-start.5
  91.8 0.0 copy-done.4
  91.8 0.9 copy-done.5
  92.7 77.4 %feed_forward.1 = (bf16[512,768]{1,0:T(8,128)(2,1)}, f32[512,768]{1,0:T(8,128)}, bf16[4,512,768]{2,1,0:T(8,128)(2,1)}, f32[8,768]{1,0:T(8,128)}, bf16[3,2,3,48,7...) custom-call(bf16[4,512,768]{2,1,0:T(8,128)(2,1)} %get-tuple-element., ...), custom_call_target="tpu_custom_call" | custom-call | flops 22000001024 | bytes 36000000 | tf_op jit(solution)/shard_map/feed_forward/pallas_call | solution.py:1129
  170.1 4.1 %collective-permute-start.6 = (bf16[2,3,48,768]{3,2,1,0:T(8,128)(2,1)}, bf16[2,3,48,768]{3,2,1,0:T(8,128)(2,1)S(1)}, u32[]{:S(2)}, u32[]{:S(2)}) collective-permute-start(bf16[2,3,48,768]{3,2,1,0:T(8,128)(2,1)} %get-tuple-element.63), channel_id=1, source_target_pairs={{0,1},{1,0},{2,3},{3,2},{4,5},{5,4},{6,7},{7,6},{8,9},{9,8},{10,11... | collective-permute-start | bytes 1327112 | tf_op jit(solution)/shard_map/ppermute | solution.py:1170
  174.1 1.6 collective-permute-start.3
  175.7 1.4 collective-permute-start.4
  177.1 0.7 collective-permute-start.5
  177.8 29.5 %attend_backward.1 = (bf16[768,768]{1,0:T(8,128)(2,1)}, bf16[4,512,768]{2,1,0:T(8,128)(2,1)}) custom-call(s32[1,2048]{1,0:T(1,128)} %get-tuple-element.48.first, s32[1,2048]{1,0:T(1,128)} %get-tuple-element.49.end, bf16[4,512,768]{2,1,0:T(8,128)(2,1)} %get-tuple-element.64.gb_in, bf16[4,512,768]{2,1,0:T(8,128)(2,1)} %get-tuple-element.47.tok.tok_in, ...), custom_call_target="tpu_custom_call" | custom-call | flops 40000000000 | bytes 24000000 | tf_op jit(solution)/shard_map/attend_backward/pallas_call | solution.py:1173
  207.2 0.0 collective-permute-done.3
  207.2 2.1 select_bitcast_fusion
  209.4 0.0 collective-permute-done.6.zr_in
  209.4 0.0 copy-start.3
  209.4 0.0 collective-permute-done.4.recv_a_in
  209.4 0.0 copy-start.2
  209.4 0.0 collective-permute-done.5.recv_b_in
  209.4 0.7 copy-done.3
  210.1 0.4 copy-done.2
  210.6 77.3 %finish.1 = (bf16[3,768,768]{2,1,0:T(8,128)(2,1)}, bf16[768,768]{1,0:T(8,128)(2,1)}, f32[512,768]{1,0:T(8,128)}, f32[8,768]{1,0:T(8,128)}) custom-call(bf16[3,2,3,48,768]{4,3,2,1,0:T(8,128)(2,1)} %get-tuple-element.59.keep_a_in, bf16[3,2,3,48,768]{4,3,2,1,0:T(8,128)(2,1)} %get-tuple-element.60.keep_b_in, bf16[3,2,3,48,768]{4,3,2,1,0:T(8,128)(2,1)} %copy-done.2, ...), custom_call_target="tpu_custom_call" | custom-call | tf_op jit(solution)/shard_map/finish/pallas_call | solution.py:1205
  287.9 0.0 copy-start.1
  287.9 8.1 %widen.1 = (f32[576,768]{1,0:T(8,128)}, f32[192,768]{1,0:T(8,128)}, f32[768,2,768]{2,1,0:T(2,128)}, f32[768,768]{1,0:T(8,128)}, f32[1,512,768]{2,1,0:T(8,128)}, /*index=5*/f32[2,768]{1,0:T(2,128)}, f32[2,768]{1,0:T(2,128)}) custom-call(bf16[768,768]{1,0:T(8,128)(2,1)} %get-tuple-element.75.attn.out_rows, bf16[768,768]{1,0:T(8,128)(2,1)} %get-tuple-element.75.attn.out_rows, ...), custom_call_target="tpu_custom_call" | custom-call | bytes 18000000 | tf_op jit(solution)/shard_map/widen/pallas_call | solution.py:1240
  296.1 0.0 copy-done.1
  (2 shorter events, 0.0 us)
Async XLA Ops:
  0.6 1.3 copy-start
  67.8 22.1 %collective-permute-start.1 = (bf16[2,3,96,768]{3,2,1,0:T(8,128)(2,1)}, bf16[2,3,96,768]{3,2,1,0:T(8,128)(2,1)S(1)}, u32[]{:S(2)}, u32[]{:S(2)}) collective-permute-start(bf16[2,3,96,768]{3,2,1,0:T(8,128)(2,1)} %get-tuple-element.56.zb), channel_id=1, source_target_pairs={{0,16},{4,20},{8,24},{12,28},{16,0},{20,4},{24,8},{28,12},{1,17},{... | collective-permute-start | bytes 2654216 | tf_op jit(solution)/shard_map/ppermute | solution.py:1035
  69.4 22.4 %collective-permute-start = (bf16[2,3,96,768]{3,2,1,0:T(8,128)(2,1)}, bf16[2,3,96,768]{3,2,1,0:T(8,128)(2,1)S(1)}, u32[]{:S(2)}, u32[]{:S(2)}) collective-permute-start(bf16[2,3,96,768]{3,2,1,0:T(8,128)(2,1)} %get-tuple-element.56.zb), channel_id=1, source_target_pairs={{0,8},{4,12},{8,0},{12,4},{16,24},{20,28},{24,16},{28,20},{1,9},{5... | collective-permute-start | bytes 2654216 | tf_op jit(solution)/shard_map/ppermute | solution.py:1035
  70.9 18.3 %collective-permute-start.2 = (bf16[3,96,768]{2,1,0:T(8,128)(2,1)}, bf16[3,96,768]{2,1,0:T(8,128)(2,1)}, u32[]{:S(2)}, u32[]{:S(2)}) collective-permute-start(bf16[3,96,768]{2,1,0:T(8,128)(2,1)} %get-tuple-element.57), channel_id=1, source_target_pairs={{0,1},{1,0},{2,3},{3,2},{4,5},{5,4},{6,7},{7,6},{8,9},{9,8},{10,11... | collective-permute-start | bytes 1327112 | tf_op jit(solution)/shard_map/ppermute | solution.py:1102
  89.9 1.8 copy-start.4
  91.8 0.9 copy-start.5
  170.1 39.3 %collective-permute-start.6 = (bf16[2,3,48,768]{3,2,1,0:T(8,128)(2,1)}, bf16[2,3,48,768]{3,2,1,0:T(8,128)(2,1)S(1)}, u32[]{:S(2)}, u32[]{:S(2)}) collective-permute-start(bf16[2,3,48,768]{3,2,1,0:T(8,128)(2,1)} %get-tuple-element.63), channel_id=1, source_target_pairs={{0,1},{1,0},{2,3},{3,2},{4,5},{5,4},{6,7},{7,6},{8,9},{9,8},{10,11... | collective-permute-start | bytes 1327112 | tf_op jit(solution)/shard_map/ppermute | solution.py:1170
  174.1 33.1 %collective-permute-start.3 = (bf16[512,768]{1,0:T(8,128)(2,1)}, bf16[512,768]{1,0:T(8,128)(2,1)}, u32[]{:S(2)}, u32[]{:S(2)}) collective-permute-start(bf16[512,768]{1,0:T(8,128)(2,1)} %get-tuple-element.58), channel_id=1, source_target_pairs={{2,4},{3,5},{4,2},{5,3},{10,12},{11,13},{12,10},{13,11},{18,20},{1... | collective-permute-start | bytes 2359304 | tf_op jit(solution)/shard_map/ppermute | solution.py:1040
  175.7 33.7 %collective-permute-start.4 = (bf16[3,2,3,48,768]{4,3,2,1,0:T(8,128)(2,1)}, bf16[3,2,3,48,768]{4,3,2,1,0:T(8,128)(2,1)S(1)}, u32[]{:S(2)}, u32[]{:S(2)}) collective-permute-start(bf16[3,2,3,48,768]{4,3,2,1,0:T(8,128)(2,1)} %get-tuple-element.61), channel_id=1, source_target_pairs={{0,16},{4,20},{8,24},{12,28},{16,0},{20,4},{24,8},{28,12},{1,17},{... | collective-permute-start | bytes 3981320 | tf_op jit(solution)/shard_map/ppermute | solution.py:1035
  177.1 32.3 %collective-permute-start.5 = (bf16[3,2,3,48,768]{4,3,2,1,0:T(8,128)(2,1)}, bf16[3,2,3,48,768]{4,3,2,1,0:T(8,128)(2,1)}, u32[]{:S(2)}, u32[]{:S(2)}) collective-permute-start(bf16[3,2,3,48,768]{4,3,2,1,0:T(8,128)(2,1)} %get-tuple-element.62), channel_id=1, source_target_pairs={{0,8},{4,12},{8,0},{12,4},{16,24},{20,28},{24,16},{28,20},{1,9},{5... | collective-permute-start | bytes 3981320 | tf_op jit(solution)/shard_map/ppermute | solution.py:1035
  209.4 0.8 copy-start.3
  209.4 1.2 copy-start.2
  287.9 8.1 %copy-start.1 = (bf16[768,768]{1,0:T(8,128)(2,1)S(1)}, bf16[768,768]{1,0:T(8,128)(2,1)}, u32[]{:S(2)}) copy-start(bf16[768,768]{1,0:T(8,128)(2,1)} %param.15) | copy-start | bytes 3538948

commit v8 on v7

--- a/solution.py
+++ b/solution.py
@@ -586,14 +586,14 @@
     def rows(ch):
         return pl.ds(ch * CHUNK, CHUNK)
 
-    partial.wait()
     cores = [
-        [links.start(part.at[shard, rows(ch)], from_core.at[i, rows(ch)], me.sib) for ch in range(CHUNKS)]
+        [links.start(part_in.at[shard, rows(ch)], from_core.at[i, rows(ch)], me.sib) for ch in range(CHUNKS)]
         for i, shard in ((1, me.slot3), (0, me.slot2))
     ]
     ff2, ff1 = [Corner(me, links, view_3d(w.at[ez]), *(src.at[ez - 1] for src in (zb, zx, zy))) for ez in (2, 1)]
     ff3 = Spread(me, links, view_3d(w.at[3]), zc)
     zs = []
+    partial.wait()
     for ch in range(CHUNKS):
         cores[0][ch].wait_recv()
         at = rows(ch)
@@ -611,9 +611,26 @@
     ff2.third()
     ff1.third()
     loads[0].wait()
+    loads[1].wait()
+    def forward(ez, at=pl.ds(0, 512)):
+        gate = nn(nb[at], w[ez, 0])
+        up = nn(nb[at], w[ez, 1])
+        sig = 1.0 / (1.0 + jnp.exp(-gate))
+        active = gate * sig
+        low = (active * up).astype(BF16)
+        hid[ez, at] = low
+        slope_u[ez, at] = active.astype(BF16)
+        slope_g[ez, at] = (up * sig * (1.0 + gate * (1.0 - sig))).astype(BF16)
+        total[at] += nn(low, w[ez, 2])
+
     for ch in range(CHUNKS):
-        if ch == CHUNKS - 1:
+        if ch == CHUNKS // 2:
+            forward(0, pl.ds(0, 256))
             ff3.second()
+            for load in loads[2:]:
+                load.wait()
+            ff2.last()
+            forward(2, pl.ds(0, 256))
         cores[1][ch].wait_recv()
         zs[ch].wait_recv()
         at = rows(ch)
@@ -626,23 +643,8 @@
         nb[at] = normed.astype(BF16)
         nbt[:, ch * CHUNK : (ch + 1) * CHUNK] = normed.T.astype(BF16)
 
-    def forward(ez):
-        gate = nn(nb[...], w[ez, 0])
-        up = nn(nb[...], w[ez, 1])
-        sig = 1.0 / (1.0 + jnp.exp(-gate))
-        active = gate * sig
-        low = (active * up).astype(BF16)
-        hid[ez] = low
-        slope_u[ez] = active.astype(BF16)
-        slope_g[ez] = (up * sig * (1.0 + gate * (1.0 - sig))).astype(BF16)
-        total[...] += nn(low, w[ez, 2])
-
-    loads[1].wait()
-    forward(0)
-    for load in loads[2:]:
-        load.wait()
-    ff2.last()
-    forward(2)
+    forward(0, pl.ds(256, 256))
+    forward(2, pl.ds(256, 256))
     ff3.third()
     ff1.last()
     forward(1)
@@ -674,13 +676,15 @@
     halves = []
     first, last = pl.ds(0, 48), pl.ds(48, 48)
 
-    def slopes(ez):
-        grad_hidden = nt(gm[...], w[ez, 2])
-        gate = (grad_hidden * slope_g[ez].astype(F32)).astype(BF16)
-        up = (grad_hidden * slope_u[ez].astype(F32)).astype(BF16)
-        slope_g[ez] = gate
-        slope_u[ez] = up
-        total[...] += nt(gate, w[ez, 0]) + nt(up, w[ez, 1])
+    upper, lower = pl.ds(0, 256), pl.ds(256, 256)
+
+    def slopes(ez, at=pl.ds(0, 512)):
+        grad_hidden = nt(gm[at], w[ez, 2])
+        gate = (grad_hidden * slope_g[ez, at].astype(F32)).astype(BF16)
+        up = (grad_hidden * slope_u[ez, at].astype(F32)).astype(BF16)
+        slope_g[ez, at] = gate
+        slope_u[ez, at] = up
+        total[at] += nt(gate, w[ez, 0]) + nt(up, w[ez, 1])
 
     def weights(n):
         i, ez = n % 2, order[n]
@@ -746,16 +750,13 @@
     slopes(3)
     weights(0)
     slopes(1)
-    slopes(0)
     settle(0)
     plane_1 = plane_first()
-    slopes(2)
-    g = total[...]
-    sums[0:1, :] = jnp.sum(g * norm1[...], axis=0, keepdims=True)
-    sums[2:3, :] = jnp.sum(g, axis=0, keepdims=True)
-    sums[4:8, :] = jnp.zeros((4, 768), F32)
     to_pair, to_core, on_core = [], [], []
     for ch in range(CHUNKS):
+        if ch % 2 == 0:
+            slopes(0, lower if ch else upper)
+            slopes(2, lower if ch else upper)
         at = rows(ch)
         made = norm_backward(total[at] * gain[0:1, :], norm1[at], inv1[at, 0:1])
         gz1[at] = made
@@ -764,6 +765,10 @@
         to_pair.append(links.start(own_g.at[at], mine, me.z1))
         to_core.append(links.start(own_g.at[at], mine, me.sib))
     kept_g = moves.start(own_g, gb.at[me.slot])
+    g = total[...]
+    sums[0:1, :] = jnp.sum(g * norm1[...], axis=0, keepdims=True)
+    sums[2:3, :] = jnp.sum(g, axis=0, keepdims=True)
+    sums[4:8, :] = jnp.zeros((4, 768), F32)
     weights(1)
     weights(2)
     settle(1)

time: 301 us -> 297 us (0.987)
    pallas_call x1, Pallas kernels: 29.5 us -> 35.2 us  [on_device(): pl.pallas_call(attend_backward_kernel, name='attend_backward', out_shape=...]
    pallas_call x1, Pallas kernels: 77.4 us -> 71.9 us  [on_device(): pl.pallas_call(feed_forward_kernel, name='feed_forward', out_shape=(shape...]
    pallas_call x1, Pallas kernels: 77.3 us -> 72.7 us  [on_device(): pl.pallas_call(functools.partial(finish_kernel, extra), name='finish', ou...]
    pallas_call x1, Pallas kernels: 18.3 us -> 22.6 us  [on_device(): pl.pallas_call(attend_forward_kernel, name='attend_forward', out_shape=(h...]
  transfers between devices with their start and end apart: 7 -> 7, of which waited for: 2 -> 0; matrix products, arithmetic and copies ran while one was open for 1% -> 1% of each run, Pallas kernels for 16% -> 20%
where the time goes in v8:
time: 297 us; the launch traced here: 294 us
  Pallas kernels  274 us (92%)
  starting transfers between devices  10.4 us (4%)
  local copies, waits for them, and re-layouts  5.22 us (2%)
    pallas_call x1, Pallas kernels, on_device(): pl.pallas_call(functools.partial(finish_kernel, extra), name='finish', ou...  72.7 us
    pallas_call x1, Pallas kernels, on_device(): pl.pallas_call(feed_forward_kernel, name='feed_forward', out_shape=(shape...  71.9 us
    pallas_call x1, Pallas kernels, on_device(): pl.pallas_call(start_kernel, name='start', out_shape=(held(4, 512, 768),...  63.5 us
    pallas_call x1, Pallas kernels, on_device(): pl.pallas_call(attend_backward_kernel, name='attend_backward', out_shape=...  35.2 us
    pallas_call x1, Pallas kernels, on_device(): pl.pallas_call(attend_forward_kernel, name='attend_forward', out_shape=(h...  22.6 us
    pallas_call x1, Pallas kernels, on_device(): pl.pallas_call(widen_kernel, name='widen', grid=(6,), out_shape=(shape(57...  8.12 us
  transfers between devices with their start and end apart: 7, of which 0 were waited for; matrix products, arithmetic and copies ran while one was open for 1% of the time, Pallas kernels for 20%

profile of v8, /device:TPU:0, one launch (start us, length us, event | category | flops | bytes accessed | tf_op | source)
XLA Modules:
  0.0 293.7 jit_solution(8316474411723792289)
XLA Ops:
  0.6 0.0 copy-start
  0.7 1.3 copy-done
  1.9 1.5 constant_dynamic-slice_fusion
  3.5 0.8 pad_maximum_fusion.fb
  4.3 63.5 %start.1 = (bf16[4,512,768]{2,1,0:T(8,128)(2,1)}, bf16[768,768]{1,0:T(8,128)(2,1)}, bf16[3,768,768]{2,1,0:T(8,128)(2,1)}, bf16[2,3,96,768]{3,2,1,0:T(8,128)(2,1)...) custom-call(bf16[512,768]{1,0:T(8,128)(2,1)} %bitcast.17, ...), custom_call_target="tpu_custom_call" | custom-call | tf_op jit(solution)/shard_map/start/pallas_call | solution.py:1077
  67.8 1.6 collective-permute-start.1
  69.4 1.5 collective-permute-start
  70.9 0.0 collective-permute-start.2
  70.9 22.6 %attend_forward.1 = (bf16[192,2048]{1,0:T(8,128)(2,1)}, f32[8,2048]{1,0:T(8,128)}, bf16[4,512,768]{2,1,0:T(8,128)(2,1)}) custom-call(s32[1,2048]{1,0:T(1,128)} %get-tuple-element.48.first, s32[1,2048]{1,0:T(1,128)} %get-tuple-element.49.end, bf16[768,768]{1,0:T(8,128)(2,1)} %get-tuple-element.50.w_in, bf16[3,128,2048]{2,1,0:T(8,128)(2,1)} %get-tuple-element.51.qa_in, ...), custom_call_target="tpu_custom_call" | custom-call | flops 20000000000 | bytes 24000000 | tf_op jit(solution)/shard_map/attend_forward/pallas_call | solution.py:1110
  93.5 0.0 collective-permute-done.2.zc
  93.5 0.0 collective-permute-done.1.zy
  93.5 0.0 copy-start.4
  93.5 0.0 collective-permute-done.zx
  93.5 0.0 copy-start.5
  93.5 0.9 copy-done.4
  94.4 0.3 copy-done.5
  94.7 71.9 %feed_forward.1 = (bf16[512,768]{1,0:T(8,128)(2,1)}, f32[512,768]{1,0:T(8,128)}, bf16[4,512,768]{2,1,0:T(8,128)(2,1)}, f32[8,768]{1,0:T(8,128)}, bf16[3,2,3,48,7...) custom-call(bf16[4,512,768]{2,1,0:T(8,128)(2,1)} %get-tuple-element., ...), custom_call_target="tpu_custom_call" | custom-call | flops 22000001024 | bytes 36000000 | tf_op jit(solution)/shard_map/feed_forward/pallas_call | solution.py:1134
  166.7 3.7 %collective-permute-start.6 = (bf16[2,3,48,768]{3,2,1,0:T(8,128)(2,1)}, bf16[2,3,48,768]{3,2,1,0:T(8,128)(2,1)S(1)}, u32[]{:S(2)}, u32[]{:S(2)}) collective-permute-start(bf16[2,3,48,768]{3,2,1,0:T(8,128)(2,1)} %get-tuple-element.63), channel_id=1, source_target_pairs={{0,1},{1,0},{2,3},{3,2},{4,5},{5,4},{6,7},{7,6},{8,9},{9,8},{10,11... | collective-permute-start | bytes 1327112 | tf_op jit(solution)/shard_map/ppermute | solution.py:1175
  170.3 1.6 collective-permute-start.3
  171.9 1.6 collective-permute-start.4
  173.5 0.5 collective-permute-start.5
  174.0 35.2 %attend_backward.1 = (bf16[768,768]{1,0:T(8,128)(2,1)}, bf16[4,512,768]{2,1,0:T(8,128)(2,1)}) custom-call(s32[1,2048]{1,0:T(1,128)} %get-tuple-element.48.first, s32[1,2048]{1,0:T(1,128)} %get-tuple-element.49.end, bf16[4,512,768]{2,1,0:T(8,128)(2,1)} %get-tuple-element.64.gb_in, bf16[4,512,768]{2,1,0:T(8,128)(2,1)} %get-tuple-element.47.tok.tok_in, ...), custom_call_target="tpu_custom_call" | custom-call | flops 40000000000 | bytes 24000000 | tf_op jit(solution)/shard_map/attend_backward/pallas_call | solution.py:1178
  209.2 0.0 collective-permute-done.3
  209.2 2.1 select_bitcast_fusion
  211.4 0.0 collective-permute-done.6.zr_in
  211.4 0.0 copy-start.3
  211.4 0.0 collective-permute-done.4.recv_a_in
  211.4 0.0 copy-start.2
  211.4 0.0 collective-permute-done.5.recv_b_in
  211.4 0.7 copy-done.3
  212.1 0.4 copy-done.2
  212.6 72.7 %finish.1 = (bf16[3,768,768]{2,1,0:T(8,128)(2,1)}, bf16[768,768]{1,0:T(8,128)(2,1)}, f32[512,768]{1,0:T(8,128)}, f32[8,768]{1,0:T(8,128)}) custom-call(bf16[3,2,3,48,768]{4,3,2,1,0:T(8,128)(2,1)} %get-tuple-element.59.keep_a_in, bf16[3,2,3,48,768]{4,3,2,1,0:T(8,128)(2,1)} %get-tuple-element.60.keep_b_in, bf16[3,2,3,48,768]{4,3,2,1,0:T(8,128)(2,1)} %copy-done.2, ...), custom_call_target="tpu_custom_call" | custom-call | tf_op jit(solution)/shard_map/finish/pallas_call | solution.py:1210
  285.3 0.0 copy-start.1
  285.3 8.1 %widen.1 = (f32[576,768]{1,0:T(8,128)}, f32[192,768]{1,0:T(8,128)}, f32[768,2,768]{2,1,0:T(2,128)}, f32[768,768]{1,0:T(8,128)}, f32[1,512,768]{2,1,0:T(8,128)}, /*index=5*/f32[2,768]{1,0:T(2,128)}, f32[2,768]{1,0:T(2,128)}) custom-call(bf16[768,768]{1,0:T(8,128)(2,1)} %get-tuple-element.75.attn.out_rows, bf16[768,768]{1,0:T(8,128)(2,1)} %get-tuple-element.75.attn.out_rows, ...), custom_call_target="tpu_custom_call" | custom-call | bytes 18000000 | tf_op jit(solution)/shard_map/widen/pallas_call | solution.py:1245
  293.5 0.0 copy-done.1
  (2 shorter events, 0.0 us)
Async XLA Ops:
  0.6 1.3 copy-start
  67.8 25.7 %collective-permute-start.1 = (bf16[2,3,96,768]{3,2,1,0:T(8,128)(2,1)}, bf16[2,3,96,768]{3,2,1,0:T(8,128)(2,1)S(1)}, u32[]{:S(2)}, u32[]{:S(2)}) collective-permute-start(bf16[2,3,96,768]{3,2,1,0:T(8,128)(2,1)} %get-tuple-element.56.zb), channel_id=1, source_target_pairs={{0,16},{4,20},{8,24},{12,28},{16,0},{20,4},{24,8},{28,12},{1,17},{... | collective-permute-start | bytes 2654216 | tf_op jit(solution)/shard_map/ppermute | solution.py:1040
  69.4 24.1 %collective-permute-start = (bf16[2,3,96,768]{3,2,1,0:T(8,128)(2,1)}, bf16[2,3,96,768]{3,2,1,0:T(8,128)(2,1)S(1)}, u32[]{:S(2)}, u32[]{:S(2)}) collective-permute-start(bf16[2,3,96,768]{3,2,1,0:T(8,128)(2,1)} %get-tuple-element.56.zb), channel_id=1, source_target_pairs={{0,8},{4,12},{8,0},{12,4},{16,24},{20,28},{24,16},{28,20},{1,9},{5... | collective-permute-start | bytes 2654216 | tf_op jit(solution)/shard_map/ppermute | solution.py:1040
  70.9 22.6 %collective-permute-start.2 = (bf16[3,96,768]{2,1,0:T(8,128)(2,1)}, bf16[3,96,768]{2,1,0:T(8,128)(2,1)}, u32[]{:S(2)}, u32[]{:S(2)}) collective-permute-start(bf16[3,96,768]{2,1,0:T(8,128)(2,1)} %get-tuple-element.57), channel_id=1, source_target_pairs={{0,1},{1,0},{2,3},{3,2},{4,5},{5,4},{6,7},{7,6},{8,9},{9,8},{10,11... | collective-permute-start | bytes 1327112 | tf_op jit(solution)/shard_map/ppermute | solution.py:1107
  93.5 0.9 copy-start.4
  93.5 1.2 copy-start.5
  166.7 44.7 %collective-permute-start.6 = (bf16[2,3,48,768]{3,2,1,0:T(8,128)(2,1)}, bf16[2,3,48,768]{3,2,1,0:T(8,128)(2,1)S(1)}, u32[]{:S(2)}, u32[]{:S(2)}) collective-permute-start(bf16[2,3,48,768]{3,2,1,0:T(8,128)(2,1)} %get-tuple-element.63), channel_id=1, source_target_pairs={{0,1},{1,0},{2,3},{3,2},{4,5},{5,4},{6,7},{7,6},{8,9},{9,8},{10,11... | collective-permute-start | bytes 1327112 | tf_op jit(solution)/shard_map/ppermute | solution.py:1175
  170.3 38.9 %collective-permute-start.3 = (bf16[512,768]{1,0:T(8,128)(2,1)}, bf16[512,768]{1,0:T(8,128)(2,1)}, u32[]{:S(2)}, u32[]{:S(2)}) collective-permute-start(bf16[512,768]{1,0:T(8,128)(2,1)} %get-tuple-element.58), channel_id=1, source_target_pairs={{2,4},{3,5},{4,2},{5,3},{10,12},{11,13},{12,10},{13,11},{18,20},{1... | collective-permute-start | bytes 2359304 | tf_op jit(solution)/shard_map/ppermute | solution.py:1045
  171.9 39.5 %collective-permute-start.4 = (bf16[3,2,3,48,768]{4,3,2,1,0:T(8,128)(2,1)}, bf16[3,2,3,48,768]{4,3,2,1,0:T(8,128)(2,1)S(1)}, u32[]{:S(2)}, u32[]{:S(2)}) collective-permute-start(bf16[3,2,3,48,768]{4,3,2,1,0:T(8,128)(2,1)} %get-tuple-element.61), channel_id=1, source_target_pairs={{0,16},{4,20},{8,24},{12,28},{16,0},{20,4},{24,8},{28,12},{1,17},{... | collective-permute-start | bytes 3981320 | tf_op jit(solution)/shard_map/ppermute | solution.py:1040
  173.5 37.9 %collective-permute-start.5 = (bf16[3,2,3,48,768]{4,3,2,1,0:T(8,128)(2,1)}, bf16[3,2,3,48,768]{4,3,2,1,0:T(8,128)(2,1)}, u32[]{:S(2)}, u32[]{:S(2)}) collective-permute-start(bf16[3,2,3,48,768]{4,3,2,1,0:T(8,128)(2,1)} %get-tuple-element.62), channel_id=1, source_target_pairs={{0,8},{4,12},{8,0},{12,4},{16,24},{20,28},{24,16},{28,20},{1,9},{5... | collective-permute-start | bytes 3981320 | tf_op jit(solution)/shard_map/ppermute | solution.py:1040
  211.4 0.8 copy-start.3
  211.4 1.2 copy-start.2
  285.3 8.1 %copy-start.1 = (bf16[768,768]{1,0:T(8,128)(2,1)S(1)}, bf16[768,768]{1,0:T(8,128)(2,1)}, u32[]{:S(2)}) copy-start(bf16[768,768]{1,0:T(8,128)(2,1)} %param.15) | copy-start | bytes 3538948

commit v9 on v8

--- a/solution.py
+++ b/solution.py
@@ -560,7 +560,7 @@
 def feed_forward_kernel(
     tok, part_in, cot_in, gain, bias, wf0, zb, zx, zy, zc,
     out, gz1, gb, sums, keep_a, keep_b, send_a, send_b, zs_out,
-    part, own_g, w, slope_g, slope_u, hid, nb, nbt, gm, gmt, total, norm1, inv1, dw, lw, xs, cot, from_core, from_z, to_z,
+    part, own_g, w, slope_g, slope_u, hid, nb, nbt, gm, gmt, total, norm1, inv1, dw, lw, xs, cot, out_v, from_core, from_z, to_z,
     f1a, f1b, f2a, f2b, send, recv, local, out_sem, trade_sem,
 ):
     me = Place()
@@ -651,7 +651,25 @@
     ff3.last()
     forward(3)
     n2, i2 = norm_forward(total[...])
-    out[...] = (n2 * gain[1:2, :] + bias[1:2, :]).astype(BF16)
+    out_v[...] = (n2 * gain[1:2, :] + bias[1:2, :]).astype(BF16)
+
+    def out_here():
+        return pltpu.make_async_copy(out_v, out, local.at[14])
+
+    def out_there():
+        return pltpu.make_async_remote_copy(
+            src_ref=out_v, dst_ref=out, send_sem=trade_sem.at[2], recv_sem=trade_sem.at[3], device_id=me.pair,
+            device_id_type=MESH,
+        )
+
+    @pl.when(me.cross == 0)
+    def _():
+        out_here().start()
+
+    @pl.when(me.cross == 1)
+    def _():
+        out_there().start()
+
 
     @pl.when(me.cross == 0)
     def _():
@@ -795,6 +813,14 @@
             copy.wait_send()
     links.wait_sends()
 
+    @pl.when(me.cross == 0)
+    def _():
+        out_here().wait()
+
+    @pl.when(me.cross == 1)
+    def _():
+        out_there().wait()
+
 
 def finish_kernel(
     extra, keep_a_in, keep_b_in, recv_a_in, recv_b_in, zr_in, ga_in, part_in, gz1_in, sums_in,
@@ -1031,18 +1057,8 @@
     dp, tensor = mesh.shape["dp"], mesh.shape["tensor"]
     assert tensor == 4 and dp >= 8 and dp & (dp - 1) == 0
     extra = [1 << b for b in range(3, dp.bit_length() - 1)]
-    both = ("dp", "tensor")
-
-    def cell(i, k):
-        return i * tensor + k
-
     def over(x, bit):
         return lax.ppermute(x, "dp", [(i, i ^ bit) for i in range(dp)])
-
-    away = [(i, k) for i in range(dp) for k in range(tensor) if (i & 1) != (k >> 1)]
-
-    def trade(x):
-        return lax.ppermute(x, both, [(cell(i, k), cell(i ^ 1, k ^ 2)) for i, k in away])
 
     smem = pl.BlockSpec(memory_space=pltpu.SMEM)
     vmem = pl.BlockSpec(memory_space=pltpu.VMEM)
@@ -1065,9 +1081,7 @@
         return pltpu.CompilerParams(vmem_limit_bytes=mib << 20, collective_id=number, has_side_effects=True)
 
     def on_device(tokens, segments, w_qkv, w_out, w_gate_up, w_down, norm_gain, norm_bias, cotangent):
-        p, z = lax.axis_index("dp"), lax.axis_index("tensor")
-        swapped = (p & 1) != (z >> 1)
-        place = p & 7
+        place = lax.axis_index("dp") & 7
 
         rows = lax.dynamic_slice(w_gate_up, (place * 96, 0, 0), (96, 2, 768))
         block = jnp.stack([rows[:, 0], rows[:, 1], lax.dynamic_slice(w_down, (place * 96, 0), (96, 768))])
@@ -1135,11 +1149,11 @@
             feed_forward_kernel,
             name="feed_forward",
             out_shape=(
-                shape(512, 768), shape(512, 768, dtype=F32), held(4, 512, 768), shape(8, 768, dtype=F32),
+                held(512, 768), shape(512, 768, dtype=F32), held(4, 512, 768), shape(8, 768, dtype=F32),
                 *(held(*plane),) * 4, shape(2, 3, 48, 768),
             ),
             in_specs=[far, far, hbm, vmem, vmem] + [far] * 5,
-            out_specs=(vmem, vmem, far, vmem) + (far,) * 4 + (vmem,),
+            out_specs=(far, vmem, far, vmem) + (far,) * 4 + (vmem,),
             scratch_shapes=[
                 pltpu.VMEM((4, 512, 768), BF16),
                 pltpu.VMEM((512, 768), BF16),
@@ -1158,6 +1172,7 @@
                 pltpu.VMEM((4, 4, 3, 96, 768), BF16),
                 pltpu.VMEM((512, 768), BF16),
                 pltpu.VMEM((512, 768), BF16),
+                pltpu.VMEM((512, 768), BF16),
                 pltpu.VMEM((2, 512, 768), BF16),
                 pltpu.VMEM((512, 768), BF16),
                 pltpu.VMEM((512, 768), BF16),
@@ -1165,7 +1180,7 @@
                 pltpu.VMEM((2, 3, 48, 768), BF16),
                 pltpu.VMEM((3, 48, 768), BF16),
                 pltpu.VMEM((3, 48, 768), BF16),
-                dma(80), dma(80), dma(16), dma(3, 8), dma(2),
+                dma(80), dma(80), dma(16), dma(3, 8), dma(4),
             ],
             compiler_params=params(62, 1),
             cost_estimate=pl.CostEstimate(flops=22_000_000_000, bytes_accessed=36_000_000, transcendentals=3_000_000),
@@ -1173,7 +1188,6 @@
 
         recv_a, recv_b = over(send_a, 4), over(send_b, 2)
         zr = lax.ppermute(zs, "tensor", [(i, i ^ 1) for i in range(tensor)])
-        output = jnp.where(swapped, trade(out), out)[None]
 
         grads, part = pl.pallas_call(
             attend_backward_kernel,
@@ -1245,32 +1259,32 @@
         g_qkv, g_out, g_gate_up, g_down, g_tok, gains, biases = pl.pallas_call(
             widen_kernel,
             name="widen",
-            grid=(6,),
+            grid=(3,),
             out_shape=(
                 shape(576, 768, dtype=F32), shape(192, 768, dtype=F32), shape(768, 2, 768, dtype=F32),
                 shape(768, 768, dtype=F32), shape(1, 512, 768, dtype=F32), *(shape(2, 768, dtype=F32),) * 2,
             ),
             in_specs=[
-                pl.BlockSpec((96, 768), lambda i: (i, 0)),
-                pl.BlockSpec((32, 768), lambda i: (18 + i, 0)),
-                pl.BlockSpec((2, 128, 768), lambda i: (0, i, 0)),
-                pl.BlockSpec((1, 768, 128), lambda i: (2, 0, i)),
-                pl.BlockSpec((128, 768), lambda i: (jnp.minimum(i, 3), 0)),
+                pl.BlockSpec((192, 768), lambda i: (i, 0)),
+                pl.BlockSpec((64, 768), lambda i: (9 + i, 0)),
+                pl.BlockSpec((2, 256, 768), lambda i: (0, i, 0)),
+                pl.BlockSpec((1, 768, 256), lambda i: (2, 0, i)),
+                pl.BlockSpec((256, 768), lambda i: (jnp.minimum(i, 1), 0)),
                 pl.BlockSpec((8, 768), lambda i: (0, 0)),
             ],
             out_specs=(
-                pl.BlockSpec((96, 768), lambda i: (i, 0)),
-                pl.BlockSpec((32, 768), lambda i: (i, 0)),
-                pl.BlockSpec((128, 2, 768), lambda i: (i, 0, 0)),
-                pl.BlockSpec((128, 768), lambda i: (i, 0)),
-                pl.BlockSpec((1, 128, 768), lambda i: (0, jnp.minimum(i, 3), 0)),
+                pl.BlockSpec((192, 768), lambda i: (i, 0)),
+                pl.BlockSpec((64, 768), lambda i: (i, 0)),
+                pl.BlockSpec((256, 2, 768), lambda i: (i, 0, 0)),
+                pl.BlockSpec((256, 768), lambda i: (i, 0)),
+                pl.BlockSpec((1, 256, 768), lambda i: (0, jnp.minimum(i, 1), 0)),
                 pl.BlockSpec((2, 768), lambda i: (0, 0)),
                 pl.BlockSpec((2, 768), lambda i: (0, 0)),
             ),
             compiler_params=params(62),
             cost_estimate=pl.CostEstimate(flops=0, bytes_accessed=18_000_000, transcendentals=0),
         )(g_attn, g_attn, g_ff, g_ff, g_tok, sums)
-        return output, g_tok, g_qkv.reshape(3, 192, 768).transpose(2, 0, 1), g_out, g_gate_up, g_down, gains, biases
+        return out[None], g_tok, g_qkv.reshape(3, 192, 768).transpose(2, 0, 1), g_out, g_gate_up, g_down, gains, biases
 
     placed = (
         P("dp", "tensor", None),

time: 297 us -> 294 us (0.990)
  transfers between devices with their start and end apart: 7 -> 6, of which waited for: 0 -> 0; matrix products, arithmetic and copies ran while one was open for 1% -> 0% of each run, Pallas kernels for 20% -> 19%
where the time goes in v9:
time: 294 us; the launch traced here: 289 us
  Pallas kernels  274 us (93%)
  starting transfers between devices  7.48 us (3%)
  local copies, waits for them, and re-layouts  6.09 us (2%)
    pallas_call x1, Pallas kernels, on_device(): pl.pallas_call(feed_forward_kernel, name='feed_forward', out_shape=(held(...  73.9 us
    pallas_call x1, Pallas kernels, on_device(): pl.pallas_call(functools.partial(finish_kernel, extra), name='finish', ou...  73.1 us
    pallas_call x1, Pallas kernels, on_device(): pl.pallas_call(start_kernel, name='start', out_shape=(held(4, 512, 768),...  63.5 us
    pallas_call x1, Pallas kernels, on_device(): pl.pallas_call(attend_backward_kernel, name='attend_backward', out_shape=...  34.1 us
    pallas_call x1, Pallas kernels, on_device(): pl.pallas_call(attend_forward_kernel, name='attend_forward', out_shape=(h...  21.7 us
    pallas_call x1, Pallas kernels, on_device(): pl.pallas_call(widen_kernel, name='widen', grid=(3,), out_shape=(shape(57...  7.21 us
  transfers between devices with their start and end apart: 6, of which 0 were waited for; matrix products, arithmetic and copies ran while one was open for 0% of the time, Pallas kernels for 19%

profile of v9, /device:TPU:0, one launch (start us, length us, event | category | flops | bytes accessed | tf_op | source)
XLA Modules:
  0.0 288.9 jit_solution(14465279591290038449)
XLA Ops:
  0.6 0.0 copy-start
  0.7 1.3 copy-done
  1.9 1.5 constant_dynamic-slice_fusion
  3.5 0.8 pad_maximum_fusion.fb
  4.3 63.5 %start.1 = (bf16[4,512,768]{2,1,0:T(8,128)(2,1)}, bf16[768,768]{1,0:T(8,128)(2,1)}, bf16[3,768,768]{2,1,0:T(8,128)(2,1)}, bf16[2,3,96,768]{3,2,1,0:T(8,128)(2,1)...) custom-call(bf16[512,768]{1,0:T(8,128)(2,1)} %bitcast.17, ...), custom_call_target="tpu_custom_call" | custom-call | tf_op jit(solution)/shard_map/start/pallas_call | solution.py:1091
  67.8 1.6 collective-permute-start.1
  69.4 1.5 collective-permute-start
  70.9 0.0 collective-permute-start.2
  70.9 21.7 %attend_forward.1 = (bf16[192,2048]{1,0:T(8,128)(2,1)}, f32[8,2048]{1,0:T(8,128)}, bf16[4,512,768]{2,1,0:T(8,128)(2,1)}) custom-call(s32[1,2048]{1,0:T(1,128)} %get-tuple-element.48.first, s32[1,2048]{1,0:T(1,128)} %get-tuple-element.49.end, bf16[768,768]{1,0:T(8,128)(2,1)} %get-tuple-element.50.w_in, bf16[3,128,2048]{2,1,0:T(8,128)(2,1)} %get-tuple-element.51.qa_in, ...), custom_call_target="tpu_custom_call" | custom-call | flops 20000000000 | bytes 24000000 | tf_op jit(solution)/shard_map/attend_forward/pallas_call | solution.py:1124
  92.6 0.0 collective-permute-done.2.zc
  92.6 0.0 collective-permute-done.1.zy
  92.6 0.0 copy-start.5
  92.6 0.0 collective-permute-done.zx
  92.6 0.0 copy-start.6
  92.6 0.9 copy-done.5
  93.5 0.3 copy-done.6
  93.8 73.9 %feed_forward.1 = (bf16[512,768]{1,0:T(8,128)(2,1)}, f32[512,768]{1,0:T(8,128)}, bf16[4,512,768]{2,1,0:T(8,128)(2,1)}, f32[8,768]{1,0:T(8,128)}, bf16[3,2,3,48,7...) custom-call(bf16[4,512,768]{2,1,0:T(8,128)(2,1)} %get-tuple-element., ...), custom_call_target="tpu_custom_call" | custom-call | flops 22000001024 | bytes 36000000 | tf_op jit(solution)/shard_map/feed_forward/pallas_call | solution.py:1148
  167.8 2.3 collective-permute-start.5
  170.1 0.7 collective-permute-start.3
  170.8 1.4 collective-permute-start.4
  172.2 34.1 %attend_backward.1 = (bf16[768,768]{1,0:T(8,128)(2,1)}, bf16[4,512,768]{2,1,0:T(8,128)(2,1)}) custom-call(s32[1,2048]{1,0:T(1,128)} %get-tuple-element.48.first, s32[1,2048]{1,0:T(1,128)} %get-tuple-element.49.end, bf16[4,512,768]{2,1,0:T(8,128)(2,1)} %get-tuple-element.64.gb_in, bf16[4,512,768]{2,1,0:T(8,128)(2,1)} %get-tuple-element.47.tok.tok_in, ...), custom_call_target="tpu_custom_call" | custom-call | flops 40000000000 | bytes 24000000 | tf_op jit(solution)/shard_map/attend_backward/pallas_call | solution.py:1192
  206.2 0.0 collective-permute-done.5.zr_in
  206.2 0.0 copy-start.4
  206.2 0.0 collective-permute-done.3.recv_a_in
  206.3 0.0 copy-start.2
  206.3 0.0 collective-permute-done.4.recv_b_in
  206.3 0.7 copy-done.4
  207.0 0.4 copy-done.2
  207.4 73.1 %finish.1 = (bf16[3,768,768]{2,1,0:T(8,128)(2,1)}, bf16[768,768]{1,0:T(8,128)(2,1)}, f32[512,768]{1,0:T(8,128)}, f32[8,768]{1,0:T(8,128)}) custom-call(bf16[3,2,3,48,768]{4,3,2,1,0:T(8,128)(2,1)} %get-tuple-element.59.keep_a_in, bf16[3,2,3,48,768]{4,3,2,1,0:T(8,128)(2,1)} %get-tuple-element.60.keep_b_in, bf16[3,2,3,48,768]{4,3,2,1,0:T(8,128)(2,1)} %copy-done.2, ...), custom_call_target="tpu_custom_call" | custom-call | tf_op jit(solution)/shard_map/finish/pallas_call | solution.py:1224
  280.6 0.0 copy-start.3
  280.6 0.0 copy-start.1
  280.6 7.2 %widen.1 = (f32[576,768]{1,0:T(8,128)}, f32[192,768]{1,0:T(8,128)}, f32[768,2,768]{2,1,0:T(2,128)}, f32[768,768]{1,0:T(8,128)}, f32[1,512,768]{2,1,0:T(8,128)}, /*index=5*/f32[2,768]{1,0:T(2,128)}, f32[2,768]{1,0:T(2,128)}) custom-call(bf16[768,768]{1,0:T(8,128)(2,1)} %get-tuple-element.75.attn.out_rows, bf16[768,768]{1,0:T(8,128)(2,1)} %get-tuple-element.75.attn.out_rows, ...), custom_call_target="tpu_custom_call" | custom-call | bytes 18000000 | tf_op jit(solution)/shard_map/widen/pallas_call | solution.py:1259
  287.8 0.0 copy-done.3
  287.8 0.9 copy.25
  288.7 0.0 copy-done.1
  (2 shorter events, 0.0 us)
Async XLA Ops:
  0.6 1.3 copy-start
  67.8 24.8 %collective-permute-start.1 = (bf16[2,3,96,768]{3,2,1,0:T(8,128)(2,1)}, bf16[2,3,96,768]{3,2,1,0:T(8,128)(2,1)S(1)}, u32[]{:S(2)}, u32[]{:S(2)}) collective-permute-start(bf16[2,3,96,768]{3,2,1,0:T(8,128)(2,1)} %get-tuple-element.56.zb), channel_id=1, source_target_pairs={{0,16},{4,20},{8,24},{12,28},{16,0},{20,4},{24,8},{28,12},{1,17},{... | collective-permute-start | bytes 2654216 | tf_op jit(solution)/shard_map/ppermute | solution.py:1061
  69.4 23.3 %collective-permute-start = (bf16[2,3,96,768]{3,2,1,0:T(8,128)(2,1)}, bf16[2,3,96,768]{3,2,1,0:T(8,128)(2,1)S(1)}, u32[]{:S(2)}, u32[]{:S(2)}) collective-permute-start(bf16[2,3,96,768]{3,2,1,0:T(8,128)(2,1)} %get-tuple-element.56.zb), channel_id=1, source_target_pairs={{0,8},{4,12},{8,0},{12,4},{16,24},{20,28},{24,16},{28,20},{1,9},{5... | collective-permute-start | bytes 2654216 | tf_op jit(solution)/shard_map/ppermute | solution.py:1061
  70.9 21.7 %collective-permute-start.2 = (bf16[3,96,768]{2,1,0:T(8,128)(2,1)}, bf16[3,96,768]{2,1,0:T(8,128)(2,1)}, u32[]{:S(2)}, u32[]{:S(2)}) collective-permute-start(bf16[3,96,768]{2,1,0:T(8,128)(2,1)} %get-tuple-element.57), channel_id=1, source_target_pairs={{0,1},{1,0},{2,3},{3,2},{4,5},{5,4},{6,7},{7,6},{8,9},{9,8},{10,11... | collective-permute-start | bytes 1327112 | tf_op jit(solution)/shard_map/ppermute | solution.py:1121
  92.6 0.9 copy-start.5
  92.6 1.2 copy-start.6
  167.8 38.5 %collective-permute-start.5 = (bf16[2,3,48,768]{3,2,1,0:T(8,128)(2,1)}, bf16[2,3,48,768]{3,2,1,0:T(8,128)(2,1)S(1)}, u32[]{:S(2)}, u32[]{:S(2)}) collective-permute-start(bf16[2,3,48,768]{3,2,1,0:T(8,128)(2,1)} %get-tuple-element.63), channel_id=1, source_target_pairs={{0,1},{1,0},{2,3},{3,2},{4,5},{5,4},{6,7},{7,6},{8,9},{9,8},{10,11... | collective-permute-start | bytes 1327112 | tf_op jit(solution)/shard_map/ppermute | solution.py:1190
  170.1 36.1 %collective-permute-start.3 = (bf16[3,2,3,48,768]{4,3,2,1,0:T(8,128)(2,1)}, bf16[3,2,3,48,768]{4,3,2,1,0:T(8,128)(2,1)S(1)}, u32[]{:S(2)}, u32[]{:S(2)}) collective-permute-start(bf16[3,2,3,48,768]{4,3,2,1,0:T(8,128)(2,1)} %get-tuple-element.61), channel_id=1, source_target_pairs={{0,16},{4,20},{8,24},{12,28},{16,0},{20,4},{24,8},{28,12},{1,17},{... | collective-permute-start | bytes 3981320 | tf_op jit(solution)/shard_map/ppermute | solution.py:1061
  170.8 35.5 %collective-permute-start.4 = (bf16[3,2,3,48,768]{4,3,2,1,0:T(8,128)(2,1)}, bf16[3,2,3,48,768]{4,3,2,1,0:T(8,128)(2,1)}, u32[]{:S(2)}, u32[]{:S(2)}) collective-permute-start(bf16[3,2,3,48,768]{4,3,2,1,0:T(8,128)(2,1)} %get-tuple-element.62), channel_id=1, source_target_pairs={{0,8},{4,12},{8,0},{12,4},{16,24},{20,28},{24,16},{28,20},{1,9},{5... | collective-permute-start | bytes 3981320 | tf_op jit(solution)/shard_map/ppermute | solution.py:1061
  206.2 0.8 copy-start.4
  206.3 1.2 copy-start.2
  280.6 7.2 %copy-start.3 = (bf16[512,768]{1,0:T(8,128)(2,1)S(1)}, bf16[512,768]{1,0:T(8,128)(2,1)}, u32[]{:S(2)}) copy-start(bf16[512,768]{1,0:T(8,128)(2,1)} %get-tuple-element.58) | copy-start | bytes 2359300
  280.6 8.1 %copy-start.1 = (bf16[768,768]{1,0:T(8,128)(2,1)S(1)}, bf16[768,768]{1,0:T(8,128)(2,1)}, u32[]{:S(2)}) copy-start(bf16[768,768]{1,0:T(8,128)(2,1)} %param.15) | copy-start | bytes 3538948
